TPU v7x, 256 devices: a whole 4x4x8 slice. The times are simulated.
256 devices in a mesh: chan: 16 (over z, x_lo), row: 4 (over y), col: 4 (over x_hi, core).
Axes of the slice: x: 4 (x_hi: 2, x_lo: 2; x = x_hi * 2 + x_lo), y: 4, z: 8, core: 2. Of those that a mesh axis runs over, the one named last changes fastest.
Arguments:
- voltages: bfloat16 [1024, 128, 2, 2048], P(('row', 'col'), 'chan'), may hold values from -6 to 6
- fir_taps: float32 [8, 2048], replicated, may hold values from -2 to 2
Outputs:
- visibilities: float32 [256, 2, 1024, 1024], P('chan', None, 'row', 'col')
All inputs are finite; a program needn't handle non-finite values.
Results may differ from a plain program's by a relative error of at most 0.0067.
Values may be sent and summed in bfloat16 or wider, within the bound.
No kernel may reach another device: no remote copies, remote signals or barrier semaphores. Data moves between devices by JAX's collectives and lax.ppermute only.
A program may use at most 64 MiB of HBM per device.

v0:
```python
import math

import jax
import jax.numpy as jnp
from jax import lax
from jax.sharding import PartitionSpec as P

CH_DEV = 16


def shifted(block, axis, distance):
    devices = range(lax.axis_size(axis))
    route = [(i - distance, i) for i in devices if i - distance in devices]
    return lax.ppermute(block, axis, route)


def dft_table(length, kept):
    index = jnp.arange(length, dtype=jnp.int32)
    chosen = jnp.arange(kept, dtype=jnp.int32)
    phase = (index[:, None] * chosen[None, :] % length).astype(jnp.float32) * (
        2.0 * math.pi / length
    )
    cosine = jnp.cos(phase) / math.sqrt(length)
    sine = jnp.sin(phase) / math.sqrt(length)
    upper = jnp.concatenate([cosine, -sine], axis=1)
    lower = jnp.concatenate([sine, cosine], axis=1)
    return jnp.concatenate([upper, lower], axis=0).astype(jnp.bfloat16)


def per_device(voltages, fir_taps):
    in_count, spec_count, parts_count, sample_count = voltages.shape
    tap_count = fir_taps.shape[0]
    kept_count = CH_DEV * lax.axis_size("chan")
    frames = voltages.reshape(in_count, spec_count, 2 * sample_count)
    rim_frames = shifted(frames[:, : tap_count - 1, :], "chan", -1)
    extended = jnp.concatenate([frames, rim_frames], axis=1)
    taps_both = jnp.concatenate([fir_taps, fir_taps], axis=1)
    windowed = jnp.zeros((in_count, spec_count, 2 * sample_count), jnp.float32)
    for step in range(tap_count):
        windowed = (
            windowed
            + extended[:, step : step + spec_count, :].astype(jnp.float32) * taps_both[step]
        )
    windowed = windowed.astype(jnp.bfloat16)
    table = dft_table(sample_count, kept_count)
    spectra = jnp.einsum("itm,mk->kit", windowed, table, preferred_element_type=jnp.float32)
    spectra = spectra.astype(jnp.bfloat16).reshape(2, kept_count, in_count, spec_count)
    turned = lax.all_to_all(spectra, "chan", split_axis=1, concat_axis=3, tiled=True)
    everyone = lax.all_gather(turned, ("row", "col"), axis=2, tiled=True)
    block_size = in_count * lax.axis_size("col")
    row_start = lax.axis_index("row") * block_size
    col_start = lax.axis_index("col") * block_size
    row_inputs = lax.dynamic_slice_in_dim(everyone, row_start, block_size, 2)
    col_inputs = lax.dynamic_slice_in_dim(everyone, col_start, block_size, 2)
    flipped = jnp.stack([-col_inputs[1], col_inputs[0]])
    real_part = jnp.einsum(
        "pcit,pcjt->cij", row_inputs, col_inputs, preferred_element_type=jnp.float32
    )
    imag_part = jnp.einsum(
        "pcit,pcjt->cij", row_inputs, flipped, preferred_element_type=jnp.float32
    )
    total_frames = jnp.float32(turned.shape[3])
    return jnp.stack([real_part, imag_part], axis=1) / total_frames


def solution(mesh):
    return jax.shard_map(
        per_device,
        mesh=mesh,
        in_specs=(P(("row", "col"), "chan", None, None), P()),
        out_specs=P("chan", None, "row", "col"),
        check_vma=False,
    )
```

profile of v0, /device:TPU:1, one launch (start us, length us, event | category | flops | bytes accessed | tf_op | source)
XLA Modules:
  0.0 258.1 jit_solution(139955586888520341)
XLA Ops:
  6.5 0.0 all-gather.2.cloned.1.call-start
  6.5 7.8 %reshape.14 = bf16[64,8,4096]{2,1,0:T(8,128)(2,1)} reshape(bf16[64,8,2,2048]{3,2,1,0:T(2,128)(2,1)} %param.2) | data formatting | bytes 8388608 | tf_op jit(solution)/shard_map/reshape | solution.py:34
  14.3 0.0 copy-start.2
  14.3 0.0 copy-start
  14.3 4.6 %copy.32 = bf16[64,7,4096]{2,0,1:T(8,128)(2,1)S(1)} copy(bf16[64,7,4096]{2,1,0:T(8,128)(2,1)} %bitcast.32) | data formatting | bytes 7340032
  18.9 1.5 collective-permute-start
  20.4 0.0 copy-done.2
  20.5 8.0 %fusion.17 = bf16[2048,256]{1,0:T(8,128)(2,1)S(1)} fusion(), kind=kLoop, calls=%fused_computation.28 | loop fusion | flops 8388608 | bytes 1048576 | tf_op jit(solution)/shard_map/convert.2
  28.5 8.6 %negate_convert_fusion = (bf16[2048,256]{1,0:T(8,128)(2,1)S(1)}, bf16[2048,256]{1,0:T(8,128)(2,1)S(1)}) fusion(), kind=kLoop, calls=%fused_computation.22 | loop fusion | flops 9961472 | bytes 2097152 | tf_op jit(solution)/shard_map/convert.5
  37.1 0.1 fusion.26
  37.2 0.0 copy-done
  37.2 2.3 constant_dynamic-update-slice_fusion.3
  39.5 60.1 %collective-permute-done = bf16[64,7,4096]{2,0,1:T(8,128)(2,1)S(1)} collective-permute-done((bf16[64,7,4096]{2,0,1:T(8,128)(2,1)S(1)}, bf16[64,7,4096]{2,0,1:T(8,128)(2,1)S(1)}, u32[]{:S(2)}, u32[]{:S(2)}) %collective-permute-start) | collective-permute-done | bytes 3670048 | tf_op jit(solution)/shard_map/ppermute | solution.py:14
  99.6 0.4 constant_dynamic-update-slice_fusion.2
  100.0 0.0 copy-start.1
  100.0 3.2 %copy-done.1 = bf16[64,15,4096]{2,0,1:T(8,128)(2,1)} copy-done((bf16[64,15,4096]{2,0,1:T(8,128)(2,1)}, bf16[64,15,4096]{2,0,1:T(8,128)(2,1)S(1)}, u32[]{:S(2)}) %copy-start.1) | copy-done | bytes 7864344
  103.2 25.2 %fusion.20 = bf16[512,64,8]{0,1,2:T(8,128)(2,1)} fusion(bf16[64,15,4096]{2,0,1:T(8,128)(2,1)} %copy-done.1, f32[4096]{0:T(1024)S(1)} %bitcast.37, f32[4096]{0:T(1024)S(1)} %bitcast.38, f32[4096]{0:T(1024)S(1)} %bitcast.39, f32[4096]{0:T(1024)S(1)} %bitcast.40, f32[4096]{0:T(1024)S(1)} %bitcast.41, f32[4096]{0:T(1024)S(1)} %bitcast.42, ...), kind=kOutput, calls=%fused_computation.31 | convolution fusion | flops 2214854656 | bytes 37355520 | tf_op jit(solution)/shard_map/itm,mk->kit/dot_general | solution.py:46
  128.4 1.2 reshape.15
  129.6 1.3 copy.18
  130.9 0.7 reshape.19
  131.6 27.1 %all_to_all.18 = bf16[16,2,8192]{2,1,0:T(2,128)(2,1)S(1)} all-to-all(bf16[16,2,8192]{2,1,0:T(2,128)(2,1)S(1)} %reshape.19), channel_id=1, replica_groups=mesh['chan'=16,'row'=4,'col'=4] {'chan'}, dimensions={0} | all-to-all | bytes 1048576 | tf_op jit(solution)/shard_map/all_to_all | solution.py:48
  158.7 0.7 reshape.20
  159.4 0.3 copy.33
  159.7 1.1 copy.21
  160.8 0.0 all-gather.2.cloned.1.call-update
  160.9 78.3 %all-gather.2.cloned.1.call-done = bf16[2,16,1024,128]{3,2,0,1:T(8,128)(2,1)} async-done(((bf16[2,16,64,128]{3,2,0,1:T(8,128)(2,1)}), bf16[2,16,1024,128]{3,2,0,1:T(8,128)(2,1)}) %all-gather.2.cloned.1.call-update) | async-done | bytes 8388624 | tf_op jit(solution)/shard_map/all_gather | solution.py:49
  239.1 1.8 dynamic-slice_negate_fusion
  241.0 3.0 %convolution_bitcast_fusion.1 = f32[16,1,256,256]{3,2,0,1:T(8,128)S(1)} fusion(bf16[2,16,1024,128]{3,2,0,1:T(8,128)(2,1)} %all-gather.2.cloned.1.call-done, s32[]{:T(128)S(6)} %select_n.21, s32[]{:T(128)S(6)} %select_n.20), kind=kOutput, calls=%fused_computation.14 | convolution fusion | flops 536870912 | bytes 8388616 | tf_op jit(solution)/shard_map/pcit,pcjt->cij/dot_general | solution.py:56
  244.0 2.4 convolution_bitcast_fusion
  246.3 0.9 maximum_multiply_fusion
  247.3 4.0 %copy.22 = f32[16,2,256,256]{3,2,1,0:T(8,128)} copy(f32[16,2,256,256]{3,2,0,1:T(8,128)S(1)} %maximum_multiply_fusion) | data formatting | bytes 16777216 | tf_op jit(solution)/shard_map/div | solution.py:63
  (2 shorter events, 0.0 us)
Async XLA Ops:
  6.5 232.6 %all-gather.2.cloned.1.call-start = ((), (), s32[]{:S(2)}) async-start(), calls=%async_computation.1 | async-start | bytes 8912896 | tf_op jit(solution)/shard_map/all_gather | solution.py:49
  14.3 6.1 %copy-start.2 = (f32[8,2048]{1,0:T(8,128)S(1)}, f32[8,2048]{1,0:T(8,128)}, u32[]{:S(2)}) copy-start(f32[8,2048]{1,0:T(8,128)} %param.3) | copy-start | bytes 196612
  14.3 22.9 %copy-start = (bf16[64,8,4096]{2,1,0:T(8,128)(2,1)S(1)}, bf16[64,8,4096]{2,1,0:T(8,128)(2,1)}, u32[]{:S(2)}) copy-start(bf16[64,8,4096]{2,1,0:T(8,128)(2,1)} %reshape.14) | copy-start | bytes 12582916
  18.9 80.7 %collective-permute-start = (bf16[64,7,4096]{2,0,1:T(8,128)(2,1)S(1)}, bf16[64,7,4096]{2,0,1:T(8,128)(2,1)S(1)}, u32[]{:S(2)}, u32[]{:S(2)}) collective-permute-start(bf16[64,7,4096]{2,0,1:T(8,128)(2,1)S(1)} %copy.32), channel_id=1, source_target_pairs={{16,0},{32,16},{48,32},{64,48},{80,64},{96,80},{112,96},{128,112},... | collective-permute-start | bytes 11010056 | tf_op jit(solution)/shard_map/ppermute | solution.py:14
  100.0 3.2 %copy-start.1 = (bf16[64,15,4096]{2,0,1:T(8,128)(2,1)}, bf16[64,15,4096]{2,0,1:T(8,128)(2,1)S(1)}, u32[]{:S(2)}) copy-start(bf16[64,15,4096]{2,0,1:T(8,128)(2,1)S(1)} %constant_dynamic-update-slice_fusion.2) | copy-start | bytes 23592964
Sparse Core Ops, SparseCore 0:
  161.0 78.1 all-gather.1
where the time goes:
time: 258 us
  waiting for transfers between devices  138 us (53%)
  matrix products  30.5 us (12%)
  local copies, waits for them, and re-layouts  27.6 us (11%)
  blocking collectives  27.1 us (11%)
  other arithmetic  19.4 us (8%)
  between operations  13.5 us (5%)
    all_gather x1, waiting for transfers between devices, per_device(): everyone = lax.all_gather(turned, ('row', 'col'), axis=2, tiled=True)  78.3 us
    ppermute x1, waiting for transfers between devices, shifted(): return lax.ppermute(block, axis, route)  60.1 us
    all_to_all x1, blocking collectives, per_device(): lax.all_to_all(spectra, 'chan', split_axis=1, concat_axis=3, tiled=True)  27.1 us
    dot_general x1, matrix products, per_device(): jnp.einsum('itm,mk->kit', windowed, table, preferred_element_type=jnp.flo...  25.2 us
    another operation x2, other arithmetic  16.6 us
    unnamed x11, local copies, waits for them, and re-layouts  11.5 us
    reshape x1, local copies, waits for them, and re-layouts, per_device(): frames = voltages.reshape(in_count, spec_count, 2 * sample_count)  7.77 us
  transfers between devices with their start and end apart: 2, of which 2 were waited for; matrix products, arithmetic and copies ran while one was open for 7% of the time, Pallas kernels for 0%

commit v1 on v0

v1 whole, which is shorter than its diff:
```python
import math

import jax
import jax.numpy as jnp
import numpy as np
from jax import lax
from jax.experimental import pallas as pl
from jax.experimental.pallas import tpu as pltpu
from jax.sharding import PartitionSpec as P

import ml_dtypes

NCH = 2048
KEEP = 256
TAPS = 8
ROWS = 1024
PITCH = 1024
GROUP = 16
CHUNKS = 1
LANES = 128
MIB = 1 << 20


def dft_table():
    index = np.arange(NCH, dtype=np.int64)
    chosen = np.arange(KEEP, dtype=np.int64)
    phase = (index[:, None] * chosen[None, :] % NCH).astype(np.float32) * np.float32(
        2.0 * math.pi / NCH
    )
    cosine = np.cos(phase) / np.float32(math.sqrt(NCH))
    sine = np.sin(phase) / np.float32(math.sqrt(NCH))
    upper = np.stack([cosine, -sine], axis=1)
    lower = np.stack([sine, cosine], axis=1)
    table = np.stack([upper, lower], axis=0)
    table = table.reshape(2, NCH // LANES, LANES, 2, KEEP // 2, 2)
    table = table.transpose(3, 5, 4, 1, 0, 2)
    return np.ascontiguousarray(table.reshape(2 * KEEP, 2 * NCH)).astype(ml_dtypes.bfloat16)


def spectra_kernel(x_ref, taps_ref, table_ref, own_ref, pre_ref, fir_ref, wide_ref, acc_ref):
    group = pl.program_id(0)

    @pl.when(group == 0)
    def _():
        acc_ref[...] = jnp.zeros_like(acc_ref)
        for rho in range(GROUP):
            fir_ref[pl.ds(rho * PITCH + 512, 64), :] = jnp.zeros((64, LANES), jnp.float32)

    taps = [taps_ref[k] for k in range(TAPS)]

    def filter_input(i, carry):
        frame = [x_ref[i, t].astype(jnp.float32) for t in range(TAPS)]
        for t in range(TAPS):
            total = frame[t] * taps[0]
            for k in range(1, TAPS - t):
                total = total + frame[t + k] * taps[k]
            fir_ref[pl.ds(t * 64 + i, GROUP, stride=PITCH), :] = total
        for t in range(1, TAPS):
            total = frame[0] * taps[TAPS - t]
            for f in range(1, t):
                total = total + frame[f] * taps[TAPS - t + f]
            fir_ref[pl.ds(512 + t * 64 + i, GROUP, stride=PITCH), :] = total
        return carry

    lax.fori_loop(0, 64, filter_input, 0)

    def narrow(n, carry):
        row = pl.multiple_of(n * 128, 128)
        for rho in range(GROUP):
            wide_ref[pl.ds(row, 128), pl.ds(rho * LANES, LANES)] = fir_ref[
                pl.ds(rho * PITCH + row, 128), :
            ].astype(jnp.bfloat16)
        return carry

    lax.fori_loop(0, ROWS // 128, narrow, 0)

    def transform(n, carry):
        row = pl.multiple_of(n * 256, 256)
        acc_ref[:, pl.ds(row, 256)] += lax.dot_general(
            table_ref[...],
            wide_ref[pl.ds(row, 256), :],
            (((1,), (1,)), ((), ())),
            preferred_element_type=jnp.float32,
        )
        return carry

    lax.fori_loop(0, ROWS // 256, transform, 0)

    @pl.when(group == pl.num_programs(0) - 1)
    def _():
        low = lax.broadcasted_iota(jnp.int32, (128, LANES), 1) < 64
        for half in range(2):
            for t2 in range(4):
                lanes = pl.ds((half * 4 + t2) * LANES, LANES)
                for p in range(2):
                    zero = acc_ref[pl.ds(p * 256, 128), lanes]
                    one = acc_ref[pl.ds(p * 256 + 128, 128), lanes]
                    even = jnp.where(low, zero, pltpu.roll(one, 64, 1))
                    odd = jnp.where(low, pltpu.roll(zero, 64, 1), one)
                    row = half * 2048 + p * 8 + 2 * t2
                    fir_ref[pl.ds(row, 128, stride=16), :] = even
                    fir_ref[pl.ds(row + 1, 128, stride=16), :] = odd
        own_ref[...] = fir_ref[pl.ds(0, 2048), :]
        pre_ref[...] = fir_ref[pl.ds(2048, 2048), :].astype(jnp.bfloat16)


def spectra(voltages, fir_taps, table):
    x = voltages.reshape(64, 8, 2, 16, LANES).transpose(0, 1, 3, 2, 4).reshape(64, 8, 32, LANES)
    taps = fir_taps.reshape(TAPS, 16, 1, LANES)
    taps = jnp.broadcast_to(taps, (TAPS, 16, 2, LANES)).reshape(TAPS, 32, LANES)
    return pl.pallas_call(
        spectra_kernel,
        grid=(32 // GROUP,),
        in_specs=[
            pl.BlockSpec((64, 8, GROUP, LANES), lambda g: (0, 0, g, 0)),
            pl.BlockSpec((TAPS, GROUP, LANES), lambda g: (0, g, 0)),
            pl.BlockSpec((512, GROUP * LANES), lambda g: (0, g)),
        ],
        out_specs=[
            pl.BlockSpec((2048, LANES), lambda g: (0, 0)),
            pl.BlockSpec((2048, LANES), lambda g: (0, 0)),
        ],
        out_shape=[
            jax.ShapeDtypeStruct((2048, LANES), jnp.float32),
            jax.ShapeDtypeStruct((2048, LANES), jnp.bfloat16),
        ],
        scratch_shapes=[
            pltpu.VMEM((GROUP * PITCH, LANES), jnp.float32),
            pltpu.VMEM((ROWS, GROUP * LANES), jnp.bfloat16),
            pltpu.VMEM((512, ROWS), jnp.float32),
        ],
        compiler_params=pltpu.CompilerParams(vmem_limit_bytes=40 * MIB),
        cost_estimate=pl.CostEstimate(
            flops=2 * 1024 * 4096 * 512, bytes_accessed=12 * MIB, transcendentals=0
        ),
    )(x, taps, table)


def correlate_kernel(place_ref, *refs):
    rows, cols, out_ref, side_ref = refs[:4], refs[4:8], refs[-2], refs[-1]
    low = lax.broadcasted_iota(jnp.int32, (256, LANES), 1) < 64
    for k in range(4):
        side_ref[place_ref[k]] = rows[k][...].reshape(256, LANES).astype(jnp.float32)
        side_ref[4 + place_ref[4 + k]] = cols[k][...].reshape(256, LANES).astype(jnp.float32)

    def joined(first, channel):
        parts = []
        for b in (first, first + 2):
            left, right = side_ref[b], side_ref[b + 1]
            if channel == 0:
                parts.append(jnp.where(low, left, pltpu.roll(right, 64, 1)))
            else:
                parts.append(jnp.where(low, pltpu.roll(left, 64, 1), right))
        return jnp.concatenate(parts, axis=1)

    for channel in range(2):
        left = joined(0, channel).astype(jnp.bfloat16)
        right = joined(4, channel)
        pairs = right.reshape(16, 2, 8, 256)
        flipped = jnp.concatenate([-pairs[:, 1:], pairs[:, :1]], axis=1).reshape(256, 256)
        for part, other in ((0, right), (1, flipped)):
            out_ref[channel, part] = lax.dot_general(
                left,
                other.astype(jnp.bfloat16),
                (((0,), (0,)), ((), ())),
                preferred_element_type=jnp.float32,
            ) * (1.0 / 128.0)


def correlate(place, rows, cols, chunk, earlier):
    steps = 8 // CHUNKS
    in_specs = [pl.BlockSpec((16, 16, LANES), lambda g, place: (0, g, 0)) for _ in range(8)]
    operands = [*rows, *cols]
    aliases = {}
    if earlier is not None:
        in_specs.append(pl.BlockSpec(memory_space=pl.ANY))
        operands.append(earlier)
        aliases = {9: 0}
    return pl.pallas_call(
        correlate_kernel,
        grid_spec=pltpu.PrefetchScalarGridSpec(
            num_scalar_prefetch=1,
            grid=(steps,),
            in_specs=in_specs,
            out_specs=pl.BlockSpec(
                (2, 2, 256, 256), lambda g, place: (chunk * steps + g, 0, 0, 0)
            ),
            scratch_shapes=[pltpu.VMEM((8, 256, LANES), jnp.float32)],
        ),
        out_shape=jax.ShapeDtypeStruct((16, 2, 256, 256), jnp.float32),
        input_output_aliases=aliases,
        compiler_params=pltpu.CompilerParams(vmem_limit_bytes=24 * MIB),
        cost_estimate=pl.CostEstimate(
            flops=2**30 // CHUNKS, bytes_accessed=12 * MIB // CHUNKS, transcendentals=0
        ),
    )(place, *operands)


def per_device(voltages, fir_taps, table):
    own, pre = spectra(voltages, fir_taps, table)
    own = own.reshape(16, CHUNKS, 128 // CHUNKS, LANES)
    pre = pre.reshape(16, CHUNKS, 128 // CHUNKS, LANES)
    row, col = lax.axis_index("row"), lax.axis_index("col")
    row_places = [col ^ k for k in range(4)]
    col_places = [row, (row + 3) % 4, (row + 1) % 4, (row + 2) % 4]
    place = jnp.stack(row_places + col_places).astype(jnp.int32)
    back = [(s, s - 1) for s in range(1, 16)]
    ring = range(4)
    result = None
    for chunk in range(CHUNKS):
        rim = lax.ppermute(pre[:, chunk], "chan", back)
        whole = (own[:, chunk] + rim.astype(jnp.float32)).astype(jnp.bfloat16)
        turned = lax.all_to_all(whole, "chan", split_axis=0, concat_axis=0, tiled=True)
        crossed = lax.ppermute(
            turned, ("row", "col"), [(4 * r + c, 4 * c + r) for r in ring for c in ring]
        )
        far = lax.ppermute(turned, "col", [(c, c ^ 2) for c in ring])
        near = lax.ppermute(turned, "col", [(c, c ^ 1) for c in ring])
        both = lax.ppermute(far, "col", [(c, c ^ 1) for c in ring])
        cols = [crossed] + [
            lax.ppermute(crossed, "row", [(r, (r + d) % 4) for r in ring]) for d in (1, 3, 2)
        ]
        result = correlate(place, [turned, near, far, both], cols, chunk, result)
    return result


def solution(mesh):
    table = dft_table()

    def run(voltages, fir_taps):
        return jax.shard_map(
            per_device,
            mesh=mesh,
            in_specs=(P(("row", "col"), "chan", None, None), P(), P()),
            out_specs=P("chan", None, "row", "col"),
            check_vma=False,
        )(voltages, fir_taps, jnp.asarray(table))

    return run
```

time: 258 us -> 130 us (0.50)
  waiting for transfers between devices: 138 us -> 40.4 us
  Pallas kernels: 0 us -> 36.7 us
  matrix products: 30.5 us -> 0 us
  local copies, waits for them, and re-layouts: 27.6 us -> 5.35 us
  other arithmetic: 19.4 us -> 0.13 us
  starting transfers between devices: 1.47 us -> 20 us
  between operations: 13.5 us -> 0.07 us
    all_gather x1 -> x0, waiting for transfers between devices: 78.3 us -> none  [per_device(): everyone = lax.all_gather(turned, ('row', 'col'), axis=2, tiled=True)]
    pallas_call x0 -> x2, Pallas kernels: none -> 36.7 us  [the longest x1 27.5 us: spectra(): pl.pallas_call(spectra_kernel, grid=(32 // GROUP,), in_specs=[pl.BlockSpe...]
    dot_general x3 -> x0, matrix products: 30.5 us -> none  [the longest x1 25.2 us: per_device(): jnp.einsum('itm,mk->kit', windowed, table, preferred_element_type=jnp.flo...]
    ppermute x1 -> x8, waiting for transfers between devices: 60.1 us -> 40.4 us  [the longest x3 12.2 us: per_device(): lax.ppermute(crossed, 'row', [(r, (r + d) % 4) for r in ring])]
    ppermute x1 -> x8, starting transfers between devices: 1.47 us -> 20 us  [the longest x1 6.69 us: per_device(): lax.ppermute(turned, ('row', 'col'), [(4 * r + c, 4 * c + r) for r in rin...]
    another operation x2 -> x0, other arithmetic: 16.6 us -> none
    reshape x3 -> x0, local copies, waits for them, and re-layouts: 10.2 us -> none  [the longest x1 7.77 us: per_device(): frames = voltages.reshape(in_count, spec_count, 2 * sample_count)]
    unnamed x11 -> x4, local copies, waits for them, and re-layouts: 11.5 us -> 4.37 us
  transfers between devices with their start and end apart: 2 -> 8, of which waited for: 2 -> 5; matrix products, arithmetic and copies ran while one was open for 7% -> 0% of each run, Pallas kernels for 0% -> 0%
where the time goes in v1:
time: 130 us
  waiting for transfers between devices  40.4 us (31%)
  Pallas kernels  36.7 us (28%)
  blocking collectives  27.1 us (21%)
  starting transfers between devices  20 us (15%)
  local copies, waits for them, and re-layouts  5.35 us (4%)
    pallas_call x1, Pallas kernels, spectra(): pl.pallas_call(spectra_kernel, grid=(32 // GROUP,), in_specs=[pl.BlockSpe...  27.5 us
    all_to_all x1, blocking collectives, per_device(): lax.all_to_all(whole, 'chan', split_axis=0, concat_axis=0, tiled=True)  27.1 us
    ppermute x3, waiting for transfers between devices, per_device(): lax.ppermute(crossed, 'row', [(r, (r + d) % 4) for r in ring])  12.2 us
    ppermute x1, waiting for transfers between devices, per_device(): rim = lax.ppermute(pre[:, chunk], 'chan', back)  12 us
    pallas_call x1, Pallas kernels, correlate(): pl.pallas_call(correlate_kernel, grid_spec=pltpu.PrefetchScalarGridSpec(n...  9.14 us
    ppermute x1, waiting for transfers between devices, per_device(): far = lax.ppermute(turned, 'col', [(c, c ^ 2) for c in ring])  8.84 us
    ppermute x1, waiting for transfers between devices, per_device(): lax.ppermute(turned, ('row', 'col'), [(4 * r + c, 4 * c + r) for r in rin...  7.4 us
    ppermute x1, starting transfers between devices, per_device(): lax.ppermute(turned, ('row', 'col'), [(4 * r + c, 4 * c + r) for r in rin...  6.69 us
  transfers between devices with their start and end apart: 8, of which 5 were waited for; matrix products, arithmetic and copies ran while one was open for 0% of the time, Pallas kernels for 0%

profile of v1, /device:TPU:1, one launch (start us, length us, event | category | flops | bytes accessed | tf_op | source)
XLA Modules:
  0.0 129.7 jit_solution(12941344735163872395)
XLA Ops:
  0.0 0.9 copy.5
  0.9 0.0 copy-start
  0.9 2.2 %copy-done = bf16[64,8,2,2048]{3,2,1,0:T(2,128)(2,1)S(1)} copy-done((bf16[64,8,2,2048]{3,2,1,0:T(2,128)(2,1)S(1)}, bf16[64,8,2,2048]{3,2,1,0:T(2,128)(2,1)}, u32[]{:S(2)}) %copy-start) | copy-done | bytes 4194328
  3.1 0.0 copy-start.1
  3.1 2.2 %copy-done.1 = bf16[512,4096]{1,0:T(8,128)(2,1)S(1)} copy-done((bf16[512,4096]{1,0:T(8,128)(2,1)S(1)}, bf16[512,4096]{1,0:T(8,128)(2,1)}, u32[]{:S(2)}) %copy-start.1) | copy-done | bytes 4194328
  5.3 27.5 %shard_map.37 = (f32[2048,128]{1,0:T(8,128)S(1)}, bf16[2048,128]{1,0:T(8,128)(2,1)S(1)}) custom-call(bf16[64,8,32,128]{3,2,1,0:T(8,128)(2,1)S(1)} %bitcast.19, f32[8,32,128]{2,1,0:T(8,128)S(1)} %bitcast.18, bf16[512,4096]{1,0:T(8,128)(2,1)S(1)} %copy-done.1), custom_call_target="tpu_custom_call" | custom-call | flops 4294967296 | bytes 12582912 | tf_op jit(solution)/shard_map/pallas_call | solution.py:111
  32.8 1.3 collective-permute-start
  34.1 12.0 %collective-permute-done = bf16[16,128,128]{2,1,0:T(8,128)(2,1)S(1)} collective-permute-done((bf16[16,128,128]{2,1,0:T(8,128)(2,1)S(1)}, bf16[16,128,128]{2,1,0:T(8,128)(2,1)S(1)}, u32[]{:S(2)}, u32[]{:S(2)}) %collective-permute-start) | collective-permute-done | bytes 524320 | tf_op jit(solution)/shard_map/ppermute | solution.py:211
  46.1 0.1 add_convert_fusion
  46.2 27.1 %all_to_all.5.refs_0_ = bf16[16,128,128]{2,1,0:T(8,128)(2,1)S(1)} all-to-all(bf16[16,128,128]{2,1,0:T(8,128)(2,1)S(1)} %add_convert_fusion), channel_id=1, replica_groups=mesh['chan'=16,'row'=4,'col'=4] {'chan'}, dimensions={0} | all-to-all | bytes 1048576 | tf_op jit(solution)/shard_map/all_to_all | solution.py:213
  73.4 6.7 %collective-permute-start.4 = (bf16[16,128,128]{2,1,0:T(8,128)(2,1)S(1)}, bf16[16,128,128]{2,1,0:T(8,128)(2,1)S(1)}, u32[]{:S(2)}, u32[]{:S(2)}) collective-permute-start(bf16[16,128,128]{2,1,0:T(8,128)(2,1)S(1)} %all_to_all.5.refs_0_), channel_id=1, source_target_pairs={{0,0},{1,4},{2,8},{3,12},{4,1},{5,5},{6,9},{7,13},{8,2},{9,6},{10,... | collective-permute-start | bytes 1572872 | tf_op jit(solution)/shard_map/ppermute | solution.py:214
  80.1 4.2 %collective-permute-start.2 = (bf16[16,128,128]{2,1,0:T(8,128)(2,1)S(1)}, bf16[16,128,128]{2,1,0:T(8,128)(2,1)S(1)}, u32[]{:S(2)}, u32[]{:S(2)}) collective-permute-start(bf16[16,128,128]{2,1,0:T(8,128)(2,1)S(1)} %all_to_all.5.refs_0_), channel_id=1, source_target_pairs={{0,2},{1,3},{2,0},{3,1},{4,6},{5,7},{6,4},{7,5},{8,10},{9,11},{10,... | collective-permute-start | bytes 1572872 | tf_op jit(solution)/shard_map/ppermute | solution.py:217
  84.3 0.9 collective-permute-start.1
  85.1 7.4 %collective-permute-done.4.refs_4_ = bf16[16,128,128]{2,1,0:T(8,128)(2,1)S(1)} collective-permute-done((bf16[16,128,128]{2,1,0:T(8,128)(2,1)S(1)}, bf16[16,128,128]{2,1,0:T(8,128)(2,1)S(1)}, u32[]{:S(2)}, u32[]{:S(2)}) %collective-permute-start.4) | collective-permute-done | bytes 524320 | tf_op jit(solution)/shard_map/ppermute | solution.py:214
  92.5 4.3 %collective-permute-start.7 = (bf16[16,128,128]{2,1,0:T(8,128)(2,1)S(1)}, bf16[16,128,128]{2,1,0:T(8,128)(2,1)S(1)}, u32[]{:S(2)}, u32[]{:S(2)}) collective-permute-start(bf16[16,128,128]{2,1,0:T(8,128)(2,1)S(1)} %collective-permute-done.4.refs_4_), channel_id=1, source_target_pairs={{0,8},{4,12},{8,0},{12,4},{1,9},{5,13},{9,1},{13,5},{2,10},{6,14},... | collective-permute-start | bytes 1572872 | tf_op jit(solution)/shard_map/ppermute | solution.py:221
  96.9 0.0 collective-permute-start.6
  96.9 1.5 %collective-permute-start.5 = (bf16[16,128,128]{2,1,0:T(8,128)(2,1)S(1)}, bf16[16,128,128]{2,1,0:T(8,128)(2,1)}, u32[]{:S(2)}, u32[]{:S(2)}) collective-permute-start(bf16[16,128,128]{2,1,0:T(8,128)(2,1)S(1)} %collective-permute-done.4.refs_4_), channel_id=1, source_target_pairs={{0,4},{4,8},{8,12},{12,0},{1,5},{5,9},{9,13},{13,1},{2,6},{6,10},{... | collective-permute-start | bytes 1572872 | tf_op jit(solution)/shard_map/ppermute | solution.py:221
  98.3 8.8 %collective-permute-done.2.refs_2_ = bf16[16,128,128]{2,1,0:T(8,128)(2,1)S(1)} collective-permute-done((bf16[16,128,128]{2,1,0:T(8,128)(2,1)S(1)}, bf16[16,128,128]{2,1,0:T(8,128)(2,1)S(1)}, u32[]{:S(2)}, u32[]{:S(2)}) %collective-permute-start.2) | collective-permute-done | bytes 524320 | tf_op jit(solution)/shard_map/ppermute | solution.py:217
  107.2 1.1 collective-permute-start.3
  108.3 0.1 stack.35.place_ref
  108.4 0.0 collective-permute-done.1.refs_1_
  108.4 0.0 collective-permute-done.7.refs_7_
  108.4 9.0 %collective-permute-done.6.refs_6_ = bf16[16,128,128]{2,1,0:T(8,128)(2,1)S(1)} collective-permute-done((bf16[16,128,128]{2,1,0:T(8,128)(2,1)S(1)}, bf16[16,128,128]{2,1,0:T(8,128)(2,1)S(1)}, u32[]{:S(2)}, u32[]{:S(2)}) %collective-permute-start.6) | collective-permute-done | bytes 524320 | tf_op jit(solution)/shard_map/ppermute | solution.py:221
  117.4 3.2 %collective-permute-done.5.refs_5_ = bf16[16,128,128]{2,1,0:T(8,128)(2,1)} collective-permute-done((bf16[16,128,128]{2,1,0:T(8,128)(2,1)S(1)}, bf16[16,128,128]{2,1,0:T(8,128)(2,1)}, u32[]{:S(2)}, u32[]{:S(2)}) %collective-permute-start.5) | collective-permute-done | bytes 524320 | tf_op jit(solution)/shard_map/ppermute | solution.py:221
  120.6 0.0 collective-permute-done.3.refs_3_
  120.6 9.1 %shard_map.38 = f32[16,2,256,256]{3,2,1,0:T(8,128)} custom-call(s32[8]{0:T(128)S(1)} %stack.35.place_ref, bf16[16,128,128]{2,1,0:T(8,128)(2,1)S(1)} %all_to_all.5.refs_0_, bf16[16,128,128]{2,1,0:T(8,128)(2,1)S(1)} %collective-permute-done.1.refs_1_, bf16[16,128,128]{2,1,0:T(8,128)(2,1)S(1)} %collective-permute-done.2.refs_2_, ...), custom_call_target="tpu_custom_call" | custom-call | flops 1073741824 | bytes 12582912 | tf_op jit(solution)/shard_map/pallas_call | solution.py:179
  (1 shorter events, 0.0 us)
Async XLA Ops:
  0.9 2.2 %copy-start = (bf16[64,8,2,2048]{3,2,1,0:T(2,128)(2,1)S(1)}, bf16[64,8,2,2048]{3,2,1,0:T(2,128)(2,1)}, u32[]{:S(2)}) copy-start(bf16[64,8,2,2048]{3,2,1,0:T(2,128)(2,1)} %param.3) | copy-start | bytes 12582916
  3.1 2.2 %copy-start.1 = (bf16[512,4096]{1,0:T(8,128)(2,1)S(1)}, bf16[512,4096]{1,0:T(8,128)(2,1)}, u32[]{:S(2)}) copy-start(bf16[512,4096]{1,0:T(8,128)(2,1)} %constant.35.clone.table_ref) | copy-start | bytes 12582916
  32.8 13.3 %collective-permute-start = (bf16[16,128,128]{2,1,0:T(8,128)(2,1)S(1)}, bf16[16,128,128]{2,1,0:T(8,128)(2,1)S(1)}, u32[]{:S(2)}, u32[]{:S(2)}) collective-permute-start(bf16[16,128,128]{2,1,0:T(8,128)(2,1)S(1)} %bitcast.20), channel_id=1, source_target_pairs={{16,0},{32,16},{48,32},{64,48},{80,64},{96,80},{112,96},{128,112},... | collective-permute-start | bytes 1572872 | tf_op jit(solution)/shard_map/ppermute | solution.py:211
  73.4 19.2 %collective-permute-start.4 = (bf16[16,128,128]{2,1,0:T(8,128)(2,1)S(1)}, bf16[16,128,128]{2,1,0:T(8,128)(2,1)S(1)}, u32[]{:S(2)}, u32[]{:S(2)}) collective-permute-start(bf16[16,128,128]{2,1,0:T(8,128)(2,1)S(1)} %all_to_all.5.refs_0_), channel_id=1, source_target_pairs={{0,0},{1,4},{2,8},{3,12},{4,1},{5,5},{6,9},{7,13},{8,2},{9,6},{10,... | collective-permute-start | bytes 1572872 | tf_op jit(solution)/shard_map/ppermute | solution.py:214
  80.1 27.1 %collective-permute-start.2 = (bf16[16,128,128]{2,1,0:T(8,128)(2,1)S(1)}, bf16[16,128,128]{2,1,0:T(8,128)(2,1)S(1)}, u32[]{:S(2)}, u32[]{:S(2)}) collective-permute-start(bf16[16,128,128]{2,1,0:T(8,128)(2,1)S(1)} %all_to_all.5.refs_0_), channel_id=1, source_target_pairs={{0,2},{1,3},{2,0},{3,1},{4,6},{5,7},{6,4},{7,5},{8,10},{9,11},{10,... | collective-permute-start | bytes 1572872 | tf_op jit(solution)/shard_map/ppermute | solution.py:217
  84.3 24.1 %collective-permute-start.1 = (bf16[16,128,128]{2,1,0:T(8,128)(2,1)S(1)}, bf16[16,128,128]{2,1,0:T(8,128)(2,1)S(1)}, u32[]{:S(2)}, u32[]{:S(2)}) collective-permute-start(bf16[16,128,128]{2,1,0:T(8,128)(2,1)S(1)} %all_to_all.5.refs_0_), channel_id=1, source_target_pairs={{0,1},{1,0},{2,3},{3,2},{4,5},{5,4},{6,7},{7,6},{8,9},{9,8},{10,11... | collective-permute-start | bytes 1572872 | tf_op jit(solution)/shard_map/ppermute | solution.py:218
  92.5 15.8 %collective-permute-start.7 = (bf16[16,128,128]{2,1,0:T(8,128)(2,1)S(1)}, bf16[16,128,128]{2,1,0:T(8,128)(2,1)S(1)}, u32[]{:S(2)}, u32[]{:S(2)}) collective-permute-start(bf16[16,128,128]{2,1,0:T(8,128)(2,1)S(1)} %collective-permute-done.4.refs_4_), channel_id=1, source_target_pairs={{0,8},{4,12},{8,0},{12,4},{1,9},{5,13},{9,1},{13,5},{2,10},{6,14},... | collective-permute-start | bytes 1572872 | tf_op jit(solution)/shard_map/ppermute | solution.py:221
  96.9 20.5 %collective-permute-start.6 = (bf16[16,128,128]{2,1,0:T(8,128)(2,1)S(1)}, bf16[16,128,128]{2,1,0:T(8,128)(2,1)S(1)}, u32[]{:S(2)}, u32[]{:S(2)}) collective-permute-start(bf16[16,128,128]{2,1,0:T(8,128)(2,1)S(1)} %collective-permute-done.4.refs_4_), channel_id=1, source_target_pairs={{0,12},{4,0},{8,4},{12,8},{1,13},{5,1},{9,5},{13,9},{2,14},{6,2},{... | collective-permute-start | bytes 1572872 | tf_op jit(solution)/shard_map/ppermute | solution.py:221
  96.9 23.7 %collective-permute-start.5 = (bf16[16,128,128]{2,1,0:T(8,128)(2,1)S(1)}, bf16[16,128,128]{2,1,0:T(8,128)(2,1)}, u32[]{:S(2)}, u32[]{:S(2)}) collective-permute-start(bf16[16,128,128]{2,1,0:T(8,128)(2,1)S(1)} %collective-permute-done.4.refs_4_), channel_id=1, source_target_pairs={{0,4},{4,8},{8,12},{12,0},{1,5},{5,9},{9,13},{13,1},{2,6},{6,10},{... | collective-permute-start | bytes 1572872 | tf_op jit(solution)/shard_map/ppermute | solution.py:221
  107.2 13.4 %collective-permute-start.3 = (bf16[16,128,128]{2,1,0:T(8,128)(2,1)S(1)}, bf16[16,128,128]{2,1,0:T(8,128)(2,1)}, u32[]{:S(2)}, u32[]{:S(2)}) collective-permute-start(bf16[16,128,128]{2,1,0:T(8,128)(2,1)S(1)} %collective-permute-done.2.refs_2_), channel_id=1, source_target_pairs={{0,1},{1,0},{2,3},{3,2},{4,5},{5,4},{6,7},{7,6},{8,9},{9,8},{10,11... | collective-permute-start | bytes 1572872 | tf_op jit(solution)/shard_map/ppermute | solution.py:219

commit v2 on v1

v2 whole, which is shorter than its diff:
```python
import functools
import math

import jax
import jax.numpy as jnp
import numpy as np
from jax import lax
from jax.experimental import pallas as pl
from jax.experimental.pallas import tpu as pltpu
from jax.sharding import PartitionSpec as P

import ml_dtypes

NCH = 2048
KEEP = 256
TAPS = 8
PITCH = 521
VLIM = 56
GROUP = 16
CHUNKS = 1
LANES = 128
MIB = 1 << 20


def dft_table():
    index = np.arange(NCH, dtype=np.int64)
    chosen = np.arange(KEEP, dtype=np.int64)
    phase = (index[:, None] * chosen[None, :] % NCH).astype(np.float32) * np.float32(
        2.0 * math.pi / NCH
    )
    cosine = np.cos(phase) / np.float32(math.sqrt(NCH))
    sine = np.sin(phase) / np.float32(math.sqrt(NCH))
    upper = np.stack([cosine, -sine], axis=1)
    lower = np.stack([sine, cosine], axis=1)
    table = np.stack([upper, lower], axis=0)
    table = table.reshape(2, NCH // LANES, LANES, 2, KEEP // 2, 2)
    table = table.transpose(3, 5, 4, 1, 0, 2)
    return np.ascontiguousarray(table.reshape(2 * KEEP, 2 * NCH)).astype(ml_dtypes.bfloat16)


def spectra_kernel(rim, x_ref, taps_ref, table_ref, out_ref, fir_ref, wide_ref, acc_ref):
    group = pl.program_id(0)

    @pl.when(group == 0)
    def _():
        acc_ref[...] = jnp.zeros_like(acc_ref)
        if rim:
            for rho in range(GROUP):
                fir_ref[pl.ds(rho * PITCH, 64), :] = jnp.zeros((64, LANES), jnp.float32)

    taps = [taps_ref[k] for k in range(TAPS)]

    def filter_input(i, carry):
        frame = [x_ref[i, t].astype(jnp.float32) for t in range(TAPS)]
        for t in range(1 if rim else 0, TAPS):
            pairs = [(f, TAPS - t + f) for f in range(t)] if rim else [
                (t + k, k) for k in range(TAPS - t)
            ]
            total = None
            for f, k in pairs:
                term = frame[f] * taps[k]
                total = term if total is None else total + term
            fir_ref[pl.ds(t * 64 + i, GROUP, stride=PITCH), :] = total
        return carry

    lax.fori_loop(0, 64, filter_input, 0)

    def transform(n, carry):
        row = pl.multiple_of(n * 256, 256)
        for rho in range(GROUP):
            wide_ref[:, pl.ds(rho * LANES, LANES)] = fir_ref[
                pl.ds(rho * PITCH + row, 256), :
            ].astype(jnp.bfloat16)
        acc_ref[:, pl.ds(row, 256)] += lax.dot_general(
            table_ref[...],
            wide_ref[...],
            (((1,), (1,)), ((), ())),
            preferred_element_type=jnp.float32,
        )
        return carry

    lax.fori_loop(0, 2, transform, 0)

    @pl.when(group == pl.num_programs(0) - 1)
    def _():
        low = lax.broadcasted_iota(jnp.int32, (128, LANES), 1) < 64
        for t2 in range(4):
            lanes = pl.ds(t2 * LANES, LANES)
            for p in range(2):
                zero = acc_ref[pl.ds(p * 256, 128), lanes]
                one = acc_ref[pl.ds(p * 256 + 128, 128), lanes]
                even = jnp.where(low, zero, pltpu.roll(one, 64, 1))
                odd = jnp.where(low, pltpu.roll(zero, 64, 1), one)
                row = p * 8 + 2 * t2
                fir_ref[pl.ds(row, 128, stride=17), :] = even
                fir_ref[pl.ds(row + 1, 128, stride=17), :] = odd
        for pair in range(128):
            out_ref[pl.ds(pair * 16, 16), :] = fir_ref[pl.ds(pair * 17, 16), :].astype(
                out_ref.dtype
            )


def spectra(x, taps, table, rim):
    return pl.pallas_call(
        functools.partial(spectra_kernel, rim),
        grid=(32 // GROUP,),
        in_specs=[
            pl.BlockSpec((64, 8, GROUP, LANES), lambda g: (0, 0, g, 0)),
            pl.BlockSpec((TAPS, GROUP, LANES), lambda g: (0, g, 0)),
            pl.BlockSpec((512, GROUP * LANES), lambda g: (0, g)),
        ],
        out_specs=pl.BlockSpec((2048, LANES), lambda g: (0, 0)),
        out_shape=jax.ShapeDtypeStruct((2048, LANES), jnp.bfloat16 if rim else jnp.float32),
        scratch_shapes=[
            pltpu.VMEM((GROUP * PITCH, LANES), jnp.float32),
            pltpu.VMEM((256, GROUP * LANES), jnp.bfloat16),
            pltpu.VMEM((512, 512), jnp.float32),
        ],
        compiler_params=pltpu.CompilerParams(vmem_limit_bytes=VLIM * MIB),
        cost_estimate=pl.CostEstimate(
            flops=2 * 512 * 4096 * 512, bytes_accessed=10 * MIB, transcendentals=0
        ),
    )(x, taps, table)


def prepared(voltages, fir_taps):
    x = voltages.reshape(64, 8, 2, 16, LANES).transpose(0, 1, 3, 2, 4).reshape(64, 8, 32, LANES)
    taps = fir_taps.reshape(TAPS, 16, 1, LANES)
    taps = jnp.broadcast_to(taps, (TAPS, 16, 2, LANES)).reshape(TAPS, 32, LANES)
    return x, taps


def correlate_kernel(place_ref, *refs):
    rows, cols, tails, out_ref, side_ref = refs[:4], refs[4:7], refs[7:9], refs[-2], refs[-1]
    steps = pl.num_programs(0)
    low = lax.broadcasted_iota(jnp.int32, (256, LANES), 1) < 64
    for k, block in enumerate([*rows, *cols]):
        side_ref[place_ref[k]] = block[...].reshape(256, LANES).astype(jnp.float32)
    for half, block in enumerate(tails):

        @pl.when(pl.program_id(0) // (steps // 2) == half)
        def _():
            side_ref[place_ref[7]] = block[...].reshape(256, LANES).astype(jnp.float32)

    def joined(first, channel):
        parts = []
        for b in (first, first + 2):
            left, right = side_ref[b], side_ref[b + 1]
            if channel == 0:
                parts.append(jnp.where(low, left, pltpu.roll(right, 64, 1)))
            else:
                parts.append(jnp.where(low, pltpu.roll(left, 64, 1), right))
        return jnp.concatenate(parts, axis=1)

    for channel in range(2):
        left = joined(0, channel).astype(jnp.bfloat16)
        right = joined(4, channel)
        pairs = right.reshape(16, 2, 8, 256)
        flipped = jnp.concatenate([-pairs[:, 1:], pairs[:, :1]], axis=1).reshape(256, 256)
        for part, other in ((0, right), (1, flipped)):
            out_ref[channel, part] = lax.dot_general(
                left,
                other.astype(jnp.bfloat16),
                (((0,), (0,)), ((), ())),
                preferred_element_type=jnp.float32,
            ) * (1.0 / 128.0)


def correlate(place, rows, cols, tails, chunk, earlier):
    steps = 8 // CHUNKS
    block = (16, 16, LANES)
    in_specs = [pl.BlockSpec(block, lambda g, place: (0, g, 0)) for _ in range(7)]
    in_specs.append(
        pl.BlockSpec(block, lambda g, place: (0, jnp.minimum(g, steps // 2 - 1), 0))
    )
    in_specs.append(
        pl.BlockSpec(block, lambda g, place: (0, jnp.maximum(g - steps // 2, 0), 0))
    )
    operands = [*rows, *cols, *tails]
    aliases = {}
    if earlier is not None:
        in_specs.append(pl.BlockSpec(memory_space=pl.ANY))
        operands.append(earlier)
        aliases = {10: 0}
    return pl.pallas_call(
        correlate_kernel,
        grid_spec=pltpu.PrefetchScalarGridSpec(
            num_scalar_prefetch=1,
            grid=(steps,),
            in_specs=in_specs,
            out_specs=pl.BlockSpec(
                (2, 2, 256, 256), lambda g, place: (chunk * steps + g, 0, 0, 0)
            ),
            scratch_shapes=[pltpu.VMEM((8, 256, LANES), jnp.float32)],
        ),
        out_shape=jax.ShapeDtypeStruct((16, 2, 256, 256), jnp.float32),
        input_output_aliases=aliases,
        compiler_params=pltpu.CompilerParams(vmem_limit_bytes=24 * MIB),
        cost_estimate=pl.CostEstimate(
            flops=2**30 // CHUNKS, bytes_accessed=12 * MIB // CHUNKS, transcendentals=0
        ),
    )(place, *operands)


def per_device(voltages, fir_taps, table):
    x, taps = prepared(voltages, fir_taps)
    pre = spectra(x, taps, table, True)
    own = spectra(x, taps, table, False)
    own = own.reshape(16, CHUNKS, 128 // CHUNKS, LANES)
    pre = pre.reshape(16, CHUNKS, 128 // CHUNKS, LANES)
    row, col = lax.axis_index("row"), lax.axis_index("col")
    row_places = [col ^ k for k in range(4)]
    col_places = [row, (row + 3) % 4, (row + 1) % 4, (row + 2) % 4]
    place = jnp.stack(row_places + [4 + c for c in col_places]).astype(jnp.int32)
    back = [(s, s - 1) for s in range(1, 16)]
    ring = range(4)
    result = None
    for chunk in range(CHUNKS):
        rim = lax.ppermute(pre[:, chunk], "chan", back)
        whole = (own[:, chunk] + rim.astype(jnp.float32)).astype(jnp.bfloat16)
        turned = lax.all_to_all(whole, "chan", split_axis=0, concat_axis=0, tiled=True)
        crossed = lax.ppermute(
            turned, ("row", "col"), [(4 * r + c, 4 * c + r) for r in ring for c in ring]
        )
        far = lax.ppermute(turned, "col", [(c, c ^ 2) for c in ring])
        near = lax.ppermute(turned, "col", [(c, c ^ 1) for c in ring])
        both = lax.ppermute(far, "col", [(c, c ^ 1) for c in ring])
        lower = lax.ppermute(crossed, "row", [(r, (r + 1) % 4) for r in ring])
        upper = lax.ppermute(crossed, "row", [(r, (r - 1) % 4) for r in ring])
        half = 64 // CHUNKS
        tails = [
            lax.ppermute(lower[:, :half], "row", [(r, (r + 1) % 4) for r in ring]),
            lax.ppermute(upper[:, half:], "row", [(r, (r - 1) % 4) for r in ring]),
        ]
        result = correlate(
            place, [turned, near, far, both], [crossed, lower, upper], tails, chunk, result
        )
    return result


def solution(mesh):
    table = dft_table()

    def run(voltages, fir_taps):
        return jax.shard_map(
            per_device,
            mesh=mesh,
            in_specs=(P(("row", "col"), "chan", None, None), P(), P()),
            out_specs=P("chan", None, "row", "col"),
            check_vma=False,
        )(voltages, fir_taps, jnp.asarray(table))

    return run
```

time: 130 us -> 108 us (0.83); the launches traced: 130 us -> 106 us
  waiting for transfers between devices: 40.4 us -> 24.7 us
  Pallas kernels: 36.7 us -> 28.4 us
  local copies, waits for them, and re-layouts: 5.35 us -> 3.09 us
    ppermute x1, waiting for transfers between devices: 12 us -> 2.29 us  [per_device(): rim = lax.ppermute(pre[:, chunk], 'chan', back)]
    pallas_call x1 -> x2, Pallas kernels: 27.5 us -> 19.4 us  [spectra(): pl.pallas_call(functools.partial(spectra_kernel, rim), grid=(32 // GROUP,...]
    ppermute x3 -> x4, waiting for transfers between devices: 12.2 us -> 5.97 us  [the longest x1 5.96 us: per_device(): lax.ppermute(upper[:, half:], 'row', [(r, (r - 1) % 4) for r in ring])]
    unnamed x4 -> x0, local copies, waits for them, and re-layouts: 4.37 us -> none
    ppermute x1, starting transfers between devices: 0.85 us -> 4.73 us  [per_device(): near = lax.ppermute(turned, 'col', [(c, c ^ 1) for c in ring])]
    ppermute x3 -> x4, starting transfers between devices: 5.79 us -> 3.2 us  [the longest x1 1.73 us: per_device(): upper = lax.ppermute(crossed, 'row', [(r, (r - 1) % 4) for r in ring])]
    slice x0 -> x2, local copies, waits for them, and re-layouts: none -> 1.45 us  [the longest x1 0.72 us: per_device(): upper[:, half:]]
  transfers between devices with their start and end apart: 8 -> 9, of which waited for: 5 -> 4; matrix products, arithmetic and copies ran while one was open for 0% -> 1% of each run, Pallas kernels for 0% -> 9%
where the time goes in v2:
time: 108 us; the launch traced here: 106 us
  Pallas kernels  28.4 us (26%)
  blocking collectives  27.1 us (25%)
  waiting for transfers between devices  24.7 us (23%)
  starting transfers between devices  21.2 us (20%)
  local copies, waits for them, and re-layouts  3.09 us (3%)
  other arithmetic  1.35 us (1%)
    all_to_all x1, blocking collectives, per_device(): lax.all_to_all(whole, 'chan', split_axis=0, concat_axis=0, tiled=True)  27.1 us
    pallas_call x2, Pallas kernels, spectra(): pl.pallas_call(functools.partial(spectra_kernel, rim), grid=(32 // GROUP,...  19.4 us
    pallas_call x1, Pallas kernels, correlate(): pl.pallas_call(correlate_kernel, grid_spec=pltpu.PrefetchScalarGridSpec(n...  9.05 us
    ppermute x1, waiting for transfers between devices, per_device(): lax.ppermute(turned, ('row', 'col'), [(4 * r + c, 4 * c + r) for r in rin...  8.25 us
    ppermute x1, waiting for transfers between devices, per_device(): far = lax.ppermute(turned, 'col', [(c, c ^ 2) for c in ring])  8.16 us
    ppermute x1, starting transfers between devices, per_device(): lax.ppermute(turned, ('row', 'col'), [(4 * r + c, 4 * c + r) for r in rin...  6.71 us
    ppermute x1, waiting for transfers between devices, per_device(): lax.ppermute(upper[:, half:], 'row', [(r, (r - 1) % 4) for r in ring])  5.96 us
    ppermute x1, starting transfers between devices, per_device(): near = lax.ppermute(turned, 'col', [(c, c ^ 1) for c in ring])  4.73 us
  transfers between devices with their start and end apart: 9, of which 4 were waited for; matrix products, arithmetic and copies ran while one was open for 1% of the time, Pallas kernels for 9%

profile of v2, /device:TPU:1, one launch (start us, length us, event | category | flops | bytes accessed | tf_op | source)
XLA Modules:
  0.0 106.0 jit_solution(11715350975862315689)
XLA Ops:
  0.0 0.9 copy.5
  0.9 0.7 broadcast_in_dim.8
  1.6 9.5 %shard_map.38 = bf16[2048,128]{1,0:T(8,128)(2,1)} custom-call(bf16[64,8,32,128]{3,2,1,0:T(8,128)(2,1)} %bitcast.17, f32[8,32,128]{2,1,0:T(8,128)} %bitcast.20, bf16[512,4096]{1,0:T(8,128)(2,1)} %constant.35.clone.table_ref), custom_call_target="tpu_custom_call" | custom-call | flops 2147483648 | bytes 10485760 | tf_op jit(solution)/shard_map/pallas_call | solution.py:104
  11.1 1.3 %collective-permute-start = (bf16[16,128,128]{2,1,0:T(8,128)(2,1)}, bf16[16,128,128]{2,1,0:T(8,128)(2,1)S(1)}, u32[]{:S(2)}, u32[]{:S(2)}) collective-permute-start(bf16[16,128,128]{2,1,0:T(8,128)(2,1)} %bitcast.22), channel_id=1, source_target_pairs={{16,0},{32,16},{48,32},{64,48},{80,64},{96,80},{112,96},{128,112},... | collective-permute-start | bytes 1572872 | tf_op jit(solution)/shard_map/ppermute | solution.py:219
  12.4 9.9 %shard_map.37 = f32[2048,128]{1,0:T(8,128)} custom-call(bf16[64,8,32,128]{3,2,1,0:T(8,128)(2,1)} %bitcast.18, f32[8,32,128]{2,1,0:T(8,128)} %bitcast.21, bf16[512,4096]{1,0:T(8,128)(2,1)} %constant.35.clone.table_ref), custom_call_target="tpu_custom_call" | custom-call | flops 2147483648 | bytes 10485760 | tf_op jit(solution)/shard_map/pallas_call | solution.py:104
  22.2 2.3 %collective-permute-done = bf16[16,128,128]{2,1,0:T(8,128)(2,1)S(1)} collective-permute-done((bf16[16,128,128]{2,1,0:T(8,128)(2,1)}, bf16[16,128,128]{2,1,0:T(8,128)(2,1)S(1)}, u32[]{:S(2)}, u32[]{:S(2)}) %collective-permute-start) | collective-permute-done | bytes 524320 | tf_op jit(solution)/shard_map/ppermute | solution.py:219
  24.5 1.4 %add_convert_fusion = bf16[16,128,128]{2,1,0:T(8,128)(2,1)S(1)} fusion(f32[16,128,128]{2,1,0:T(8,128)} %bitcast.19, bf16[16,128,128]{2,1,0:T(8,128)(2,1)S(1)} %collective-permute-done), kind=kLoop, calls=%fused_computation | loop fusion | flops 786432 | bytes 2097152 | tf_op jit(solution)/shard_map/convert_element_type | solution.py:220
  25.9 27.1 %all_to_all.5.refs_0_ = bf16[16,128,128]{2,1,0:T(8,128)(2,1)S(1)} all-to-all(bf16[16,128,128]{2,1,0:T(8,128)(2,1)S(1)} %add_convert_fusion), channel_id=1, replica_groups=mesh['chan'=16,'row'=4,'col'=4] {'chan'}, dimensions={0} | all-to-all | bytes 1048576 | tf_op jit(solution)/shard_map/all_to_all | solution.py:221
  53.0 6.7 %collective-permute-start.4 = (bf16[16,128,128]{2,1,0:T(8,128)(2,1)S(1)}, bf16[16,128,128]{2,1,0:T(8,128)(2,1)S(1)}, u32[]{:S(2)}, u32[]{:S(2)}) collective-permute-start(bf16[16,128,128]{2,1,0:T(8,128)(2,1)S(1)} %all_to_all.5.refs_0_), channel_id=1, source_target_pairs={{0,0},{1,4},{2,8},{3,12},{4,1},{5,5},{6,9},{7,13},{8,2},{9,6},{10,... | collective-permute-start | bytes 1572872 | tf_op jit(solution)/shard_map/ppermute | solution.py:222
  59.7 4.2 %collective-permute-start.2 = (bf16[16,128,128]{2,1,0:T(8,128)(2,1)S(1)}, bf16[16,128,128]{2,1,0:T(8,128)(2,1)S(1)}, u32[]{:S(2)}, u32[]{:S(2)}) collective-permute-start(bf16[16,128,128]{2,1,0:T(8,128)(2,1)S(1)} %all_to_all.5.refs_0_), channel_id=1, source_target_pairs={{0,2},{1,3},{2,0},{3,1},{4,6},{5,7},{6,4},{7,5},{8,10},{9,11},{10,... | collective-permute-start | bytes 1572872 | tf_op jit(solution)/shard_map/ppermute | solution.py:225
  63.9 8.3 %collective-permute-done.4.refs_4_ = bf16[16,128,128]{2,1,0:T(8,128)(2,1)S(1)} collective-permute-done((bf16[16,128,128]{2,1,0:T(8,128)(2,1)S(1)}, bf16[16,128,128]{2,1,0:T(8,128)(2,1)S(1)}, u32[]{:S(2)}, u32[]{:S(2)}) %collective-permute-start.4) | collective-permute-done | bytes 524320 | tf_op jit(solution)/shard_map/ppermute | solution.py:222
  72.2 1.7 %collective-permute-start.6 = (bf16[16,128,128]{2,1,0:T(8,128)(2,1)S(1)}, bf16[16,128,128]{2,1,0:T(8,128)(2,1)S(1)}, u32[]{:S(2)}, u32[]{:S(2)}) collective-permute-start(bf16[16,128,128]{2,1,0:T(8,128)(2,1)S(1)} %collective-permute-done.4.refs_4_), channel_id=1, source_target_pairs={{0,12},{4,0},{8,4},{12,8},{1,13},{5,1},{9,5},{13,9},{2,14},{6,2},{... | collective-permute-start | bytes 1572872 | tf_op jit(solution)/shard_map/ppermute | solution.py:229
  73.9 0.0 collective-permute-start.5
  73.9 4.7 %collective-permute-start.1 = (bf16[16,128,128]{2,1,0:T(8,128)(2,1)S(1)}, bf16[16,128,128]{2,1,0:T(8,128)(2,1)S(1)}, u32[]{:S(2)}, u32[]{:S(2)}) collective-permute-start(bf16[16,128,128]{2,1,0:T(8,128)(2,1)S(1)} %all_to_all.5.refs_0_), channel_id=1, source_target_pairs={{0,1},{1,0},{2,3},{3,2},{4,5},{5,4},{6,7},{7,6},{8,9},{9,8},{10,11... | collective-permute-start | bytes 1572872 | tf_op jit(solution)/shard_map/ppermute | solution.py:226
  78.7 8.2 %collective-permute-done.2.refs_2_ = bf16[16,128,128]{2,1,0:T(8,128)(2,1)S(1)} collective-permute-done((bf16[16,128,128]{2,1,0:T(8,128)(2,1)S(1)}, bf16[16,128,128]{2,1,0:T(8,128)(2,1)S(1)}, u32[]{:S(2)}, u32[]{:S(2)}) %collective-permute-start.2) | collective-permute-done | bytes 524320 | tf_op jit(solution)/shard_map/ppermute | solution.py:225
  86.8 1.1 %collective-permute-start.3 = (bf16[16,128,128]{2,1,0:T(8,128)(2,1)S(1)}, bf16[16,128,128]{2,1,0:T(8,128)(2,1)}, u32[]{:S(2)}, u32[]{:S(2)}) collective-permute-start(bf16[16,128,128]{2,1,0:T(8,128)(2,1)S(1)} %collective-permute-done.2.refs_2_), channel_id=1, source_target_pairs={{0,1},{1,0},{2,3},{3,2},{4,5},{5,4},{6,7},{7,6},{8,9},{9,8},{10,11... | collective-permute-start | bytes 1572872 | tf_op jit(solution)/shard_map/ppermute | solution.py:227
  87.9 0.0 collective-permute-done.6.refs_6_
  87.9 0.7 slice.9
  88.7 0.0 collective-permute-start.8
  88.7 0.0 collective-permute-done.5.refs_5_
  88.7 0.7 slice.8
  89.4 1.5 %collective-permute-start.7 = (bf16[16,64,128]{2,1,0:T(8,128)(2,1)}, bf16[16,64,128]{2,1,0:T(8,128)(2,1)}, u32[]{:S(2)}, u32[]{:S(2)}) collective-permute-start(bf16[16,64,128]{2,1,0:T(8,128)(2,1)} %slice.8), channel_id=1, source_target_pairs={{0,4},{4,8},{8,12},{12,0},{1,5},{5,9},{9,13},{13,1},{2,6},{6,10},{... | collective-permute-start | bytes 786440 | tf_op jit(solution)/shard_map/ppermute | solution.py:232
  90.9 0.1 stack.35.place_ref
  90.9 0.0 collective-permute-done.1.refs_1_
  90.9 0.0 collective-permute-done.3.refs_3_
  91.0 6.0 %collective-permute-done.8.refs_8_ = bf16[16,64,128]{2,1,0:T(8,128)(2,1)S(1)} collective-permute-done((bf16[16,64,128]{2,1,0:T(8,128)(2,1)}, bf16[16,64,128]{2,1,0:T(8,128)(2,1)S(1)}, u32[]{:S(2)}, u32[]{:S(2)}) %collective-permute-start.8) | collective-permute-done | bytes 262176 | tf_op jit(solution)/shard_map/ppermute | solution.py:233
  96.9 0.0 collective-permute-done.7.refs_7_
  96.9 9.1 %shard_map.39 = f32[16,2,256,256]{3,2,1,0:T(8,128)} custom-call(s32[8]{0:T(128)S(1)} %stack.35.place_ref, bf16[16,128,128]{2,1,0:T(8,128)(2,1)S(1)} %all_to_all.5.refs_0_, bf16[16,128,128]{2,1,0:T(8,128)(2,1)S(1)} %collective-permute-done.1.refs_1_, bf16[16,128,128]{2,1,0:T(8,128)(2,1)S(1)} %collective-permute-done.2.refs_2_, ...), custom_call_target="tpu_custom_call" | custom-call | flops 1073741824 | bytes 12582912 | tf_op jit(solution)/shard_map/pallas_call | solution.py:185
Async XLA Ops:
  11.1 13.4 %collective-permute-start = (bf16[16,128,128]{2,1,0:T(8,128)(2,1)}, bf16[16,128,128]{2,1,0:T(8,128)(2,1)S(1)}, u32[]{:S(2)}, u32[]{:S(2)}) collective-permute-start(bf16[16,128,128]{2,1,0:T(8,128)(2,1)} %bitcast.22), channel_id=1, source_target_pairs={{16,0},{32,16},{48,32},{64,48},{80,64},{96,80},{112,96},{128,112},... | collective-permute-start | bytes 1572872 | tf_op jit(solution)/shard_map/ppermute | solution.py:219
  53.0 19.2 %collective-permute-start.4 = (bf16[16,128,128]{2,1,0:T(8,128)(2,1)S(1)}, bf16[16,128,128]{2,1,0:T(8,128)(2,1)S(1)}, u32[]{:S(2)}, u32[]{:S(2)}) collective-permute-start(bf16[16,128,128]{2,1,0:T(8,128)(2,1)S(1)} %all_to_all.5.refs_0_), channel_id=1, source_target_pairs={{0,0},{1,4},{2,8},{3,12},{4,1},{5,5},{6,9},{7,13},{8,2},{9,6},{10,... | collective-permute-start | bytes 1572872 | tf_op jit(solution)/shard_map/ppermute | solution.py:222
  59.7 27.1 %collective-permute-start.2 = (bf16[16,128,128]{2,1,0:T(8,128)(2,1)S(1)}, bf16[16,128,128]{2,1,0:T(8,128)(2,1)S(1)}, u32[]{:S(2)}, u32[]{:S(2)}) collective-permute-start(bf16[16,128,128]{2,1,0:T(8,128)(2,1)S(1)} %all_to_all.5.refs_0_), channel_id=1, source_target_pairs={{0,2},{1,3},{2,0},{3,1},{4,6},{5,7},{6,4},{7,5},{8,10},{9,11},{10,... | collective-permute-start | bytes 1572872 | tf_op jit(solution)/shard_map/ppermute | solution.py:225
  72.2 15.7 %collective-permute-start.6 = (bf16[16,128,128]{2,1,0:T(8,128)(2,1)S(1)}, bf16[16,128,128]{2,1,0:T(8,128)(2,1)S(1)}, u32[]{:S(2)}, u32[]{:S(2)}) collective-permute-start(bf16[16,128,128]{2,1,0:T(8,128)(2,1)S(1)} %collective-permute-done.4.refs_4_), channel_id=1, source_target_pairs={{0,12},{4,0},{8,4},{12,8},{1,13},{5,1},{9,5},{13,9},{2,14},{6,2},{... | collective-permute-start | bytes 1572872 | tf_op jit(solution)/shard_map/ppermute | solution.py:229
  73.9 14.7 %collective-permute-start.5 = (bf16[16,128,128]{2,1,0:T(8,128)(2,1)S(1)}, bf16[16,128,128]{2,1,0:T(8,128)(2,1)S(1)}, u32[]{:S(2)}, u32[]{:S(2)}) collective-permute-start(bf16[16,128,128]{2,1,0:T(8,128)(2,1)S(1)} %collective-permute-done.4.refs_4_), channel_id=1, source_target_pairs={{0,4},{4,8},{8,12},{12,0},{1,5},{5,9},{9,13},{13,1},{2,6},{6,10},{... | collective-permute-start | bytes 1572872 | tf_op jit(solution)/shard_map/ppermute | solution.py:228
  73.9 17.0 %collective-permute-start.1 = (bf16[16,128,128]{2,1,0:T(8,128)(2,1)S(1)}, bf16[16,128,128]{2,1,0:T(8,128)(2,1)S(1)}, u32[]{:S(2)}, u32[]{:S(2)}) collective-permute-start(bf16[16,128,128]{2,1,0:T(8,128)(2,1)S(1)} %all_to_all.5.refs_0_), channel_id=1, source_target_pairs={{0,1},{1,0},{2,3},{3,2},{4,5},{5,4},{6,7},{7,6},{8,9},{9,8},{10,11... | collective-permute-start | bytes 1572872 | tf_op jit(solution)/shard_map/ppermute | solution.py:226
  86.8 4.1 %collective-permute-start.3 = (bf16[16,128,128]{2,1,0:T(8,128)(2,1)S(1)}, bf16[16,128,128]{2,1,0:T(8,128)(2,1)}, u32[]{:S(2)}, u32[]{:S(2)}) collective-permute-start(bf16[16,128,128]{2,1,0:T(8,128)(2,1)S(1)} %collective-permute-done.2.refs_2_), channel_id=1, source_target_pairs={{0,1},{1,0},{2,3},{3,2},{4,5},{5,4},{6,7},{7,6},{8,9},{9,8},{10,11... | collective-permute-start | bytes 1572872 | tf_op jit(solution)/shard_map/ppermute | solution.py:227
  88.7 8.3 %collective-permute-start.8 = (bf16[16,64,128]{2,1,0:T(8,128)(2,1)}, bf16[16,64,128]{2,1,0:T(8,128)(2,1)S(1)}, u32[]{:S(2)}, u32[]{:S(2)}) collective-permute-start(bf16[16,64,128]{2,1,0:T(8,128)(2,1)} %slice.9), channel_id=1, source_target_pairs={{0,12},{4,0},{8,4},{12,8},{1,13},{5,1},{9,5},{13,9},{2,14},{6,2},{... | collective-permute-start | bytes 786440 | tf_op jit(solution)/shard_map/ppermute | solution.py:233
  89.4 7.5 %collective-permute-start.7 = (bf16[16,64,128]{2,1,0:T(8,128)(2,1)}, bf16[16,64,128]{2,1,0:T(8,128)(2,1)}, u32[]{:S(2)}, u32[]{:S(2)}) collective-permute-start(bf16[16,64,128]{2,1,0:T(8,128)(2,1)} %slice.8), channel_id=1, source_target_pairs={{0,4},{4,8},{8,12},{12,0},{1,5},{5,9},{9,13},{13,1},{2,6},{6,10},{... | collective-permute-start | bytes 786440 | tf_op jit(solution)/shard_map/ppermute | solution.py:232

commit v3 on v2

v3 whole, which is shorter than its diff:
```python
import functools
import math

import jax
import jax.numpy as jnp
import numpy as np
from jax import lax
from jax.experimental import pallas as pl
from jax.experimental.pallas import tpu as pltpu
from jax.sharding import PartitionSpec as P

import ml_dtypes

NCH = 2048
KEEP = 256
TAPS = 8
PITCH = 521
VLIM = 56
INPUTS = 16
GROUP = 16
LANES = 128
MIB = 1 << 20


def dft_table():
    index = np.arange(NCH, dtype=np.int64)
    chosen = np.arange(KEEP, dtype=np.int64)
    phase = (index[:, None] * chosen[None, :] % NCH).astype(np.float32) * np.float32(
        2.0 * math.pi / NCH
    )
    cosine = np.cos(phase) / np.float32(math.sqrt(NCH))
    sine = np.sin(phase) / np.float32(math.sqrt(NCH))
    table = np.stack([cosine, sine], axis=0)[:, : NCH // 2]
    table = table.reshape(2, NCH // 2, KEEP // 2, 2).transpose(3, 0, 2, 1)
    return np.ascontiguousarray(table.reshape(2, KEEP, NCH // 2)).astype(ml_dtypes.bfloat16)


def spectra_kernel(rim, x_ref, taps_ref, table_ref, out_ref, fir_ref, wide_ref, acc_ref):
    step = pl.program_id(0)

    if rim:

        @pl.when(step == 0)
        def _():
            for rho in range(2 * GROUP):
                fir_ref[pl.ds(rho * PITCH, 64), :] = jnp.zeros((64, LANES), jnp.float32)

    def filter_input(n, carry):
        i = step * INPUTS + n
        for piece in range(2):
            rows = slice(8 * piece, 8 * piece + 8)
            halves = []
            for part in range(2):
                taps = [taps_ref[k, pl.ds(16 * part + 8 * piece, 8), :] for k in range(TAPS)]
                frame = [
                    x_ref[n, t, pl.ds(16 * part, 16), :].astype(jnp.float32)[rows]
                    for t in range(TAPS)
                ]
                totals = []
                for t in range(1 if rim else 0, TAPS):
                    pairs = [(f, TAPS - t + f) for f in range(t)] if rim else [
                        (t + k, k) for k in range(TAPS - t)
                    ]
                    total = None
                    for f, k in pairs:
                        term = frame[f] * taps[k]
                        total = term if total is None else total + term
                    totals.append(total)
                halves.append(totals)
            for t, (early, late) in enumerate(zip(*halves), 1 if rim else 0):
                base = t * 64 + i + 8 * piece * PITCH
                fir_ref[pl.ds(base, 8, stride=PITCH), :] = early + late
                fir_ref[pl.ds(base + GROUP * PITCH, 8, stride=PITCH), :] = early - late
        return carry

    lax.fori_loop(0, INPUTS, filter_input, 0)

    @pl.when(step == pl.num_programs(0) - 1)
    def _():
        def transform(low_bit, carry):
            for p in range(2):
                for cb in range(8):
                    wide_ref[:, pl.ds(cb * LANES, LANES)] = fir_ref[
                        pl.ds((low_bit * GROUP + cb * 2 + p) * PITCH, 512), :
                    ].astype(jnp.bfloat16)
                acc_ref[low_bit, p] = lax.dot_general(
                    table_ref[low_bit],
                    wide_ref[...],
                    (((1,), (1,)), ((), ())),
                    preferred_element_type=jnp.float32,
                )
            return carry

        lax.fori_loop(0, 2, transform, 0)

        low = lax.broadcasted_iota(jnp.int32, (128, LANES), 1) < 64
        for t2 in range(4):
            lanes = pl.ds(t2 * LANES, LANES)
            for p in range(2):
                pair = []
                for low_bit in range(2):
                    cosine = acc_ref[low_bit, p, pl.ds(0, 128), lanes]
                    sine = acc_ref[low_bit, 1 - p, pl.ds(128, 128), lanes]
                    pair.append(cosine + sine if p == 0 else cosine - sine)
                zero, one = pair
                even = jnp.where(low, zero, pltpu.roll(one, 64, 1))
                odd = jnp.where(low, pltpu.roll(zero, 64, 1), one)
                row = p * 8 + 2 * t2
                fir_ref[pl.ds(row, 128, stride=17), :] = even
                fir_ref[pl.ds(row + 1, 128, stride=17), :] = odd
        for pair in range(128):
            out_ref[pl.ds(pair * 16, 16), :] = fir_ref[pl.ds(pair * 17, 16), :].astype(
                out_ref.dtype
            )


def spectra(x, taps, table, rim):
    return pl.pallas_call(
        functools.partial(spectra_kernel, rim),
        grid=(64 // INPUTS,),
        in_specs=[
            pl.BlockSpec((INPUTS, 8, 32, LANES), lambda g: (g, 0, 0, 0)),
            pl.BlockSpec((TAPS, 32, LANES), lambda g: (0, 0, 0)),
            pl.BlockSpec((2, KEEP, NCH // 2), lambda g: (0, 0, 0)),
        ],
        out_specs=pl.BlockSpec((2048, LANES), lambda g: (0, 0)),
        out_shape=jax.ShapeDtypeStruct((2048, LANES), jnp.bfloat16 if rim else jnp.float32),
        scratch_shapes=[
            pltpu.VMEM((2 * GROUP * PITCH, LANES), jnp.float32),
            pltpu.VMEM((512, NCH // 2), jnp.bfloat16),
            pltpu.VMEM((2, 2, KEEP, 512), jnp.float32),
        ],
        compiler_params=pltpu.CompilerParams(vmem_limit_bytes=VLIM * MIB),
        cost_estimate=pl.CostEstimate(
            flops=2 * 512 * 2048 * 512, bytes_accessed=6 * MIB, transcendentals=0
        ),
    )(x, taps, table)


def prepared(voltages, fir_taps):
    x = voltages.reshape(64, 8, 2, 16, LANES).transpose(0, 1, 3, 2, 4).reshape(64, 8, 32, LANES)
    taps = fir_taps.reshape(TAPS, 16, 1, LANES)
    taps = jnp.broadcast_to(taps, (TAPS, 16, 2, LANES)).reshape(TAPS, 32, LANES)
    return x, taps


def correlate_kernel(late, place_ref, *refs):
    rows, cols, out_ref = refs[:4], refs[4:8], refs[-1]
    step = pl.program_id(0)
    at = pl.ds(pl.multiple_of(step * 16, 16), 16)
    odd = place_ref[5] == 1

    def block(ref):
        return ref[:, at, :].reshape(256, LANES)

    left_blocks = [block(ref) for ref in rows]
    if late:
        tail = pl.ds(pl.multiple_of(step % 4 * 16, 16), 16)
        far = jnp.where(step < 4, cols[2][:, tail, :], cols[3][:, tail, :]).reshape(256, LANES)
        right_blocks = [
            jnp.where(odd, block(cols[1]), far), jnp.where(odd, far, block(cols[0]))
        ]
    else:
        mine = block(cols[0])
        right_blocks = [
            jnp.where(odd, block(cols[1]), mine), jnp.where(odd, mine, block(cols[2]))
        ]
    for channel in range(2):
        lanes = slice(64 * channel, 64 * channel + 64)
        left = jnp.concatenate([b[:, lanes] for b in left_blocks], axis=1)
        right = jnp.concatenate([b[:, lanes] for b in right_blocks], axis=1)
        pairs = right.astype(jnp.float32).reshape(16, 2, 8, LANES)
        flipped = jnp.concatenate([-pairs[:, 1:], pairs[:, :1]], axis=1).reshape(256, LANES)
        product = lax.dot_general(
            left,
            jnp.concatenate([right, flipped.astype(jnp.bfloat16)], axis=1),
            (((0,), (0,)), ((), ())),
            preferred_element_type=jnp.float32,
        ) * (1.0 / 128.0)
        for k in range(4):
            where = pl.ds(pl.multiple_of(place_ref[k] * 64, 64), 64)
            for part in range(2):
                out_ref[channel, part, where, :] = product[
                    k * 64 : (k + 1) * 64, part * LANES : (part + 1) * LANES
                ]


def correlate(place, rows, cols, earlier):
    late = earlier is not None
    operands = [*rows, *cols]
    in_specs = [pl.BlockSpec(memory_space=pltpu.VMEM) for _ in operands]
    aliases = {}
    if late:
        in_specs.append(pl.BlockSpec(memory_space=pl.ANY))
        aliases = {1 + len(operands): 0}
        operands.append(earlier)
    return pl.pallas_call(
        functools.partial(correlate_kernel, late),
        grid_spec=pltpu.PrefetchScalarGridSpec(
            num_scalar_prefetch=1,
            grid=(8,),
            in_specs=in_specs,
            out_specs=pl.BlockSpec(
                (2, 2, 256, LANES),
                lambda g, place: (g, 0, 0, 1 - place[4] if late else place[4]),
            ),
        ),
        out_shape=jax.ShapeDtypeStruct((16, 2, 256, 256), jnp.float32),
        input_output_aliases=aliases,
        compiler_params=pltpu.CompilerParams(vmem_limit_bytes=20 * MIB),
        cost_estimate=pl.CostEstimate(
            flops=2**29, bytes_accessed=8 * MIB, transcendentals=0
        ),
    )(place, *operands)


def per_device(voltages, fir_taps, table):
    x, taps = prepared(voltages, fir_taps)
    pre = spectra(x, taps, table, True)
    own = spectra(x, taps, table, False)
    own = own.reshape(16, 128, LANES)
    pre = pre.reshape(16, 128, LANES)
    row, col = lax.axis_index("row"), lax.axis_index("col")
    place = jnp.stack([col, col ^ 1, col ^ 2, col ^ 3, row // 2, row % 2]).astype(jnp.int32)
    ring = range(4)
    up = [(r, (r + 1) % 4) for r in ring]
    down = [(r, (r - 1) % 4) for r in ring]
    rim = lax.ppermute(pre, "chan", [(s, s - 1) for s in range(1, 16)])
    whole = (own + rim.astype(jnp.float32)).astype(jnp.bfloat16)
    turned = lax.all_to_all(whole, "chan", split_axis=0, concat_axis=0, tiled=True)
    crossed = lax.ppermute(
        turned, ("row", "col"), [(4 * r + c, 4 * c + r) for r in ring for c in ring]
    )
    far = lax.ppermute(turned, "col", [(c, c ^ 2) for c in ring])
    near = lax.ppermute(turned, "col", [(c, c ^ 1) for c in ring])
    both = lax.ppermute(far, "col", [(c, c ^ 1) for c in ring])
    lower = lax.ppermute(crossed, "row", up)
    upper = lax.ppermute(crossed, "row", down)
    tails = [lax.ppermute(lower[:, :64], "row", up), lax.ppermute(upper[:, 64:], "row", down)]
    rows = [turned, near, far, both]
    result = correlate(place, rows, [crossed, lower, upper], None)
    return correlate(place, rows, [lower, upper, *tails], result)


def solution(mesh):
    table = dft_table()

    def run(voltages, fir_taps):
        return jax.shard_map(
            per_device,
            mesh=mesh,
            in_specs=(P(("row", "col"), "chan", None, None), P(), P()),
            out_specs=P("chan", None, "row", "col"),
            check_vma=False,
        )(voltages, fir_taps, jnp.asarray(table))

    return run
```

time: 108 us -> 104 us (0.963); the launches traced: 106 us -> 103 us
  waiting for transfers between devices: 24.7 us -> 20.1 us
    ppermute x5, waiting for transfers between devices: 8.25 us -> 3.65 us  [the longest x1 3.64 us: per_device(): rim = lax.ppermute(pre, 'chan', [(s, s - 1) for s in range(1, 16)])]
    pallas_call x3 -> x4, Pallas kernels: 28.4 us -> 29.2 us  [the longest x2 16.5 us: spectra(): pl.pallas_call(functools.partial(spectra_kernel, rim), grid=(64 // INPUTS...]
  transfers between devices with their start and end apart: 9 -> 9, of which waited for: 4 -> 3; matrix products, arithmetic and copies ran while one was open for 1% -> 1% of each run, Pallas kernels for 9% -> 14%
where the time goes in v3:
time: 104 us; the launch traced here: 103 us
  Pallas kernels  29.2 us (28%)
  blocking collectives  27.1 us (26%)
  starting transfers between devices  21.3 us (20%)
  waiting for transfers between devices  20.1 us (19%)
  local copies, waits for them, and re-layouts  4.12 us (4%)
  other arithmetic  1.35 us (1%)
    all_to_all x1, blocking collectives, per_device(): lax.all_to_all(whole, 'chan', split_axis=0, concat_axis=0, tiled=True)  27.1 us
    pallas_call x2, Pallas kernels, spectra(): pl.pallas_call(functools.partial(spectra_kernel, rim), grid=(64 // INPUTS...  16.5 us
    pallas_call x2, Pallas kernels, correlate(): pl.pallas_call(functools.partial(correlate_kernel, late), grid_spec=pltpu...  12.7 us
    ppermute x1, waiting for transfers between devices, per_device(): lax.ppermute(turned, ('row', 'col'), [(4 * r + c, 4 * c + r) for r in rin...  8.25 us
    ppermute x1, waiting for transfers between devices, per_device(): far = lax.ppermute(turned, 'col', [(c, c ^ 2) for c in ring])  8.16 us
    ppermute x1, starting transfers between devices, per_device(): lax.ppermute(turned, ('row', 'col'), [(4 * r + c, 4 * c + r) for r in rin...  6.71 us
    ppermute x1, starting transfers between devices, per_device(): near = lax.ppermute(turned, 'col', [(c, c ^ 1) for c in ring])  4.73 us
    ppermute x1, starting transfers between devices, per_device(): far = lax.ppermute(turned, 'col', [(c, c ^ 2) for c in ring])  4.22 us
  transfers between devices with their start and end apart: 9, of which 3 were waited for; matrix products, arithmetic and copies ran while one was open for 1% of the time, Pallas kernels for 14%

profile of v3, /device:TPU:1, one launch (start us, length us, event | category | flops | bytes accessed | tf_op | source)
XLA Modules:
  0.0 103.1 jit_solution(5539900253009353710)
XLA Ops:
  0.0 0.9 copy.6
  0.9 0.7 broadcast_in_dim.8
  1.5 8.0 %shard_map.38 = bf16[2048,128]{1,0:T(8,128)(2,1)} custom-call(bf16[64,8,32,128]{3,2,1,0:T(8,128)(2,1)} %bitcast.15, f32[8,32,128]{2,1,0:T(8,128)} %bitcast.18, bf16[2,256,1024]{2,1,0:T(8,128)(2,1)} %constant.36.clone.table_ref), custom_call_target="tpu_custom_call" | custom-call | flops 1073741824 | bytes 6291456 | tf_op jit(solution)/shard_map/pallas_call | solution.py:118
  9.5 1.3 %collective-permute-start = (bf16[16,128,128]{2,1,0:T(8,128)(2,1)}, bf16[16,128,128]{2,1,0:T(8,128)(2,1)S(1)}, u32[]{:S(2)}, u32[]{:S(2)}) collective-permute-start(bf16[16,128,128]{2,1,0:T(8,128)(2,1)} %bitcast.20), channel_id=1, source_target_pairs={{16,0},{32,16},{48,32},{64,48},{80,64},{96,80},{112,96},{128,112},... | collective-permute-start | bytes 1572872 | tf_op jit(solution)/shard_map/ppermute | solution.py:228
  10.8 8.5 %shard_map.37 = f32[2048,128]{1,0:T(8,128)} custom-call(bf16[64,8,32,128]{3,2,1,0:T(8,128)(2,1)} %bitcast.16, f32[8,32,128]{2,1,0:T(8,128)} %bitcast.19, bf16[2,256,1024]{2,1,0:T(8,128)(2,1)} %constant.36.clone.table_ref), custom_call_target="tpu_custom_call" | custom-call | flops 1073741824 | bytes 6291456 | tf_op jit(solution)/shard_map/pallas_call | solution.py:118
  19.3 3.6 %collective-permute-done = bf16[16,128,128]{2,1,0:T(8,128)(2,1)S(1)} collective-permute-done((bf16[16,128,128]{2,1,0:T(8,128)(2,1)}, bf16[16,128,128]{2,1,0:T(8,128)(2,1)S(1)}, u32[]{:S(2)}, u32[]{:S(2)}) %collective-permute-start) | collective-permute-done | bytes 524320 | tf_op jit(solution)/shard_map/ppermute | solution.py:228
  23.0 1.4 %add_convert_fusion = bf16[16,128,128]{2,1,0:T(8,128)(2,1)S(1)} fusion(f32[16,128,128]{2,1,0:T(8,128)} %bitcast.17, bf16[16,128,128]{2,1,0:T(8,128)(2,1)S(1)} %collective-permute-done), kind=kLoop, calls=%fused_computation | loop fusion | flops 786432 | bytes 2097152 | tf_op jit(solution)/shard_map/convert_element_type | solution.py:229
  24.3 27.1 %all_to_all.5.refs_0_ = bf16[16,128,128]{2,1,0:T(8,128)(2,1)S(1)} all-to-all(bf16[16,128,128]{2,1,0:T(8,128)(2,1)S(1)} %add_convert_fusion), channel_id=1, replica_groups=mesh['chan'=16,'row'=4,'col'=4] {'chan'}, dimensions={0} | all-to-all | bytes 1048576 | tf_op jit(solution)/shard_map/all_to_all | solution.py:230
  51.5 6.7 %collective-permute-start.4 = (bf16[16,128,128]{2,1,0:T(8,128)(2,1)S(1)}, bf16[16,128,128]{2,1,0:T(8,128)(2,1)S(1)}, u32[]{:S(2)}, u32[]{:S(2)}) collective-permute-start(bf16[16,128,128]{2,1,0:T(8,128)(2,1)S(1)} %all_to_all.5.refs_0_), channel_id=1, source_target_pairs={{0,0},{1,4},{2,8},{3,12},{4,1},{5,5},{6,9},{7,13},{8,2},{9,6},{10,... | collective-permute-start | bytes 1572872 | tf_op jit(solution)/shard_map/ppermute | solution.py:231
  58.2 4.2 %collective-permute-start.2 = (bf16[16,128,128]{2,1,0:T(8,128)(2,1)S(1)}, bf16[16,128,128]{2,1,0:T(8,128)(2,1)S(1)}, u32[]{:S(2)}, u32[]{:S(2)}) collective-permute-start(bf16[16,128,128]{2,1,0:T(8,128)(2,1)S(1)} %all_to_all.5.refs_0_), channel_id=1, source_target_pairs={{0,2},{1,3},{2,0},{3,1},{4,6},{5,7},{6,4},{7,5},{8,10},{9,11},{10,... | collective-permute-start | bytes 1572872 | tf_op jit(solution)/shard_map/ppermute | solution.py:234
  62.4 8.2 %collective-permute-done.4.refs_4_ = bf16[16,128,128]{2,1,0:T(8,128)(2,1)S(1)} collective-permute-done((bf16[16,128,128]{2,1,0:T(8,128)(2,1)S(1)}, bf16[16,128,128]{2,1,0:T(8,128)(2,1)S(1)}, u32[]{:S(2)}, u32[]{:S(2)}) %collective-permute-start.4) | collective-permute-done | bytes 524320 | tf_op jit(solution)/shard_map/ppermute | solution.py:231
  70.6 0.0 copy-start
  70.6 1.7 %collective-permute-start.6 = (bf16[16,128,128]{2,1,0:T(8,128)(2,1)S(1)}, bf16[16,128,128]{2,1,0:T(8,128)(2,1)S(1)}, u32[]{:S(2)}, u32[]{:S(2)}) collective-permute-start(bf16[16,128,128]{2,1,0:T(8,128)(2,1)S(1)} %collective-permute-done.4.refs_4_), channel_id=1, source_target_pairs={{0,12},{4,0},{8,4},{12,8},{1,13},{5,1},{9,5},{13,9},{2,14},{6,2},{... | collective-permute-start | bytes 1572872 | tf_op jit(solution)/shard_map/ppermute | solution.py:238
  72.4 0.0 collective-permute-start.5
  72.4 4.7 %collective-permute-start.1 = (bf16[16,128,128]{2,1,0:T(8,128)(2,1)S(1)}, bf16[16,128,128]{2,1,0:T(8,128)(2,1)S(1)}, u32[]{:S(2)}, u32[]{:S(2)}) collective-permute-start(bf16[16,128,128]{2,1,0:T(8,128)(2,1)S(1)} %all_to_all.5.refs_0_), channel_id=1, source_target_pairs={{0,1},{1,0},{2,3},{3,2},{4,5},{5,4},{6,7},{7,6},{8,9},{9,8},{10,11... | collective-permute-start | bytes 1572872 | tf_op jit(solution)/shard_map/ppermute | solution.py:235
  77.1 8.2 %collective-permute-done.2.refs_2_ = bf16[16,128,128]{2,1,0:T(8,128)(2,1)S(1)} collective-permute-done((bf16[16,128,128]{2,1,0:T(8,128)(2,1)S(1)}, bf16[16,128,128]{2,1,0:T(8,128)(2,1)S(1)}, u32[]{:S(2)}, u32[]{:S(2)}) %collective-permute-start.2) | collective-permute-done | bytes 524320 | tf_op jit(solution)/shard_map/ppermute | solution.py:234
  85.3 1.1 %collective-permute-start.3 = (bf16[16,128,128]{2,1,0:T(8,128)(2,1)S(1)}, bf16[16,128,128]{2,1,0:T(8,128)(2,1)S(1)}, u32[]{:S(2)}, u32[]{:S(2)}) collective-permute-start(bf16[16,128,128]{2,1,0:T(8,128)(2,1)S(1)} %collective-permute-done.2.refs_2_), channel_id=1, source_target_pairs={{0,1},{1,0},{2,3},{3,2},{4,5},{5,4},{6,7},{7,6},{8,9},{9,8},{10,11... | collective-permute-start | bytes 1572872 | tf_op jit(solution)/shard_map/ppermute | solution.py:236
  86.4 0.0 collective-permute-done.6.refs_6_.refs_5_
  86.4 0.7 slice.9
  87.1 0.0 collective-permute-start.8
  87.1 0.0 collective-permute-done.5.refs_5_.refs_4_
  87.1 0.0 copy-done
  87.1 0.7 slice.8
  87.9 1.5 %collective-permute-start.7 = (bf16[16,64,128]{2,1,0:T(8,128)(2,1)}, bf16[16,64,128]{2,1,0:T(8,128)(2,1)}, u32[]{:S(2)}, u32[]{:S(2)}) collective-permute-start(bf16[16,64,128]{2,1,0:T(8,128)(2,1)} %slice.8), channel_id=1, source_target_pairs={{0,4},{4,8},{8,12},{12,0},{1,5},{5,9},{9,13},{13,1},{2,6},{6,10},{... | collective-permute-start | bytes 786440 | tf_op jit(solution)/shard_map/ppermute | solution.py:239
  89.3 0.1 stack.27.place_ref
  89.4 0.0 collective-permute-done.1.refs_1_
  89.4 0.0 collective-permute-done.3.refs_3_
  89.4 0.0 copy-start.1
  89.4 1.0 %copy-done.1 = bf16[16,128,128]{2,1,0:T(8,128)(2,1)S(1)} copy-done((bf16[16,128,128]{2,1,0:T(8,128)(2,1)S(1)}, bf16[16,128,128]{2,1,0:T(8,128)(2,1)}, u32[]{:S(2)}) %copy-start.1) | copy-done | bytes 524312
  90.5 5.9 %shard_map.39.refs_8_ = f32[16,2,256,256]{3,2,1,0:T(8,128)} custom-call(s32[6]{0:T(128)S(1)} %stack.27.place_ref, bf16[16,128,128]{2,1,0:T(8,128)(2,1)S(1)} %all_to_all.5.refs_0_, bf16[16,128,128]{2,1,0:T(8,128)(2,1)S(1)} %collective-permute-done.1.refs_1_, bf16[16,128,128]{2,1,0:T(8,128)(2,1)S(1)} %collective-permute-done.2.refs_2_, ...), custom_call_target="tpu_custom_call" | custom-call | flops 536870912 | bytes 8388608 | tf_op jit(solution)/shard_map/pallas_call | solution.py:197
  96.3 0.0 collective-permute-done.8.refs_7_
  96.3 0.0 collective-permute-done.7.refs_6_
  96.3 6.8 %shard_map.40 = f32[16,2,256,256]{3,2,1,0:T(8,128)} custom-call(s32[6]{0:T(128)S(1)} %stack.27.place_ref, bf16[16,128,128]{2,1,0:T(8,128)(2,1)S(1)} %all_to_all.5.refs_0_, bf16[16,128,128]{2,1,0:T(8,128)(2,1)S(1)} %collective-permute-done.1.refs_1_, bf16[16,128,128]{2,1,0:T(8,128)(2,1)S(1)} %collective-permute-done.2.refs_2_, ...), custom_call_target="tpu_custom_call", output_to_operand_aliasing={{}: (9, {})} | custom-call | flops 536870912 | bytes 8388608 | tf_op jit(solution)/shard_map/pallas_call | solution.py:197
Async XLA Ops:
  9.5 13.5 %collective-permute-start = (bf16[16,128,128]{2,1,0:T(8,128)(2,1)}, bf16[16,128,128]{2,1,0:T(8,128)(2,1)S(1)}, u32[]{:S(2)}, u32[]{:S(2)}) collective-permute-start(bf16[16,128,128]{2,1,0:T(8,128)(2,1)} %bitcast.20), channel_id=1, source_target_pairs={{16,0},{32,16},{48,32},{64,48},{80,64},{96,80},{112,96},{128,112},... | collective-permute-start | bytes 1572872 | tf_op jit(solution)/shard_map/ppermute | solution.py:228
  51.5 19.2 %collective-permute-start.4 = (bf16[16,128,128]{2,1,0:T(8,128)(2,1)S(1)}, bf16[16,128,128]{2,1,0:T(8,128)(2,1)S(1)}, u32[]{:S(2)}, u32[]{:S(2)}) collective-permute-start(bf16[16,128,128]{2,1,0:T(8,128)(2,1)S(1)} %all_to_all.5.refs_0_), channel_id=1, source_target_pairs={{0,0},{1,4},{2,8},{3,12},{4,1},{5,5},{6,9},{7,13},{8,2},{9,6},{10,... | collective-permute-start | bytes 1572872 | tf_op jit(solution)/shard_map/ppermute | solution.py:231
  58.2 27.1 %collective-permute-start.2 = (bf16[16,128,128]{2,1,0:T(8,128)(2,1)S(1)}, bf16[16,128,128]{2,1,0:T(8,128)(2,1)S(1)}, u32[]{:S(2)}, u32[]{:S(2)}) collective-permute-start(bf16[16,128,128]{2,1,0:T(8,128)(2,1)S(1)} %all_to_all.5.refs_0_), channel_id=1, source_target_pairs={{0,2},{1,3},{2,0},{3,1},{4,6},{5,7},{6,4},{7,5},{8,10},{9,11},{10,... | collective-permute-start | bytes 1572872 | tf_op jit(solution)/shard_map/ppermute | solution.py:234
  70.6 16.5 %copy-start = (bf16[16,128,128]{2,1,0:T(8,128)(2,1)}, bf16[16,128,128]{2,1,0:T(8,128)(2,1)S(1)}, u32[]{:S(2)}) copy-start(bf16[16,128,128]{2,1,0:T(8,128)(2,1)S(1)} %collective-permute-done.4.refs_4_) | copy-start | bytes 1572868
  70.6 15.8 %collective-permute-start.6 = (bf16[16,128,128]{2,1,0:T(8,128)(2,1)S(1)}, bf16[16,128,128]{2,1,0:T(8,128)(2,1)S(1)}, u32[]{:S(2)}, u32[]{:S(2)}) collective-permute-start(bf16[16,128,128]{2,1,0:T(8,128)(2,1)S(1)} %collective-permute-done.4.refs_4_), channel_id=1, source_target_pairs={{0,12},{4,0},{8,4},{12,8},{1,13},{5,1},{9,5},{13,9},{2,14},{6,2},{... | collective-permute-start | bytes 1572872 | tf_op jit(solution)/shard_map/ppermute | solution.py:238
  72.4 14.7 %collective-permute-start.5 = (bf16[16,128,128]{2,1,0:T(8,128)(2,1)S(1)}, bf16[16,128,128]{2,1,0:T(8,128)(2,1)S(1)}, u32[]{:S(2)}, u32[]{:S(2)}) collective-permute-start(bf16[16,128,128]{2,1,0:T(8,128)(2,1)S(1)} %collective-permute-done.4.refs_4_), channel_id=1, source_target_pairs={{0,4},{4,8},{8,12},{12,0},{1,5},{5,9},{9,13},{13,1},{2,6},{6,10},{... | collective-permute-start | bytes 1572872 | tf_op jit(solution)/shard_map/ppermute | solution.py:237
  72.4 17.0 %collective-permute-start.1 = (bf16[16,128,128]{2,1,0:T(8,128)(2,1)S(1)}, bf16[16,128,128]{2,1,0:T(8,128)(2,1)S(1)}, u32[]{:S(2)}, u32[]{:S(2)}) collective-permute-start(bf16[16,128,128]{2,1,0:T(8,128)(2,1)S(1)} %all_to_all.5.refs_0_), channel_id=1, source_target_pairs={{0,1},{1,0},{2,3},{3,2},{4,5},{5,4},{6,7},{7,6},{8,9},{9,8},{10,11... | collective-permute-start | bytes 1572872 | tf_op jit(solution)/shard_map/ppermute | solution.py:235
  85.3 4.1 %collective-permute-start.3 = (bf16[16,128,128]{2,1,0:T(8,128)(2,1)S(1)}, bf16[16,128,128]{2,1,0:T(8,128)(2,1)S(1)}, u32[]{:S(2)}, u32[]{:S(2)}) collective-permute-start(bf16[16,128,128]{2,1,0:T(8,128)(2,1)S(1)} %collective-permute-done.2.refs_2_), channel_id=1, source_target_pairs={{0,1},{1,0},{2,3},{3,2},{4,5},{5,4},{6,7},{7,6},{8,9},{9,8},{10,11... | collective-permute-start | bytes 1572872 | tf_op jit(solution)/shard_map/ppermute | solution.py:236
  87.1 9.2 %collective-permute-start.8 = (bf16[16,64,128]{2,1,0:T(8,128)(2,1)}, bf16[16,64,128]{2,1,0:T(8,128)(2,1)S(1)}, u32[]{:S(2)}, u32[]{:S(2)}) collective-permute-start(bf16[16,64,128]{2,1,0:T(8,128)(2,1)} %slice.9), channel_id=1, source_target_pairs={{0,12},{4,0},{8,4},{12,8},{1,13},{5,1},{9,5},{13,9},{2,14},{6,2},{... | collective-permute-start | bytes 786440 | tf_op jit(solution)/shard_map/ppermute | solution.py:239
  87.9 8.5 %collective-permute-start.7 = (bf16[16,64,128]{2,1,0:T(8,128)(2,1)}, bf16[16,64,128]{2,1,0:T(8,128)(2,1)}, u32[]{:S(2)}, u32[]{:S(2)}) collective-permute-start(bf16[16,64,128]{2,1,0:T(8,128)(2,1)} %slice.8), channel_id=1, source_target_pairs={{0,4},{4,8},{8,12},{12,0},{1,5},{5,9},{9,13},{13,1},{2,6},{6,10},{... | collective-permute-start | bytes 786440 | tf_op jit(solution)/shard_map/ppermute | solution.py:239
  89.4 1.0 %copy-start.1 = (bf16[16,128,128]{2,1,0:T(8,128)(2,1)S(1)}, bf16[16,128,128]{2,1,0:T(8,128)(2,1)}, u32[]{:S(2)}) copy-start(bf16[16,128,128]{2,1,0:T(8,128)(2,1)} %copy-done) | copy-start | bytes 1572868

commit v4 on v3

v4 whole, which is shorter than its diff:
```python
import functools
import math

import jax
import jax.numpy as jnp
import numpy as np
from jax import lax
from jax.experimental import pallas as pl
from jax.experimental.pallas import tpu as pltpu
from jax.sharding import PartitionSpec as P

import ml_dtypes

NCH = 2048
KEEP = 256
TAPS = 8
PITCH = 521
VLIM = 56
INPUTS = 8
UNROLL = 2
GROUP = 16
LANES = 128
MIB = 1 << 20


def dft_table():
    index = np.arange(NCH, dtype=np.int64)
    chosen = np.arange(KEEP, dtype=np.int64)
    phase = (index[:, None] * chosen[None, :] % NCH).astype(np.float32) * np.float32(
        2.0 * math.pi / NCH
    )
    cosine = np.cos(phase) / np.float32(math.sqrt(NCH))
    sine = np.sin(phase) / np.float32(math.sqrt(NCH))
    table = np.stack([cosine, sine], axis=0)[:, : NCH // 2]
    table = table.reshape(2, NCH // 2, KEEP // 2, 2).transpose(3, 0, 2, 1)
    return np.ascontiguousarray(table.reshape(2, KEEP, NCH // 2)).astype(ml_dtypes.bfloat16)


def spectra_kernel(
    rim, x_any, raw_ref, table_any, out_ref,
    x_ref, taps_ref, loose_ref, table_ref, fir_ref, wide_ref, acc_ref, x_sem, table_sem,
):
    blocks = 64 // INPUTS
    loads = [
        pltpu.make_async_copy(
            x_any.at[pl.ds(b * INPUTS, INPUTS)], x_ref.at[pl.ds(b * INPUTS, INPUTS)], x_sem.at[b]
        )
        for b in range(blocks)
    ]
    for load in loads:
        load.start()
    table_load = pltpu.make_async_copy(table_any, table_ref, table_sem)
    table_load.start()
    for cb in range(16):
        chunk = raw_ref[:, cb * LANES : (cb + 1) * LANES]
        for p in range(2):
            loose_ref[pl.ds(cb * 2 + p, TAPS, stride=33), :] = chunk
    for k in range(TAPS):
        taps_ref[k] = loose_ref[pl.ds(k * 33, 32), :]

    if rim:
        for rho in range(2 * GROUP):
            fir_ref[pl.ds(rho * PITCH, 64), :] = jnp.zeros((64, LANES), jnp.float32)

    def filter_input(i, carry):
        for piece in range(2):
            rows = slice(8 * piece, 8 * piece + 8)
            halves = []
            for part in range(2):
                taps = [taps_ref[k, pl.ds(16 * part + 8 * piece, 8), :] for k in range(TAPS)]
                frame = [
                    x_ref[i, t, pl.ds(16 * part, 16), :].astype(jnp.float32)[rows]
                    for t in range(TAPS)
                ]
                totals = []
                for t in range(1 if rim else 0, TAPS):
                    pairs = [(f, TAPS - t + f) for f in range(t)] if rim else [
                        (t + k, k) for k in range(TAPS - t)
                    ]
                    total = None
                    for f, k in pairs:
                        term = frame[f] * taps[k]
                        total = term if total is None else total + term
                    totals.append(total)
                halves.append(totals)
            for t, (early, late) in enumerate(zip(*halves), 1 if rim else 0):
                base = t * 64 + i + 8 * piece * PITCH
                fir_ref[pl.ds(base, 8, stride=PITCH), :] = early + late
                fir_ref[pl.ds(base + GROUP * PITCH, 8, stride=PITCH), :] = early - late
        return carry

    for b, load in enumerate(loads):
        load.wait()
        lax.fori_loop(b * INPUTS, (b + 1) * INPUTS, filter_input, 0)

    table_load.wait()
    def transform(low_bit, carry):
        for p in range(2):
            for cb in range(8):
                wide_ref[:, pl.ds(cb * LANES, LANES)] = fir_ref[
                    pl.ds((low_bit * GROUP + cb * 2 + p) * PITCH, 512), :
                ].astype(jnp.bfloat16)
            acc_ref[low_bit, p] = lax.dot_general(
                table_ref[low_bit],
                wide_ref[...],
                (((1,), (1,)), ((), ())),
                preferred_element_type=jnp.float32,
            )
        return carry

    lax.fori_loop(0, 2, transform, 0, unroll=True)

    low = lax.broadcasted_iota(jnp.int32, (128, LANES), 1) < 64
    for t2 in range(4):
        lanes = pl.ds(t2 * LANES, LANES)
        for p in range(2):
            pair = []
            for low_bit in range(2):
                cosine = acc_ref[low_bit, p, pl.ds(0, 128), lanes]
                sine = acc_ref[low_bit, 1 - p, pl.ds(128, 128), lanes]
                pair.append(cosine + sine if p == 0 else cosine - sine)
            zero, one = pair
            even = jnp.where(low, zero, pltpu.roll(one, 64, 1))
            odd = jnp.where(low, pltpu.roll(zero, 64, 1), one)
            row = p * 8 + 2 * t2
            fir_ref[pl.ds(row, 128, stride=17), :] = even
            fir_ref[pl.ds(row + 1, 128, stride=17), :] = odd
    for pair in range(128):
        out_ref[pl.ds(pair * 16, 16), :] = fir_ref[pl.ds(pair * 17, 16), :].astype(
            out_ref.dtype
        )


def spectra(x, taps, table, rim):
    return pl.pallas_call(
        functools.partial(spectra_kernel, rim),
        in_specs=[
            pl.BlockSpec(memory_space=pl.ANY),
            pl.BlockSpec(memory_space=pltpu.VMEM),
            pl.BlockSpec(memory_space=pl.ANY),
        ],
        out_specs=pl.BlockSpec(memory_space=pltpu.VMEM),
        out_shape=jax.ShapeDtypeStruct((2048, LANES), jnp.bfloat16 if rim else jnp.float32),
        scratch_shapes=[
            pltpu.VMEM((64, 8, 32, LANES), jnp.bfloat16),
            pltpu.VMEM((TAPS, 32, LANES), jnp.float32),
            pltpu.VMEM((TAPS * 33, LANES), jnp.float32),
            pltpu.VMEM((2, KEEP, NCH // 2), jnp.bfloat16),
            pltpu.VMEM((2 * GROUP * PITCH, LANES), jnp.float32),
            pltpu.VMEM((512, NCH // 2), jnp.bfloat16),
            pltpu.VMEM((2, 2, KEEP, 512), jnp.float32),
            pltpu.SemaphoreType.DMA((64 // INPUTS,)),
            pltpu.SemaphoreType.DMA,
        ],
        compiler_params=pltpu.CompilerParams(vmem_limit_bytes=VLIM * MIB),
        cost_estimate=pl.CostEstimate(
            flops=2 * 512 * 2048 * 512, bytes_accessed=6 * MIB, transcendentals=0
        ),
    )(x, taps, table)


def prepared(voltages, fir_taps):
    x = voltages.reshape(64, 8, 2, 16, LANES).transpose(0, 1, 3, 2, 4).reshape(64, 8, 32, LANES)
    return x, fir_taps


def correlate_kernel(late, place_ref, *refs):
    rows, cols, out_ref, full_ref, sem = refs[:4], refs[4:8], refs[-3], refs[-2], refs[-1]
    odd = place_ref[5] == 1
    half = 1 - place_ref[4] if late else place_ref[4]
    lane = pl.multiple_of(half * LANES, LANES)

    def store(step):
        return pltpu.make_async_copy(
            full_ref.at[step],
            out_ref.at[pl.ds(2 * step, 2), :, :, pl.ds(lane, LANES)],
            sem.at[step],
        )

    def pair_of_channels(step, carry):
        at = pl.ds(pl.multiple_of(step * 16, 16), 16)

        def block(ref):
            return ref[:, at, :].reshape(256, LANES)

        left_blocks = [block(ref) for ref in rows]
        if late:
            tail = pl.ds(pl.multiple_of(step % 4 * 16, 16), 16)
            far = jnp.where(step < 4, cols[2][:, tail, :], cols[3][:, tail, :])
            far = far.reshape(256, LANES)
            right_blocks = [
                jnp.where(odd, block(cols[1]), far), jnp.where(odd, far, block(cols[0]))
            ]
        else:
            mine = block(cols[0])
            right_blocks = [
                jnp.where(odd, block(cols[1]), mine), jnp.where(odd, mine, block(cols[2]))
            ]
        for channel in range(2):
            lanes = slice(64 * channel, 64 * channel + 64)
            left = jnp.concatenate([b[:, lanes] for b in left_blocks], axis=1)
            right = jnp.concatenate([b[:, lanes] for b in right_blocks], axis=1)
            pairs = right.astype(jnp.float32).reshape(16, 2, 8, LANES)
            flipped = jnp.concatenate([-pairs[:, 1:], pairs[:, :1]], axis=1)
            flipped = flipped.reshape(256, LANES).astype(jnp.bfloat16)
            product = lax.dot_general(
                left,
                jnp.concatenate([right, flipped], axis=1),
                (((0,), (0,)), ((), ())),
                preferred_element_type=jnp.float32,
            ) * (1.0 / 128.0)
            for k in range(4):
                where = pl.ds(pl.multiple_of(place_ref[k] * 64, 64), 64)
                for part in range(2):
                    full_ref[step, channel, part, where, :] = product[
                        k * 64 : (k + 1) * 64, part * LANES : (part + 1) * LANES
                    ]
        store(step).start()
        return carry

    lax.fori_loop(0, 8, pair_of_channels, 0, unroll=UNROLL)
    for step in range(8):
        store(step).wait()


def correlate(place, rows, cols, earlier):
    late = earlier is not None
    operands = [*rows, *cols]
    in_specs = [pl.BlockSpec(memory_space=pltpu.SMEM)]
    in_specs += [pl.BlockSpec(memory_space=pltpu.VMEM) for _ in operands]
    aliases = {}
    if late:
        in_specs.append(pl.BlockSpec(memory_space=pl.ANY))
        aliases = {1 + len(operands): 0}
        operands.append(earlier)
    return pl.pallas_call(
        functools.partial(correlate_kernel, late),
        in_specs=in_specs,
        out_specs=pl.BlockSpec(memory_space=pl.ANY),
        out_shape=jax.ShapeDtypeStruct((16, 2, 256, 256), jnp.float32),
        scratch_shapes=[
            pltpu.VMEM((8, 2, 2, 256, LANES), jnp.float32),
            pltpu.SemaphoreType.DMA((8,)),
        ],
        input_output_aliases=aliases,
        compiler_params=pltpu.CompilerParams(vmem_limit_bytes=20 * MIB),
        cost_estimate=pl.CostEstimate(
            flops=2**29, bytes_accessed=8 * MIB, transcendentals=0
        ),
    )(place, *operands)


def per_device(voltages, fir_taps, table):
    x, taps = prepared(voltages, fir_taps)
    pre = spectra(x, taps, table, True)
    own = spectra(x, taps, table, False)
    own = own.reshape(16, 128, LANES)
    pre = pre.reshape(16, 128, LANES)
    row, col = lax.axis_index("row"), lax.axis_index("col")
    place = jnp.stack([col, col ^ 1, col ^ 2, col ^ 3, row // 2, row % 2]).astype(jnp.int32)
    ring = range(4)
    up = [(r, (r + 1) % 4) for r in ring]
    down = [(r, (r - 1) % 4) for r in ring]
    rim = lax.ppermute(pre, "chan", [(s, s - 1) for s in range(1, 16)])
    whole = (own + rim.astype(jnp.float32)).astype(jnp.bfloat16)
    turned = lax.all_to_all(whole, "chan", split_axis=0, concat_axis=0, tiled=True)
    crossed = lax.ppermute(
        turned, ("row", "col"), [(4 * r + c, 4 * c + r) for r in ring for c in ring]
    )
    far = lax.ppermute(turned, "col", [(c, c ^ 2) for c in ring])
    near = lax.ppermute(turned, "col", [(c, c ^ 1) for c in ring])
    both = lax.ppermute(far, "col", [(c, c ^ 1) for c in ring])
    lower = lax.ppermute(crossed, "row", up)
    upper = lax.ppermute(crossed, "row", down)
    tails = [lax.ppermute(lower[:, :64], "row", up), lax.ppermute(upper[:, 64:], "row", down)]
    rows = [turned, near, far, both]
    result = correlate(place, rows, [crossed, lower, upper], None)
    return correlate(place, rows, [lower, upper, *tails], result)


def solution(mesh):
    table = dft_table()

    def run(voltages, fir_taps):
        return jax.shard_map(
            per_device,
            mesh=mesh,
            in_specs=(P(("row", "col"), "chan", None, None), P(), P()),
            out_specs=P("chan", None, "row", "col"),
            check_vma=False,
        )(voltages, fir_taps, jnp.asarray(table))

    return run
```

time: 104 us -> 98.6 us (0.948)
  Pallas kernels: 29.2 us -> 23.2 us
  waiting for transfers between devices: 20.1 us -> 21.8 us
  local copies, waits for them, and re-layouts: 4.12 us -> 2.57 us
    pallas_call x4, Pallas kernels: 29.2 us -> 23.2 us  [the longest x2 14.7 us: spectra(): pl.pallas_call(functools.partial(spectra_kernel, rim), in_specs=[pl.Block...]
    broadcast_in_dim x2 -> x0, local copies, waits for them, and re-layouts: 1.54 us -> none  [prepared(): taps = jnp.broadcast_to(taps, (TAPS, 16, 2, LANES)).reshape(TAPS, 32, LANES)]
  transfers between devices with their start and end apart: 9 -> 9, of which waited for: 3 -> 4; matrix products, arithmetic and copies ran while one was open for 1% -> 2% of each run, Pallas kernels for 14% -> 12%
where the time goes in v4:
time: 98.6 us; the launch traced here: 97.3 us
  blocking collectives  27.1 us (27%)
  Pallas kernels  23.2 us (24%)
  waiting for transfers between devices  21.8 us (22%)
  starting transfers between devices  21.2 us (22%)
  local copies, waits for them, and re-layouts  2.57 us (3%)
  other arithmetic  1.35 us (1%)
    all_to_all x1, blocking collectives, per_device(): lax.all_to_all(whole, 'chan', split_axis=0, concat_axis=0, tiled=True)  27.1 us
    pallas_call x2, Pallas kernels, spectra(): pl.pallas_call(functools.partial(spectra_kernel, rim), in_specs=[pl.Block...  14.7 us
    pallas_call x2, Pallas kernels, correlate(): pl.pallas_call(functools.partial(correlate_kernel, late), in_specs=in_spe...  8.45 us
    ppermute x1, waiting for transfers between devices, per_device(): lax.ppermute(turned, ('row', 'col'), [(4 * r + c, 4 * c + r) for r in rin...  8.27 us
    ppermute x1, waiting for transfers between devices, per_device(): far = lax.ppermute(turned, 'col', [(c, c ^ 2) for c in ring])  8.16 us
    ppermute x1, starting transfers between devices, per_device(): lax.ppermute(turned, ('row', 'col'), [(4 * r + c, 4 * c + r) for r in rin...  6.7 us
    ppermute x1, starting transfers between devices, per_device(): near = lax.ppermute(turned, 'col', [(c, c ^ 1) for c in ring])  4.74 us
    ppermute x1, waiting for transfers between devices, per_device(): rim = lax.ppermute(pre, 'chan', [(s, s - 1) for s in range(1, 16)])  4.42 us
  transfers between devices with their start and end apart: 9, of which 4 were waited for; matrix products, arithmetic and copies ran while one was open for 2% of the time, Pallas kernels for 12%

profile of v4, /device:TPU:1, one launch (start us, length us, event | category | flops | bytes accessed | tf_op | source)
XLA Modules:
  0.0 97.3 jit_solution(7173277763095182518)
XLA Ops:
  0.0 7.0 %shard_map.38 = bf16[2048,128]{1,0:T(8,128)(2,1)} custom-call(bf16[64,8,32,128]{3,2,1,0:T(8,128)(2,1)} %bitcast.13, f32[8,2048]{1,0:T(8,128)} %raw_ref.3, bf16[2,256,1024]{2,1,0:T(8,128)(2,1)} %constant.36.clone.table_any), custom_call_target="tpu_custom_call" | custom-call | flops 1073741824 | bytes 6291456 | tf_op jit(solution)/shard_map/pallas_call | solution.py:135
  7.0 1.3 %collective-permute-start = (bf16[16,128,128]{2,1,0:T(8,128)(2,1)}, bf16[16,128,128]{2,1,0:T(8,128)(2,1)S(1)}, u32[]{:S(2)}, u32[]{:S(2)}) collective-permute-start(bf16[16,128,128]{2,1,0:T(8,128)(2,1)} %bitcast.16), channel_id=1, source_target_pairs={{16,0},{32,16},{48,32},{64,48},{80,64},{96,80},{112,96},{128,112},... | collective-permute-start | bytes 1572872 | tf_op jit(solution)/shard_map/ppermute | solution.py:264
  8.3 7.7 %shard_map.37 = f32[2048,128]{1,0:T(8,128)} custom-call(bf16[64,8,32,128]{3,2,1,0:T(8,128)(2,1)} %bitcast.14, f32[8,2048]{1,0:T(8,128)} %raw_ref.3, bf16[2,256,1024]{2,1,0:T(8,128)(2,1)} %constant.36.clone.table_any), custom_call_target="tpu_custom_call" | custom-call | flops 1073741824 | bytes 6291456 | tf_op jit(solution)/shard_map/pallas_call | solution.py:135
  16.0 4.4 %collective-permute-done = bf16[16,128,128]{2,1,0:T(8,128)(2,1)S(1)} collective-permute-done((bf16[16,128,128]{2,1,0:T(8,128)(2,1)}, bf16[16,128,128]{2,1,0:T(8,128)(2,1)S(1)}, u32[]{:S(2)}, u32[]{:S(2)}) %collective-permute-start) | collective-permute-done | bytes 524320 | tf_op jit(solution)/shard_map/ppermute | solution.py:264
  20.5 1.4 %add_convert_fusion = bf16[16,128,128]{2,1,0:T(8,128)(2,1)S(1)} fusion(f32[16,128,128]{2,1,0:T(8,128)} %bitcast.15, bf16[16,128,128]{2,1,0:T(8,128)(2,1)S(1)} %collective-permute-done), kind=kLoop, calls=%fused_computation | loop fusion | flops 786432 | bytes 2097152 | tf_op jit(solution)/shard_map/convert_element_type | solution.py:265
  21.8 27.1 %all_to_all.5.refs_0_ = bf16[16,128,128]{2,1,0:T(8,128)(2,1)S(1)} all-to-all(bf16[16,128,128]{2,1,0:T(8,128)(2,1)S(1)} %add_convert_fusion), channel_id=1, replica_groups=mesh['chan'=16,'row'=4,'col'=4] {'chan'}, dimensions={0} | all-to-all | bytes 1048576 | tf_op jit(solution)/shard_map/all_to_all | solution.py:266
  49.0 6.7 %collective-permute-start.4 = (bf16[16,128,128]{2,1,0:T(8,128)(2,1)S(1)}, bf16[16,128,128]{2,1,0:T(8,128)(2,1)S(1)}, u32[]{:S(2)}, u32[]{:S(2)}) collective-permute-start(bf16[16,128,128]{2,1,0:T(8,128)(2,1)S(1)} %all_to_all.5.refs_0_), channel_id=1, source_target_pairs={{0,0},{1,4},{2,8},{3,12},{4,1},{5,5},{6,9},{7,13},{8,2},{9,6},{10,... | collective-permute-start | bytes 1572872 | tf_op jit(solution)/shard_map/ppermute | solution.py:267
  55.7 4.2 %collective-permute-start.2 = (bf16[16,128,128]{2,1,0:T(8,128)(2,1)S(1)}, bf16[16,128,128]{2,1,0:T(8,128)(2,1)S(1)}, u32[]{:S(2)}, u32[]{:S(2)}) collective-permute-start(bf16[16,128,128]{2,1,0:T(8,128)(2,1)S(1)} %all_to_all.5.refs_0_), channel_id=1, source_target_pairs={{0,2},{1,3},{2,0},{3,1},{4,6},{5,7},{6,4},{7,5},{8,10},{9,11},{10,... | collective-permute-start | bytes 1572872 | tf_op jit(solution)/shard_map/ppermute | solution.py:270
  59.9 8.3 %collective-permute-done.4.refs_4_ = bf16[16,128,128]{2,1,0:T(8,128)(2,1)S(1)} collective-permute-done((bf16[16,128,128]{2,1,0:T(8,128)(2,1)S(1)}, bf16[16,128,128]{2,1,0:T(8,128)(2,1)S(1)}, u32[]{:S(2)}, u32[]{:S(2)}) %collective-permute-start.4) | collective-permute-done | bytes 524320 | tf_op jit(solution)/shard_map/ppermute | solution.py:267
  68.1 0.0 copy-start
  68.2 1.7 %collective-permute-start.6 = (bf16[16,128,128]{2,1,0:T(8,128)(2,1)S(1)}, bf16[16,128,128]{2,1,0:T(8,128)(2,1)S(1)}, u32[]{:S(2)}, u32[]{:S(2)}) collective-permute-start(bf16[16,128,128]{2,1,0:T(8,128)(2,1)S(1)} %collective-permute-done.4.refs_4_), channel_id=1, source_target_pairs={{0,12},{4,0},{8,4},{12,8},{1,13},{5,1},{9,5},{13,9},{2,14},{6,2},{... | collective-permute-start | bytes 1572872 | tf_op jit(solution)/shard_map/ppermute | solution.py:274
  69.9 0.0 collective-permute-start.5
  69.9 4.7 %collective-permute-start.1 = (bf16[16,128,128]{2,1,0:T(8,128)(2,1)S(1)}, bf16[16,128,128]{2,1,0:T(8,128)(2,1)S(1)}, u32[]{:S(2)}, u32[]{:S(2)}) collective-permute-start(bf16[16,128,128]{2,1,0:T(8,128)(2,1)S(1)} %all_to_all.5.refs_0_), channel_id=1, source_target_pairs={{0,1},{1,0},{2,3},{3,2},{4,5},{5,4},{6,7},{7,6},{8,9},{9,8},{10,11... | collective-permute-start | bytes 1572872 | tf_op jit(solution)/shard_map/ppermute | solution.py:271
  74.6 8.2 %collective-permute-done.2.refs_2_ = bf16[16,128,128]{2,1,0:T(8,128)(2,1)S(1)} collective-permute-done((bf16[16,128,128]{2,1,0:T(8,128)(2,1)S(1)}, bf16[16,128,128]{2,1,0:T(8,128)(2,1)S(1)}, u32[]{:S(2)}, u32[]{:S(2)}) %collective-permute-start.2) | collective-permute-done | bytes 524320 | tf_op jit(solution)/shard_map/ppermute | solution.py:270
  82.8 1.1 %collective-permute-start.3 = (bf16[16,128,128]{2,1,0:T(8,128)(2,1)S(1)}, bf16[16,128,128]{2,1,0:T(8,128)(2,1)S(1)}, u32[]{:S(2)}, u32[]{:S(2)}) collective-permute-start(bf16[16,128,128]{2,1,0:T(8,128)(2,1)S(1)} %collective-permute-done.2.refs_2_), channel_id=1, source_target_pairs={{0,1},{1,0},{2,3},{3,2},{4,5},{5,4},{6,7},{7,6},{8,9},{9,8},{10,11... | collective-permute-start | bytes 1572872 | tf_op jit(solution)/shard_map/ppermute | solution.py:272
  83.9 0.0 collective-permute-done.6.refs_6_.refs_5_
  83.9 0.7 slice.9
  84.6 0.0 collective-permute-start.8
  84.6 0.0 collective-permute-done.5.refs_5_.refs_4_
  84.6 0.0 copy-done
  84.6 0.7 slice.8
  85.3 1.5 %collective-permute-start.7 = (bf16[16,64,128]{2,1,0:T(8,128)(2,1)}, bf16[16,64,128]{2,1,0:T(8,128)(2,1)}, u32[]{:S(2)}, u32[]{:S(2)}) collective-permute-start(bf16[16,64,128]{2,1,0:T(8,128)(2,1)} %slice.8), channel_id=1, source_target_pairs={{0,4},{4,8},{8,12},{12,0},{1,5},{5,9},{9,13},{13,1},{2,6},{6,10},{... | collective-permute-start | bytes 786440 | tf_op jit(solution)/shard_map/ppermute | solution.py:275
  86.8 0.1 stack.27.place_ref
  86.9 0.0 collective-permute-done.1.refs_1_
  86.9 0.0 collective-permute-done.3.refs_3_
  86.9 0.0 copy-start.1
  86.9 1.0 %copy-done.1 = bf16[16,128,128]{2,1,0:T(8,128)(2,1)S(1)} copy-done((bf16[16,128,128]{2,1,0:T(8,128)(2,1)S(1)}, bf16[16,128,128]{2,1,0:T(8,128)(2,1)}, u32[]{:S(2)}) %copy-start.1) | copy-done | bytes 524312
  87.9 4.0 %shard_map.39.refs_8_ = f32[16,2,256,256]{3,2,1,0:T(8,128)} custom-call(s32[6]{0:T(128)S(1)} %stack.27.place_ref, bf16[16,128,128]{2,1,0:T(8,128)(2,1)S(1)} %all_to_all.5.refs_0_, bf16[16,128,128]{2,1,0:T(8,128)(2,1)S(1)} %collective-permute-done.1.refs_1_, bf16[16,128,128]{2,1,0:T(8,128)(2,1)S(1)} %collective-permute-done.2.refs_2_, ...), custom_call_target="tpu_custom_call" | custom-call | flops 536870912 | bytes 8388608 | tf_op jit(solution)/shard_map/pallas_call | solution.py:236
  92.0 0.9 collective-permute-done.8.refs_7_
  92.9 0.0 collective-permute-done.7.refs_6_
  92.9 4.4 %shard_map.40 = f32[16,2,256,256]{3,2,1,0:T(8,128)} custom-call(s32[6]{0:T(128)S(1)} %stack.27.place_ref, bf16[16,128,128]{2,1,0:T(8,128)(2,1)S(1)} %all_to_all.5.refs_0_, bf16[16,128,128]{2,1,0:T(8,128)(2,1)S(1)} %collective-permute-done.1.refs_1_, bf16[16,128,128]{2,1,0:T(8,128)(2,1)S(1)} %collective-permute-done.2.refs_2_, ...), custom_call_target="tpu_custom_call", output_to_operand_aliasing={{}: (9, {})} | custom-call | flops 536870912 | bytes 8388608 | tf_op jit(solution)/shard_map/pallas_call | solution.py:236
Async XLA Ops:
  7.0 13.4 %collective-permute-start = (bf16[16,128,128]{2,1,0:T(8,128)(2,1)}, bf16[16,128,128]{2,1,0:T(8,128)(2,1)S(1)}, u32[]{:S(2)}, u32[]{:S(2)}) collective-permute-start(bf16[16,128,128]{2,1,0:T(8,128)(2,1)} %bitcast.16), channel_id=1, source_target_pairs={{16,0},{32,16},{48,32},{64,48},{80,64},{96,80},{112,96},{128,112},... | collective-permute-start | bytes 1572872 | tf_op jit(solution)/shard_map/ppermute | solution.py:264
  49.0 19.2 %collective-permute-start.4 = (bf16[16,128,128]{2,1,0:T(8,128)(2,1)S(1)}, bf16[16,128,128]{2,1,0:T(8,128)(2,1)S(1)}, u32[]{:S(2)}, u32[]{:S(2)}) collective-permute-start(bf16[16,128,128]{2,1,0:T(8,128)(2,1)S(1)} %all_to_all.5.refs_0_), channel_id=1, source_target_pairs={{0,0},{1,4},{2,8},{3,12},{4,1},{5,5},{6,9},{7,13},{8,2},{9,6},{10,... | collective-permute-start | bytes 1572872 | tf_op jit(solution)/shard_map/ppermute | solution.py:267
  55.7 27.1 %collective-permute-start.2 = (bf16[16,128,128]{2,1,0:T(8,128)(2,1)S(1)}, bf16[16,128,128]{2,1,0:T(8,128)(2,1)S(1)}, u32[]{:S(2)}, u32[]{:S(2)}) collective-permute-start(bf16[16,128,128]{2,1,0:T(8,128)(2,1)S(1)} %all_to_all.5.refs_0_), channel_id=1, source_target_pairs={{0,2},{1,3},{2,0},{3,1},{4,6},{5,7},{6,4},{7,5},{8,10},{9,11},{10,... | collective-permute-start | bytes 1572872 | tf_op jit(solution)/shard_map/ppermute | solution.py:270
  68.1 16.5 %copy-start = (bf16[16,128,128]{2,1,0:T(8,128)(2,1)}, bf16[16,128,128]{2,1,0:T(8,128)(2,1)S(1)}, u32[]{:S(2)}) copy-start(bf16[16,128,128]{2,1,0:T(8,128)(2,1)S(1)} %collective-permute-done.4.refs_4_) | copy-start | bytes 1572868
  68.2 15.7 %collective-permute-start.6 = (bf16[16,128,128]{2,1,0:T(8,128)(2,1)S(1)}, bf16[16,128,128]{2,1,0:T(8,128)(2,1)S(1)}, u32[]{:S(2)}, u32[]{:S(2)}) collective-permute-start(bf16[16,128,128]{2,1,0:T(8,128)(2,1)S(1)} %collective-permute-done.4.refs_4_), channel_id=1, source_target_pairs={{0,12},{4,0},{8,4},{12,8},{1,13},{5,1},{9,5},{13,9},{2,14},{6,2},{... | collective-permute-start | bytes 1572872 | tf_op jit(solution)/shard_map/ppermute | solution.py:274
  69.9 14.7 %collective-permute-start.5 = (bf16[16,128,128]{2,1,0:T(8,128)(2,1)S(1)}, bf16[16,128,128]{2,1,0:T(8,128)(2,1)S(1)}, u32[]{:S(2)}, u32[]{:S(2)}) collective-permute-start(bf16[16,128,128]{2,1,0:T(8,128)(2,1)S(1)} %collective-permute-done.4.refs_4_), channel_id=1, source_target_pairs={{0,4},{4,8},{8,12},{12,0},{1,5},{5,9},{9,13},{13,1},{2,6},{6,10},{... | collective-permute-start | bytes 1572872 | tf_op jit(solution)/shard_map/ppermute | solution.py:273
  69.9 17.0 %collective-permute-start.1 = (bf16[16,128,128]{2,1,0:T(8,128)(2,1)S(1)}, bf16[16,128,128]{2,1,0:T(8,128)(2,1)S(1)}, u32[]{:S(2)}, u32[]{:S(2)}) collective-permute-start(bf16[16,128,128]{2,1,0:T(8,128)(2,1)S(1)} %all_to_all.5.refs_0_), channel_id=1, source_target_pairs={{0,1},{1,0},{2,3},{3,2},{4,5},{5,4},{6,7},{7,6},{8,9},{9,8},{10,11... | collective-permute-start | bytes 1572872 | tf_op jit(solution)/shard_map/ppermute | solution.py:271
  82.8 4.1 %collective-permute-start.3 = (bf16[16,128,128]{2,1,0:T(8,128)(2,1)S(1)}, bf16[16,128,128]{2,1,0:T(8,128)(2,1)S(1)}, u32[]{:S(2)}, u32[]{:S(2)}) collective-permute-start(bf16[16,128,128]{2,1,0:T(8,128)(2,1)S(1)} %collective-permute-done.2.refs_2_), channel_id=1, source_target_pairs={{0,1},{1,0},{2,3},{3,2},{4,5},{5,4},{6,7},{7,6},{8,9},{9,8},{10,11... | collective-permute-start | bytes 1572872 | tf_op jit(solution)/shard_map/ppermute | solution.py:272
  84.6 8.3 %collective-permute-start.8 = (bf16[16,64,128]{2,1,0:T(8,128)(2,1)}, bf16[16,64,128]{2,1,0:T(8,128)(2,1)S(1)}, u32[]{:S(2)}, u32[]{:S(2)}) collective-permute-start(bf16[16,64,128]{2,1,0:T(8,128)(2,1)} %slice.9), channel_id=1, source_target_pairs={{0,12},{4,0},{8,4},{12,8},{1,13},{5,1},{9,5},{13,9},{2,14},{6,2},{... | collective-permute-start | bytes 786440 | tf_op jit(solution)/shard_map/ppermute | solution.py:275
  85.3 7.5 %collective-permute-start.7 = (bf16[16,64,128]{2,1,0:T(8,128)(2,1)}, bf16[16,64,128]{2,1,0:T(8,128)(2,1)}, u32[]{:S(2)}, u32[]{:S(2)}) collective-permute-start(bf16[16,64,128]{2,1,0:T(8,128)(2,1)} %slice.8), channel_id=1, source_target_pairs={{0,4},{4,8},{8,12},{12,0},{1,5},{5,9},{9,13},{13,1},{2,6},{6,10},{... | collective-permute-start | bytes 786440 | tf_op jit(solution)/shard_map/ppermute | solution.py:275
  86.9 1.0 %copy-start.1 = (bf16[16,128,128]{2,1,0:T(8,128)(2,1)S(1)}, bf16[16,128,128]{2,1,0:T(8,128)(2,1)}, u32[]{:S(2)}) copy-start(bf16[16,128,128]{2,1,0:T(8,128)(2,1)} %copy-done) | copy-start | bytes 1572868

commit v5 on v4

--- a/solution.py
+++ b/solution.py
@@ -15,7 +15,6 @@
 KEEP = 256
 TAPS = 8
 PITCH = 521
-VLIM = 56
 INPUTS = 8
 UNROLL = 2
 GROUP = 16
@@ -152,7 +151,7 @@
             pltpu.SemaphoreType.DMA((64 // INPUTS,)),
             pltpu.SemaphoreType.DMA,
         ],
-        compiler_params=pltpu.CompilerParams(vmem_limit_bytes=VLIM * MIB),
+        compiler_params=pltpu.CompilerParams(vmem_limit_bytes=(56 if rim else 24) * MIB),
         cost_estimate=pl.CostEstimate(
             flops=2 * 512 * 2048 * 512, bytes_accessed=6 * MIB, transcendentals=0
         ),
@@ -165,7 +164,16 @@
 
 
 def correlate_kernel(late, place_ref, *refs):
-    rows, cols, out_ref, full_ref, sem = refs[:4], refs[4:8], refs[-3], refs[-2], refs[-1]
+    if late:
+        rows, cols = refs[:4], refs[4:8]
+        out_ref, full_ref, sem = refs[-3:]
+    else:
+        rows, cols = refs[:4], list(refs[4:7])
+        out_ref, full_ref, sem, mine_ref, mine_sem = refs[-5:]
+        load = pltpu.make_async_copy(cols[0], mine_ref, mine_sem)
+        load.start()
+        load.wait()
+        cols[0] = mine_ref
     odd = place_ref[5] == 1
     half = 1 - place_ref[4] if late else place_ref[4]
     lane = pl.multiple_of(half * LANES, LANES)
@@ -228,6 +236,13 @@
     operands = [*rows, *cols]
     in_specs = [pl.BlockSpec(memory_space=pltpu.SMEM)]
     in_specs += [pl.BlockSpec(memory_space=pltpu.VMEM) for _ in operands]
+    scratch = [
+        pltpu.VMEM((8, 2, 2, 256, LANES), jnp.float32),
+        pltpu.SemaphoreType.DMA((8,)),
+    ]
+    if not late:
+        in_specs[5] = pl.BlockSpec(memory_space=pl.ANY)
+        scratch += [pltpu.VMEM((16, 128, LANES), jnp.bfloat16), pltpu.SemaphoreType.DMA]
     aliases = {}
     if late:
         in_specs.append(pl.BlockSpec(memory_space=pl.ANY))
@@ -238,10 +253,7 @@
         in_specs=in_specs,
         out_specs=pl.BlockSpec(memory_space=pl.ANY),
         out_shape=jax.ShapeDtypeStruct((16, 2, 256, 256), jnp.float32),
-        scratch_shapes=[
-            pltpu.VMEM((8, 2, 2, 256, LANES), jnp.float32),
-            pltpu.SemaphoreType.DMA((8,)),
-        ],
+        scratch_shapes=scratch,
         input_output_aliases=aliases,
         compiler_params=pltpu.CompilerParams(vmem_limit_bytes=20 * MIB),
         cost_estimate=pl.CostEstimate(

time: 98.6 us -> 97.4 us (0.988)
  local copies, waits for them, and re-layouts: 2.57 us -> 6.81 us
  Pallas kernels: 23.2 us -> 20.7 us
  waiting for transfers between devices: 21.8 us -> 19.9 us
  other arithmetic: 1.35 us -> 0.13 us
    unnamed x4 -> x10, local copies, waits for them, and re-layouts: 1.04 us -> 5.29 us
    pallas_call x2, Pallas kernels: 14.7 us -> 12.2 us  [spectra(): pl.pallas_call(functools.partial(spectra_kernel, rim), in_specs=[pl.Block...]
    ppermute x1, waiting for transfers between devices: 4.42 us -> 2.65 us  [per_device(): rim = lax.ppermute(pre, 'chan', [(s, s - 1) for s in range(1, 16)])]
    convert_element_type x1, other arithmetic: 1.35 us -> 0.13 us  [per_device(): whole = (own + rim.astype(jnp.float32)).astype(jnp.bfloat16)]
  transfers between devices with their start and end apart: 9 -> 9, of which waited for: 4 -> 4; matrix products, arithmetic and copies ran while one was open for 2% -> 2% of each run, Pallas kernels for 12% -> 10%
where the time goes in v5:
time: 97.4 us; the launch traced here: 96.1 us
  blocking collectives  27.1 us (28%)
  starting transfers between devices  21.2 us (22%)
  Pallas kernels  20.7 us (21%)
  waiting for transfers between devices  19.9 us (20%)
  local copies, waits for them, and re-layouts  6.81 us (7%)
    all_to_all x1, blocking collectives, per_device(): lax.all_to_all(whole, 'chan', split_axis=0, concat_axis=0, tiled=True)  27.1 us
    pallas_call x2, Pallas kernels, spectra(): pl.pallas_call(functools.partial(spectra_kernel, rim), in_specs=[pl.Block...  12.2 us
    pallas_call x2, Pallas kernels, correlate(): pl.pallas_call(functools.partial(correlate_kernel, late), in_specs=in_spe...  8.5 us
    ppermute x1, waiting for transfers between devices, per_device(): lax.ppermute(turned, ('row', 'col'), [(4 * r + c, 4 * c + r) for r in rin...  8.27 us
    ppermute x1, waiting for transfers between devices, per_device(): far = lax.ppermute(turned, 'col', [(c, c ^ 2) for c in ring])  8.16 us
    ppermute x1, starting transfers between devices, per_device(): lax.ppermute(turned, ('row', 'col'), [(4 * r + c, 4 * c + r) for r in rin...  6.7 us
    unnamed x10, local copies, waits for them, and re-layouts  5.29 us
    ppermute x1, starting transfers between devices, per_device(): near = lax.ppermute(turned, 'col', [(c, c ^ 1) for c in ring])  4.74 us
  transfers between devices with their start and end apart: 9, of which 4 were waited for; matrix products, arithmetic and copies ran while one was open for 2% of the time, Pallas kernels for 10%

profile of v5, /device:TPU:1, one launch (start us, length us, event | category | flops | bytes accessed | tf_op | source)
XLA Modules:
  0.0 96.1 jit_solution(11006105292855875115)
XLA Ops:
  0.0 7.0 %shard_map.38 = bf16[2048,128]{1,0:T(8,128)(2,1)} custom-call(bf16[64,8,32,128]{3,2,1,0:T(8,128)(2,1)} %bitcast.13, f32[8,2048]{1,0:T(8,128)} %raw_ref.3, bf16[2,256,1024]{2,1,0:T(8,128)(2,1)} %constant.36.clone.table_any), custom_call_target="tpu_custom_call" | custom-call | flops 1073741824 | bytes 6291456 | tf_op jit(solution)/shard_map/pallas_call | solution.py:134
  7.0 1.3 %collective-permute-start = (bf16[16,128,128]{2,1,0:T(8,128)(2,1)}, bf16[16,128,128]{2,1,0:T(8,128)(2,1)S(1)}, u32[]{:S(2)}, u32[]{:S(2)}) collective-permute-start(bf16[16,128,128]{2,1,0:T(8,128)(2,1)} %bitcast.16), channel_id=1, source_target_pairs={{16,0},{32,16},{48,32},{64,48},{80,64},{96,80},{112,96},{128,112},... | collective-permute-start | bytes 1572872 | tf_op jit(solution)/shard_map/ppermute | solution.py:276
  8.3 0.0 copy-start
  8.3 2.2 %copy-done = bf16[64,8,2,2048]{3,2,1,0:T(2,128)(2,1)S(1)} copy-done((bf16[64,8,2,2048]{3,2,1,0:T(2,128)(2,1)S(1)}, bf16[64,8,2,2048]{3,2,1,0:T(2,128)(2,1)}, u32[]{:S(2)}) %copy-start) | copy-done | bytes 4194328
  10.5 0.0 copy-start.1
  10.5 1.2 %copy-done.1 = bf16[2,256,1024]{2,1,0:T(8,128)(2,1)S(1)} copy-done((bf16[2,256,1024]{2,1,0:T(8,128)(2,1)S(1)}, bf16[2,256,1024]{2,1,0:T(8,128)(2,1)}, u32[]{:S(2)}) %copy-start.1) | copy-done | bytes 1048600
  11.7 0.0 copy-start.4
  11.7 0.8 copy-done.4
  12.6 5.2 %shard_map.37 = f32[2048,128]{1,0:T(8,128)S(1)} custom-call(bf16[64,8,32,128]{3,2,1,0:T(8,128)(2,1)S(1)} %bitcast.14, f32[8,2048]{1,0:T(8,128)S(1)} %copy-done.4, bf16[2,256,1024]{2,1,0:T(8,128)(2,1)S(1)} %copy-done.1), custom_call_target="tpu_custom_call" | custom-call | flops 1073741824 | bytes 6291456 | tf_op jit(solution)/shard_map/pallas_call | solution.py:134
  17.8 2.6 %collective-permute-done = bf16[16,128,128]{2,1,0:T(8,128)(2,1)S(1)} collective-permute-done((bf16[16,128,128]{2,1,0:T(8,128)(2,1)}, bf16[16,128,128]{2,1,0:T(8,128)(2,1)S(1)}, u32[]{:S(2)}, u32[]{:S(2)}) %collective-permute-start) | collective-permute-done | bytes 524320 | tf_op jit(solution)/shard_map/ppermute | solution.py:276
  20.5 0.1 add_convert_fusion
  20.6 27.1 %all_to_all.5.refs_0_ = bf16[16,128,128]{2,1,0:T(8,128)(2,1)S(1)} all-to-all(bf16[16,128,128]{2,1,0:T(8,128)(2,1)S(1)} %add_convert_fusion), channel_id=1, replica_groups=mesh['chan'=16,'row'=4,'col'=4] {'chan'}, dimensions={0} | all-to-all | bytes 1048576 | tf_op jit(solution)/shard_map/all_to_all | solution.py:278
  47.7 6.7 %collective-permute-start.4 = (bf16[16,128,128]{2,1,0:T(8,128)(2,1)S(1)}, bf16[16,128,128]{2,1,0:T(8,128)(2,1)S(1)}, u32[]{:S(2)}, u32[]{:S(2)}) collective-permute-start(bf16[16,128,128]{2,1,0:T(8,128)(2,1)S(1)} %all_to_all.5.refs_0_), channel_id=1, source_target_pairs={{0,0},{1,4},{2,8},{3,12},{4,1},{5,5},{6,9},{7,13},{8,2},{9,6},{10,... | collective-permute-start | bytes 1572872 | tf_op jit(solution)/shard_map/ppermute | solution.py:279
  54.5 4.2 %collective-permute-start.2 = (bf16[16,128,128]{2,1,0:T(8,128)(2,1)S(1)}, bf16[16,128,128]{2,1,0:T(8,128)(2,1)S(1)}, u32[]{:S(2)}, u32[]{:S(2)}) collective-permute-start(bf16[16,128,128]{2,1,0:T(8,128)(2,1)S(1)} %all_to_all.5.refs_0_), channel_id=1, source_target_pairs={{0,2},{1,3},{2,0},{3,1},{4,6},{5,7},{6,4},{7,5},{8,10},{9,11},{10,... | collective-permute-start | bytes 1572872 | tf_op jit(solution)/shard_map/ppermute | solution.py:282
  58.7 8.3 %collective-permute-done.4.refs_4_ = bf16[16,128,128]{2,1,0:T(8,128)(2,1)S(1)} collective-permute-done((bf16[16,128,128]{2,1,0:T(8,128)(2,1)S(1)}, bf16[16,128,128]{2,1,0:T(8,128)(2,1)S(1)}, u32[]{:S(2)}, u32[]{:S(2)}) %collective-permute-start.4) | collective-permute-done | bytes 524320 | tf_op jit(solution)/shard_map/ppermute | solution.py:279
  66.9 0.0 copy-start.2
  66.9 1.7 %collective-permute-start.6 = (bf16[16,128,128]{2,1,0:T(8,128)(2,1)S(1)}, bf16[16,128,128]{2,1,0:T(8,128)(2,1)S(1)}, u32[]{:S(2)}, u32[]{:S(2)}) collective-permute-start(bf16[16,128,128]{2,1,0:T(8,128)(2,1)S(1)} %collective-permute-done.4.refs_4_), channel_id=1, source_target_pairs={{0,12},{4,0},{8,4},{12,8},{1,13},{5,1},{9,5},{13,9},{2,14},{6,2},{... | collective-permute-start | bytes 1572872 | tf_op jit(solution)/shard_map/ppermute | solution.py:286
  68.6 0.0 collective-permute-start.5
  68.6 4.7 %collective-permute-start.1 = (bf16[16,128,128]{2,1,0:T(8,128)(2,1)S(1)}, bf16[16,128,128]{2,1,0:T(8,128)(2,1)S(1)}, u32[]{:S(2)}, u32[]{:S(2)}) collective-permute-start(bf16[16,128,128]{2,1,0:T(8,128)(2,1)S(1)} %all_to_all.5.refs_0_), channel_id=1, source_target_pairs={{0,1},{1,0},{2,3},{3,2},{4,5},{5,4},{6,7},{7,6},{8,9},{9,8},{10,11... | collective-permute-start | bytes 1572872 | tf_op jit(solution)/shard_map/ppermute | solution.py:283
  73.4 8.2 %collective-permute-done.2.refs_2_ = bf16[16,128,128]{2,1,0:T(8,128)(2,1)S(1)} collective-permute-done((bf16[16,128,128]{2,1,0:T(8,128)(2,1)S(1)}, bf16[16,128,128]{2,1,0:T(8,128)(2,1)S(1)}, u32[]{:S(2)}, u32[]{:S(2)}) %collective-permute-start.2) | collective-permute-done | bytes 524320 | tf_op jit(solution)/shard_map/ppermute | solution.py:282
  81.5 1.1 %collective-permute-start.3 = (bf16[16,128,128]{2,1,0:T(8,128)(2,1)S(1)}, bf16[16,128,128]{2,1,0:T(8,128)(2,1)S(1)}, u32[]{:S(2)}, u32[]{:S(2)}) collective-permute-start(bf16[16,128,128]{2,1,0:T(8,128)(2,1)S(1)} %collective-permute-done.2.refs_2_), channel_id=1, source_target_pairs={{0,1},{1,0},{2,3},{3,2},{4,5},{5,4},{6,7},{7,6},{8,9},{9,8},{10,11... | collective-permute-start | bytes 1572872 | tf_op jit(solution)/shard_map/ppermute | solution.py:284
  82.7 0.0 collective-permute-done.6.refs_6_.refs_5_
  82.7 0.7 slice.9
  83.4 0.0 collective-permute-start.8
  83.4 0.0 collective-permute-done.5.refs_5_.refs_4_
  83.4 0.0 copy-done.2
  83.4 0.7 slice.8
  84.1 1.5 %collective-permute-start.7 = (bf16[16,64,128]{2,1,0:T(8,128)(2,1)}, bf16[16,64,128]{2,1,0:T(8,128)(2,1)}, u32[]{:S(2)}, u32[]{:S(2)}) collective-permute-start(bf16[16,64,128]{2,1,0:T(8,128)(2,1)} %slice.8), channel_id=1, source_target_pairs={{0,4},{4,8},{8,12},{12,0},{1,5},{5,9},{9,13},{13,1},{2,6},{6,10},{... | collective-permute-start | bytes 786440 | tf_op jit(solution)/shard_map/ppermute | solution.py:287
  85.6 0.1 stack.27.place_ref
  85.7 0.0 collective-permute-done.1.refs_1_
  85.7 0.0 collective-permute-done.3.refs_3_
  85.7 0.0 copy-start.3
  85.7 1.0 %copy-done.3 = bf16[16,128,128]{2,1,0:T(8,128)(2,1)S(1)} copy-done((bf16[16,128,128]{2,1,0:T(8,128)(2,1)S(1)}, bf16[16,128,128]{2,1,0:T(8,128)(2,1)}, u32[]{:S(2)}) %copy-start.3) | copy-done | bytes 524312
  86.7 4.1 %shard_map.39.refs_8_ = f32[16,2,256,256]{3,2,1,0:T(8,128)} custom-call(s32[6]{0:T(128)S(1)} %stack.27.place_ref, bf16[16,128,128]{2,1,0:T(8,128)(2,1)S(1)} %all_to_all.5.refs_0_, bf16[16,128,128]{2,1,0:T(8,128)(2,1)S(1)} %collective-permute-done.1.refs_1_, bf16[16,128,128]{2,1,0:T(8,128)(2,1)S(1)} %collective-permute-done.2.refs_2_, ...), custom_call_target="tpu_custom_call" | custom-call | flops 536870912 | bytes 8388608 | tf_op jit(solution)/shard_map/pallas_call | solution.py:251
  90.8 0.9 collective-permute-done.8.refs_7_
  91.6 0.0 collective-permute-done.7.refs_6_
  91.6 4.4 %shard_map.40 = f32[16,2,256,256]{3,2,1,0:T(8,128)} custom-call(s32[6]{0:T(128)S(1)} %stack.27.place_ref, bf16[16,128,128]{2,1,0:T(8,128)(2,1)S(1)} %all_to_all.5.refs_0_, bf16[16,128,128]{2,1,0:T(8,128)(2,1)S(1)} %collective-permute-done.1.refs_1_, bf16[16,128,128]{2,1,0:T(8,128)(2,1)S(1)} %collective-permute-done.2.refs_2_, ...), custom_call_target="tpu_custom_call", output_to_operand_aliasing={{}: (9, {})} | custom-call | flops 536870912 | bytes 8388608 | tf_op jit(solution)/shard_map/pallas_call | solution.py:251
Async XLA Ops:
  7.0 13.4 %collective-permute-start = (bf16[16,128,128]{2,1,0:T(8,128)(2,1)}, bf16[16,128,128]{2,1,0:T(8,128)(2,1)S(1)}, u32[]{:S(2)}, u32[]{:S(2)}) collective-permute-start(bf16[16,128,128]{2,1,0:T(8,128)(2,1)} %bitcast.16), channel_id=1, source_target_pairs={{16,0},{32,16},{48,32},{64,48},{80,64},{96,80},{112,96},{128,112},... | collective-permute-start | bytes 1572872 | tf_op jit(solution)/shard_map/ppermute | solution.py:276
  8.3 2.2 %copy-start = (bf16[64,8,2,2048]{3,2,1,0:T(2,128)(2,1)S(1)}, bf16[64,8,2,2048]{3,2,1,0:T(2,128)(2,1)}, u32[]{:S(2)}) copy-start(bf16[64,8,2,2048]{3,2,1,0:T(2,128)(2,1)} %param.3) | copy-start | bytes 12582916
  10.5 1.2 %copy-start.1 = (bf16[2,256,1024]{2,1,0:T(8,128)(2,1)S(1)}, bf16[2,256,1024]{2,1,0:T(8,128)(2,1)}, u32[]{:S(2)}) copy-start(bf16[2,256,1024]{2,1,0:T(8,128)(2,1)} %constant.36.clone.table_any) | copy-start | bytes 3145732
  11.7 0.8 copy-start.4
  47.7 19.2 %collective-permute-start.4 = (bf16[16,128,128]{2,1,0:T(8,128)(2,1)S(1)}, bf16[16,128,128]{2,1,0:T(8,128)(2,1)S(1)}, u32[]{:S(2)}, u32[]{:S(2)}) collective-permute-start(bf16[16,128,128]{2,1,0:T(8,128)(2,1)S(1)} %all_to_all.5.refs_0_), channel_id=1, source_target_pairs={{0,0},{1,4},{2,8},{3,12},{4,1},{5,5},{6,9},{7,13},{8,2},{9,6},{10,... | collective-permute-start | bytes 1572872 | tf_op jit(solution)/shard_map/ppermute | solution.py:279
  54.5 27.1 %collective-permute-start.2 = (bf16[16,128,128]{2,1,0:T(8,128)(2,1)S(1)}, bf16[16,128,128]{2,1,0:T(8,128)(2,1)S(1)}, u32[]{:S(2)}, u32[]{:S(2)}) collective-permute-start(bf16[16,128,128]{2,1,0:T(8,128)(2,1)S(1)} %all_to_all.5.refs_0_), channel_id=1, source_target_pairs={{0,2},{1,3},{2,0},{3,1},{4,6},{5,7},{6,4},{7,5},{8,10},{9,11},{10,... | collective-permute-start | bytes 1572872 | tf_op jit(solution)/shard_map/ppermute | solution.py:282
  66.9 16.5 %copy-start.2 = (bf16[16,128,128]{2,1,0:T(8,128)(2,1)}, bf16[16,128,128]{2,1,0:T(8,128)(2,1)S(1)}, u32[]{:S(2)}) copy-start(bf16[16,128,128]{2,1,0:T(8,128)(2,1)S(1)} %collective-permute-done.4.refs_4_) | copy-start | bytes 1572868
  66.9 15.7 %collective-permute-start.6 = (bf16[16,128,128]{2,1,0:T(8,128)(2,1)S(1)}, bf16[16,128,128]{2,1,0:T(8,128)(2,1)S(1)}, u32[]{:S(2)}, u32[]{:S(2)}) collective-permute-start(bf16[16,128,128]{2,1,0:T(8,128)(2,1)S(1)} %collective-permute-done.4.refs_4_), channel_id=1, source_target_pairs={{0,12},{4,0},{8,4},{12,8},{1,13},{5,1},{9,5},{13,9},{2,14},{6,2},{... | collective-permute-start | bytes 1572872 | tf_op jit(solution)/shard_map/ppermute | solution.py:286
  68.6 14.8 %collective-permute-start.5 = (bf16[16,128,128]{2,1,0:T(8,128)(2,1)S(1)}, bf16[16,128,128]{2,1,0:T(8,128)(2,1)S(1)}, u32[]{:S(2)}, u32[]{:S(2)}) collective-permute-start(bf16[16,128,128]{2,1,0:T(8,128)(2,1)S(1)} %collective-permute-done.4.refs_4_), channel_id=1, source_target_pairs={{0,4},{4,8},{8,12},{12,0},{1,5},{5,9},{9,13},{13,1},{2,6},{6,10},{... | collective-permute-start | bytes 1572872 | tf_op jit(solution)/shard_map/ppermute | solution.py:285
  68.6 17.0 %collective-permute-start.1 = (bf16[16,128,128]{2,1,0:T(8,128)(2,1)S(1)}, bf16[16,128,128]{2,1,0:T(8,128)(2,1)S(1)}, u32[]{:S(2)}, u32[]{:S(2)}) collective-permute-start(bf16[16,128,128]{2,1,0:T(8,128)(2,1)S(1)} %all_to_all.5.refs_0_), channel_id=1, source_target_pairs={{0,1},{1,0},{2,3},{3,2},{4,5},{5,4},{6,7},{7,6},{8,9},{9,8},{10,11... | collective-permute-start | bytes 1572872 | tf_op jit(solution)/shard_map/ppermute | solution.py:283
  81.5 4.1 %collective-permute-start.3 = (bf16[16,128,128]{2,1,0:T(8,128)(2,1)S(1)}, bf16[16,128,128]{2,1,0:T(8,128)(2,1)S(1)}, u32[]{:S(2)}, u32[]{:S(2)}) collective-permute-start(bf16[16,128,128]{2,1,0:T(8,128)(2,1)S(1)} %collective-permute-done.2.refs_2_), channel_id=1, source_target_pairs={{0,1},{1,0},{2,3},{3,2},{4,5},{5,4},{6,7},{7,6},{8,9},{9,8},{10,11... | collective-permute-start | bytes 1572872 | tf_op jit(solution)/shard_map/ppermute | solution.py:284
  83.4 8.3 %collective-permute-start.8 = (bf16[16,64,128]{2,1,0:T(8,128)(2,1)}, bf16[16,64,128]{2,1,0:T(8,128)(2,1)S(1)}, u32[]{:S(2)}, u32[]{:S(2)}) collective-permute-start(bf16[16,64,128]{2,1,0:T(8,128)(2,1)} %slice.9), channel_id=1, source_target_pairs={{0,12},{4,0},{8,4},{12,8},{1,13},{5,1},{9,5},{13,9},{2,14},{6,2},{... | collective-permute-start | bytes 786440 | tf_op jit(solution)/shard_map/ppermute | solution.py:287
  84.1 7.5 %collective-permute-start.7 = (bf16[16,64,128]{2,1,0:T(8,128)(2,1)}, bf16[16,64,128]{2,1,0:T(8,128)(2,1)}, u32[]{:S(2)}, u32[]{:S(2)}) collective-permute-start(bf16[16,64,128]{2,1,0:T(8,128)(2,1)} %slice.8), channel_id=1, source_target_pairs={{0,4},{4,8},{8,12},{12,0},{1,5},{5,9},{9,13},{13,1},{2,6},{6,10},{... | collective-permute-start | bytes 786440 | tf_op jit(solution)/shard_map/ppermute | solution.py:287
  85.7 1.0 %copy-start.3 = (bf16[16,128,128]{2,1,0:T(8,128)(2,1)S(1)}, bf16[16,128,128]{2,1,0:T(8,128)(2,1)}, u32[]{:S(2)}) copy-start(bf16[16,128,128]{2,1,0:T(8,128)(2,1)} %copy-done.2) | copy-start | bytes 1572868

commit v6 on v5

--- a/solution.py
+++ b/solution.py
@@ -90,7 +90,7 @@
 
     for b, load in enumerate(loads):
         load.wait()
-        lax.fori_loop(b * INPUTS, (b + 1) * INPUTS, filter_input, 0)
+        lax.fori_loop(b * INPUTS, (b + 1) * INPUTS, filter_input, 0, unroll=4)
 
     table_load.wait()
     def transform(low_bit, carry):
@@ -165,11 +165,11 @@
 
 def correlate_kernel(late, place_ref, *refs):
     if late:
-        rows, cols = refs[:4], refs[4:8]
+        left_ref, cols = refs[0], refs[1:5]
         out_ref, full_ref, sem = refs[-3:]
     else:
         rows, cols = refs[:4], list(refs[4:7])
-        out_ref, full_ref, sem, mine_ref, mine_sem = refs[-5:]
+        out_ref, left_ref, full_ref, sem, mine_ref, mine_sem = refs[-6:]
         load = pltpu.make_async_copy(cols[0], mine_ref, mine_sem)
         load.start()
         load.wait()
@@ -191,7 +191,6 @@
         def block(ref):
             return ref[:, at, :].reshape(256, LANES)
 
-        left_blocks = [block(ref) for ref in rows]
         if late:
             tail = pl.ds(pl.multiple_of(step % 4 * 16, 16), 16)
             far = jnp.where(step < 4, cols[2][:, tail, :], cols[3][:, tail, :])
@@ -200,13 +199,18 @@
                 jnp.where(odd, block(cols[1]), far), jnp.where(odd, far, block(cols[0]))
             ]
         else:
+            left_blocks = [block(ref) for ref in rows]
             mine = block(cols[0])
             right_blocks = [
                 jnp.where(odd, block(cols[1]), mine), jnp.where(odd, mine, block(cols[2]))
             ]
         for channel in range(2):
             lanes = slice(64 * channel, 64 * channel + 64)
-            left = jnp.concatenate([b[:, lanes] for b in left_blocks], axis=1)
+            if late:
+                left = left_ref[2 * step + channel]
+            else:
+                left = jnp.concatenate([b[:, lanes] for b in left_blocks], axis=1).T
+                left_ref[2 * step + channel] = left
             right = jnp.concatenate([b[:, lanes] for b in right_blocks], axis=1)
             pairs = right.astype(jnp.float32).reshape(16, 2, 8, LANES)
             flipped = jnp.concatenate([-pairs[:, 1:], pairs[:, :1]], axis=1)
@@ -214,7 +218,7 @@
             product = lax.dot_general(
                 left,
                 jnp.concatenate([right, flipped], axis=1),
-                (((0,), (0,)), ((), ())),
+                (((1,), (0,)), ((), ())),
                 preferred_element_type=jnp.float32,
             ) * (1.0 / 128.0)
             for k in range(4):
@@ -244,6 +248,11 @@
         in_specs[5] = pl.BlockSpec(memory_space=pl.ANY)
         scratch += [pltpu.VMEM((16, 128, LANES), jnp.bfloat16), pltpu.SemaphoreType.DMA]
     aliases = {}
+    out_specs = [pl.BlockSpec(memory_space=pl.ANY)]
+    out_shape = [jax.ShapeDtypeStruct((16, 2, 256, 256), jnp.float32)]
+    if not late:
+        out_specs.append(pl.BlockSpec(memory_space=pltpu.VMEM))
+        out_shape.append(jax.ShapeDtypeStruct((16, 256, 256), jnp.bfloat16))
     if late:
         in_specs.append(pl.BlockSpec(memory_space=pl.ANY))
         aliases = {1 + len(operands): 0}
@@ -251,8 +260,8 @@
     return pl.pallas_call(
         functools.partial(correlate_kernel, late),
         in_specs=in_specs,
-        out_specs=pl.BlockSpec(memory_space=pl.ANY),
-        out_shape=jax.ShapeDtypeStruct((16, 2, 256, 256), jnp.float32),
+        out_specs=out_specs,
+        out_shape=out_shape,
         scratch_shapes=scratch,
         input_output_aliases=aliases,
         compiler_params=pltpu.CompilerParams(vmem_limit_bytes=20 * MIB),
@@ -286,8 +295,8 @@
     upper = lax.ppermute(crossed, "row", down)
     tails = [lax.ppermute(lower[:, :64], "row", up), lax.ppermute(upper[:, 64:], "row", down)]
     rows = [turned, near, far, both]
-    result = correlate(place, rows, [crossed, lower, upper], None)
-    return correlate(place, rows, [lower, upper, *tails], result)
+    result, left = correlate(place, rows, [crossed, lower, upper], None)
+    return correlate(place, [left], [lower, upper, *tails], result)[0]
 
 
 def solution(mesh):

time: 97.4 us -> 96.3 us (0.989)
  local copies, waits for them, and re-layouts: 6.81 us -> 5.78 us
    unnamed x10 -> x6, local copies, waits for them, and re-layouts: 5.29 us -> 4.25 us
  transfers between devices with their start and end apart: 9 -> 9, of which waited for: 4 -> 4; matrix products, arithmetic and copies ran while one was open for 2% -> 2% of each run, Pallas kernels for 10% -> 11%
where the time goes in v6:
time: 96.3 us; the launch traced here: 95 us
  blocking collectives  27.1 us (28%)
  starting transfers between devices  21.2 us (22%)
  Pallas kernels  20.4 us (21%)
  waiting for transfers between devices  20.3 us (21%)
  local copies, waits for them, and re-layouts  5.78 us (6%)
    all_to_all x1, blocking collectives, per_device(): lax.all_to_all(whole, 'chan', split_axis=0, concat_axis=0, tiled=True)  27.1 us
    pallas_call x2, Pallas kernels, spectra(): pl.pallas_call(functools.partial(spectra_kernel, rim), in_specs=[pl.Block...  11.8 us
    pallas_call x2, Pallas kernels, correlate(): pl.pallas_call(functools.partial(correlate_kernel, late), in_specs=in_spe...  8.5 us
    ppermute x1, waiting for transfers between devices, per_device(): lax.ppermute(turned, ('row', 'col'), [(4 * r + c, 4 * c + r) for r in rin...  8.27 us
    ppermute x1, waiting for transfers between devices, per_device(): far = lax.ppermute(turned, 'col', [(c, c ^ 2) for c in ring])  8.16 us
    ppermute x1, starting transfers between devices, per_device(): lax.ppermute(turned, ('row', 'col'), [(4 * r + c, 4 * c + r) for r in rin...  6.7 us
    ppermute x1, starting transfers between devices, per_device(): near = lax.ppermute(turned, 'col', [(c, c ^ 1) for c in ring])  4.75 us
    unnamed x6, local copies, waits for them, and re-layouts  4.25 us
  transfers between devices with their start and end apart: 9, of which 4 were waited for; matrix products, arithmetic and copies ran while one was open for 2% of the time, Pallas kernels for 11%

profile of v6, /device:TPU:1, one launch (start us, length us, event | category | flops | bytes accessed | tf_op | source)
XLA Modules:
  0.0 95.0 jit_solution(3251341262270232676)
XLA Ops:
  0.0 6.7 %shard_map.38 = bf16[2048,128]{1,0:T(8,128)(2,1)} custom-call(bf16[64,8,32,128]{3,2,1,0:T(8,128)(2,1)} %bitcast.13, f32[8,2048]{1,0:T(8,128)} %raw_ref.3, bf16[2,256,1024]{2,1,0:T(8,128)(2,1)} %constant.36.clone.table_any), custom_call_target="tpu_custom_call" | custom-call | flops 1073741824 | bytes 6291456 | tf_op jit(solution)/shard_map/pallas_call | solution.py:134
  6.7 1.3 %collective-permute-start = (bf16[16,128,128]{2,1,0:T(8,128)(2,1)}, bf16[16,128,128]{2,1,0:T(8,128)(2,1)S(1)}, u32[]{:S(2)}, u32[]{:S(2)}) collective-permute-start(bf16[16,128,128]{2,1,0:T(8,128)(2,1)} %bitcast.16), channel_id=1, source_target_pairs={{16,0},{32,16},{48,32},{64,48},{80,64},{96,80},{112,96},{128,112},... | collective-permute-start | bytes 1572872 | tf_op jit(solution)/shard_map/ppermute | solution.py:285
  8.0 0.0 copy-start
  8.1 2.2 %copy-done = bf16[64,8,2,2048]{3,2,1,0:T(2,128)(2,1)S(1)} copy-done((bf16[64,8,2,2048]{3,2,1,0:T(2,128)(2,1)S(1)}, bf16[64,8,2,2048]{3,2,1,0:T(2,128)(2,1)}, u32[]{:S(2)}) %copy-start) | copy-done | bytes 4194328
  10.2 0.0 copy-start.1
  10.2 1.2 %copy-done.1 = bf16[2,256,1024]{2,1,0:T(8,128)(2,1)S(1)} copy-done((bf16[2,256,1024]{2,1,0:T(8,128)(2,1)S(1)}, bf16[2,256,1024]{2,1,0:T(8,128)(2,1)}, u32[]{:S(2)}) %copy-start.1) | copy-done | bytes 1048600
  11.5 0.0 copy-start.2
  11.5 0.8 copy-done.2
  12.3 5.1 %shard_map.37 = f32[2048,128]{1,0:T(8,128)S(1)} custom-call(bf16[64,8,32,128]{3,2,1,0:T(8,128)(2,1)S(1)} %bitcast.14, f32[8,2048]{1,0:T(8,128)S(1)} %copy-done.2, bf16[2,256,1024]{2,1,0:T(8,128)(2,1)S(1)} %copy-done.1), custom_call_target="tpu_custom_call" | custom-call | flops 1073741824 | bytes 6291456 | tf_op jit(solution)/shard_map/pallas_call | solution.py:134
  17.4 2.8 %collective-permute-done = bf16[16,128,128]{2,1,0:T(8,128)(2,1)S(1)} collective-permute-done((bf16[16,128,128]{2,1,0:T(8,128)(2,1)}, bf16[16,128,128]{2,1,0:T(8,128)(2,1)S(1)}, u32[]{:S(2)}, u32[]{:S(2)}) %collective-permute-start) | collective-permute-done | bytes 524320 | tf_op jit(solution)/shard_map/ppermute | solution.py:285
  20.2 0.1 add_convert_fusion
  20.3 27.1 %all_to_all.5.refs_0_ = bf16[16,128,128]{2,1,0:T(8,128)(2,1)S(1)} all-to-all(bf16[16,128,128]{2,1,0:T(8,128)(2,1)S(1)} %add_convert_fusion), channel_id=1, replica_groups=mesh['chan'=16,'row'=4,'col'=4] {'chan'}, dimensions={0} | all-to-all | bytes 1048576 | tf_op jit(solution)/shard_map/all_to_all | solution.py:287
  47.5 6.7 %collective-permute-start.4 = (bf16[16,128,128]{2,1,0:T(8,128)(2,1)S(1)}, bf16[16,128,128]{2,1,0:T(8,128)(2,1)S(1)}, u32[]{:S(2)}, u32[]{:S(2)}) collective-permute-start(bf16[16,128,128]{2,1,0:T(8,128)(2,1)S(1)} %all_to_all.5.refs_0_), channel_id=1, source_target_pairs={{0,0},{1,4},{2,8},{3,12},{4,1},{5,5},{6,9},{7,13},{8,2},{9,6},{10,... | collective-permute-start | bytes 1572872 | tf_op jit(solution)/shard_map/ppermute | solution.py:288
  54.2 4.2 %collective-permute-start.2 = (bf16[16,128,128]{2,1,0:T(8,128)(2,1)S(1)}, bf16[16,128,128]{2,1,0:T(8,128)(2,1)S(1)}, u32[]{:S(2)}, u32[]{:S(2)}) collective-permute-start(bf16[16,128,128]{2,1,0:T(8,128)(2,1)S(1)} %all_to_all.5.refs_0_), channel_id=1, source_target_pairs={{0,2},{1,3},{2,0},{3,1},{4,6},{5,7},{6,4},{7,5},{8,10},{9,11},{10,... | collective-permute-start | bytes 1572872 | tf_op jit(solution)/shard_map/ppermute | solution.py:291
  58.4 8.3 %collective-permute-done.4.refs_4_ = bf16[16,128,128]{2,1,0:T(8,128)(2,1)S(1)} collective-permute-done((bf16[16,128,128]{2,1,0:T(8,128)(2,1)S(1)}, bf16[16,128,128]{2,1,0:T(8,128)(2,1)S(1)}, u32[]{:S(2)}, u32[]{:S(2)}) %collective-permute-start.4) | collective-permute-done | bytes 524320 | tf_op jit(solution)/shard_map/ppermute | solution.py:288
  66.6 1.7 %collective-permute-start.6 = (bf16[16,128,128]{2,1,0:T(8,128)(2,1)S(1)}, bf16[16,128,128]{2,1,0:T(8,128)(2,1)S(1)}, u32[]{:S(2)}, u32[]{:S(2)}) collective-permute-start(bf16[16,128,128]{2,1,0:T(8,128)(2,1)S(1)} %collective-permute-done.4.refs_4_), channel_id=1, source_target_pairs={{0,12},{4,0},{8,4},{12,8},{1,13},{5,1},{9,5},{13,9},{2,14},{6,2},{... | collective-permute-start | bytes 1572872 | tf_op jit(solution)/shard_map/ppermute | solution.py:295
  68.4 0.0 collective-permute-start.5
  68.4 4.7 %collective-permute-start.1 = (bf16[16,128,128]{2,1,0:T(8,128)(2,1)S(1)}, bf16[16,128,128]{2,1,0:T(8,128)(2,1)S(1)}, u32[]{:S(2)}, u32[]{:S(2)}) collective-permute-start(bf16[16,128,128]{2,1,0:T(8,128)(2,1)S(1)} %all_to_all.5.refs_0_), channel_id=1, source_target_pairs={{0,1},{1,0},{2,3},{3,2},{4,5},{5,4},{6,7},{7,6},{8,9},{9,8},{10,11... | collective-permute-start | bytes 1572872 | tf_op jit(solution)/shard_map/ppermute | solution.py:292
  73.1 8.2 %collective-permute-done.2.refs_2_ = bf16[16,128,128]{2,1,0:T(8,128)(2,1)S(1)} collective-permute-done((bf16[16,128,128]{2,1,0:T(8,128)(2,1)S(1)}, bf16[16,128,128]{2,1,0:T(8,128)(2,1)S(1)}, u32[]{:S(2)}, u32[]{:S(2)}) %collective-permute-start.2) | collective-permute-done | bytes 524320 | tf_op jit(solution)/shard_map/ppermute | solution.py:291
  81.3 1.1 %collective-permute-start.3 = (bf16[16,128,128]{2,1,0:T(8,128)(2,1)S(1)}, bf16[16,128,128]{2,1,0:T(8,128)(2,1)}, u32[]{:S(2)}, u32[]{:S(2)}) collective-permute-start(bf16[16,128,128]{2,1,0:T(8,128)(2,1)S(1)} %collective-permute-done.2.refs_2_), channel_id=1, source_target_pairs={{0,1},{1,0},{2,3},{3,2},{4,5},{5,4},{6,7},{7,6},{8,9},{9,8},{10,11... | collective-permute-start | bytes 1572872 | tf_op jit(solution)/shard_map/ppermute | solution.py:293
  82.4 0.0 collective-permute-done.6.refs_6_.refs_2_
  82.4 0.7 slice.9
  83.1 0.0 collective-permute-start.8
  83.1 0.0 collective-permute-done.5.refs_5_.refs_1_
  83.1 0.7 slice.8
  83.8 1.5 %collective-permute-start.7 = (bf16[16,64,128]{2,1,0:T(8,128)(2,1)}, bf16[16,64,128]{2,1,0:T(8,128)(2,1)}, u32[]{:S(2)}, u32[]{:S(2)}) collective-permute-start(bf16[16,64,128]{2,1,0:T(8,128)(2,1)} %slice.8), channel_id=1, source_target_pairs={{0,4},{4,8},{8,12},{12,0},{1,5},{5,9},{9,13},{13,1},{2,6},{6,10},{... | collective-permute-start | bytes 786440 | tf_op jit(solution)/shard_map/ppermute | solution.py:296
  85.3 0.1 stack.27.place_ref
  85.4 0.0 collective-permute-done.1.refs_1_
  85.4 0.0 collective-permute-done.3.refs_3_
  85.4 4.9 %shard_map.39 = (f32[16,2,256,256]{3,2,1,0:T(8,128)}, bf16[16,256,256]{2,1,0:T(8,128)(2,1)S(1)}) custom-call(s32[6]{0:T(128)S(1)} %stack.27.place_ref, bf16[16,128,128]{2,1,0:T(8,128)(2,1)S(1)} %all_to_all.5.refs_0_, bf16[16,128,128]{2,1,0:T(8,128)(2,1)S(1)} %collective-permute-done.1.refs_1_, bf16[16,128,128]{2,1,0:T(8,128)(2,1)S(1)} %collective-permute-done.2.refs_2_, ...), custom_call_target="tpu_custom_call" | custom-call | flops 536870912 | bytes 8388608 | tf_op jit(solution)/shard_map/pallas_call | solution.py:260
  90.3 1.0 %collective-permute-done.8.refs_4_ = bf16[16,64,128]{2,1,0:T(8,128)(2,1)S(1)} collective-permute-done((bf16[16,64,128]{2,1,0:T(8,128)(2,1)}, bf16[16,64,128]{2,1,0:T(8,128)(2,1)S(1)}, u32[]{:S(2)}, u32[]{:S(2)}) %collective-permute-start.8) | collective-permute-done | bytes 262176 | tf_op jit(solution)/shard_map/ppermute | solution.py:296
  91.4 0.0 collective-permute-done.7.refs_3_
  91.4 3.6 %shard_map.40 = f32[16,2,256,256]{3,2,1,0:T(8,128)} custom-call(s32[6]{0:T(128)S(1)} %stack.27.place_ref, bf16[16,256,256]{2,1,0:T(8,128)(2,1)S(1)} %get-tuple-element.7.refs_0_, bf16[16,128,128]{2,1,0:T(8,128)(2,1)S(1)} %collective-permute-done.5.refs_5_.refs_1_, ...), custom_call_target="tpu_custom_call", output_to_operand_aliasing={{}: (6, {})} | custom-call | flops 536870912 | bytes 8388608 | tf_op jit(solution)/shard_map/pallas_call | solution.py:260
Async XLA Ops:
  6.7 13.4 %collective-permute-start = (bf16[16,128,128]{2,1,0:T(8,128)(2,1)}, bf16[16,128,128]{2,1,0:T(8,128)(2,1)S(1)}, u32[]{:S(2)}, u32[]{:S(2)}) collective-permute-start(bf16[16,128,128]{2,1,0:T(8,128)(2,1)} %bitcast.16), channel_id=1, source_target_pairs={{16,0},{32,16},{48,32},{64,48},{80,64},{96,80},{112,96},{128,112},... | collective-permute-start | bytes 1572872 | tf_op jit(solution)/shard_map/ppermute | solution.py:285
  8.0 2.2 %copy-start = (bf16[64,8,2,2048]{3,2,1,0:T(2,128)(2,1)S(1)}, bf16[64,8,2,2048]{3,2,1,0:T(2,128)(2,1)}, u32[]{:S(2)}) copy-start(bf16[64,8,2,2048]{3,2,1,0:T(2,128)(2,1)} %param.3) | copy-start | bytes 12582916
  10.2 1.2 %copy-start.1 = (bf16[2,256,1024]{2,1,0:T(8,128)(2,1)S(1)}, bf16[2,256,1024]{2,1,0:T(8,128)(2,1)}, u32[]{:S(2)}) copy-start(bf16[2,256,1024]{2,1,0:T(8,128)(2,1)} %constant.36.clone.table_any) | copy-start | bytes 3145732
  11.5 0.8 copy-start.2
  47.5 19.2 %collective-permute-start.4 = (bf16[16,128,128]{2,1,0:T(8,128)(2,1)S(1)}, bf16[16,128,128]{2,1,0:T(8,128)(2,1)S(1)}, u32[]{:S(2)}, u32[]{:S(2)}) collective-permute-start(bf16[16,128,128]{2,1,0:T(8,128)(2,1)S(1)} %all_to_all.5.refs_0_), channel_id=1, source_target_pairs={{0,0},{1,4},{2,8},{3,12},{4,1},{5,5},{6,9},{7,13},{8,2},{9,6},{10,... | collective-permute-start | bytes 1572872 | tf_op jit(solution)/shard_map/ppermute | solution.py:288
  54.2 27.1 %collective-permute-start.2 = (bf16[16,128,128]{2,1,0:T(8,128)(2,1)S(1)}, bf16[16,128,128]{2,1,0:T(8,128)(2,1)S(1)}, u32[]{:S(2)}, u32[]{:S(2)}) collective-permute-start(bf16[16,128,128]{2,1,0:T(8,128)(2,1)S(1)} %all_to_all.5.refs_0_), channel_id=1, source_target_pairs={{0,2},{1,3},{2,0},{3,1},{4,6},{5,7},{6,4},{7,5},{8,10},{9,11},{10,... | collective-permute-start | bytes 1572872 | tf_op jit(solution)/shard_map/ppermute | solution.py:291
  66.6 15.7 %collective-permute-start.6 = (bf16[16,128,128]{2,1,0:T(8,128)(2,1)S(1)}, bf16[16,128,128]{2,1,0:T(8,128)(2,1)S(1)}, u32[]{:S(2)}, u32[]{:S(2)}) collective-permute-start(bf16[16,128,128]{2,1,0:T(8,128)(2,1)S(1)} %collective-permute-done.4.refs_4_), channel_id=1, source_target_pairs={{0,12},{4,0},{8,4},{12,8},{1,13},{5,1},{9,5},{13,9},{2,14},{6,2},{... | collective-permute-start | bytes 1572872 | tf_op jit(solution)/shard_map/ppermute | solution.py:295
  68.4 14.8 %collective-permute-start.5 = (bf16[16,128,128]{2,1,0:T(8,128)(2,1)S(1)}, bf16[16,128,128]{2,1,0:T(8,128)(2,1)S(1)}, u32[]{:S(2)}, u32[]{:S(2)}) collective-permute-start(bf16[16,128,128]{2,1,0:T(8,128)(2,1)S(1)} %collective-permute-done.4.refs_4_), channel_id=1, source_target_pairs={{0,4},{4,8},{8,12},{12,0},{1,5},{5,9},{9,13},{13,1},{2,6},{6,10},{... | collective-permute-start | bytes 1572872 | tf_op jit(solution)/shard_map/ppermute | solution.py:294
  68.4 17.0 %collective-permute-start.1 = (bf16[16,128,128]{2,1,0:T(8,128)(2,1)S(1)}, bf16[16,128,128]{2,1,0:T(8,128)(2,1)S(1)}, u32[]{:S(2)}, u32[]{:S(2)}) collective-permute-start(bf16[16,128,128]{2,1,0:T(8,128)(2,1)S(1)} %all_to_all.5.refs_0_), channel_id=1, source_target_pairs={{0,1},{1,0},{2,3},{3,2},{4,5},{5,4},{6,7},{7,6},{8,9},{9,8},{10,11... | collective-permute-start | bytes 1572872 | tf_op jit(solution)/shard_map/ppermute | solution.py:292
  81.3 4.1 %collective-permute-start.3 = (bf16[16,128,128]{2,1,0:T(8,128)(2,1)S(1)}, bf16[16,128,128]{2,1,0:T(8,128)(2,1)}, u32[]{:S(2)}, u32[]{:S(2)}) collective-permute-start(bf16[16,128,128]{2,1,0:T(8,128)(2,1)S(1)} %collective-permute-done.2.refs_2_), channel_id=1, source_target_pairs={{0,1},{1,0},{2,3},{3,2},{4,5},{5,4},{6,7},{7,6},{8,9},{9,8},{10,11... | collective-permute-start | bytes 1572872 | tf_op jit(solution)/shard_map/ppermute | solution.py:293
  83.1 8.3 %collective-permute-start.8 = (bf16[16,64,128]{2,1,0:T(8,128)(2,1)}, bf16[16,64,128]{2,1,0:T(8,128)(2,1)S(1)}, u32[]{:S(2)}, u32[]{:S(2)}) collective-permute-start(bf16[16,64,128]{2,1,0:T(8,128)(2,1)} %slice.9), channel_id=1, source_target_pairs={{0,12},{4,0},{8,4},{12,8},{1,13},{5,1},{9,5},{13,9},{2,14},{6,2},{... | collective-permute-start | bytes 786440 | tf_op jit(solution)/shard_map/ppermute | solution.py:296
  83.8 7.5 %collective-permute-start.7 = (bf16[16,64,128]{2,1,0:T(8,128)(2,1)}, bf16[16,64,128]{2,1,0:T(8,128)(2,1)}, u32[]{:S(2)}, u32[]{:S(2)}) collective-permute-start(bf16[16,64,128]{2,1,0:T(8,128)(2,1)} %slice.8), channel_id=1, source_target_pairs={{0,4},{4,8},{8,12},{12,0},{1,5},{5,9},{9,13},{13,1},{2,6},{6,10},{... | collective-permute-start | bytes 786440 | tf_op jit(solution)/shard_map/ppermute | solution.py:296

commit v7 on v6

--- a/solution.py
+++ b/solution.py
@@ -16,7 +16,7 @@
 TAPS = 8
 PITCH = 521
 INPUTS = 8
-UNROLL = 2
+UNROLL = 4
 GROUP = 16
 LANES = 128
 MIB = 1 << 20
@@ -143,9 +143,9 @@
         scratch_shapes=[
             pltpu.VMEM((64, 8, 32, LANES), jnp.bfloat16),
             pltpu.VMEM((TAPS, 32, LANES), jnp.float32),
-            pltpu.VMEM((TAPS * 33, LANES), jnp.float32),
+            pltpu.VMEM(((TAPS + 1) * 33, LANES), jnp.float32),
             pltpu.VMEM((2, KEEP, NCH // 2), jnp.bfloat16),
-            pltpu.VMEM((2 * GROUP * PITCH, LANES), jnp.float32),
+            pltpu.VMEM(((2 * GROUP + 1) * PITCH, LANES), jnp.float32),
             pltpu.VMEM((512, NCH // 2), jnp.bfloat16),
             pltpu.VMEM((2, 2, KEEP, 512), jnp.float32),
             pltpu.SemaphoreType.DMA((64 // INPUTS,)),

time: 96.3 us -> 96.2 us (level)
  transfers between devices with their start and end apart: 9 -> 9, of which waited for: 4 -> 4; matrix products, arithmetic and copies ran while one was open for 2% -> 2% of each run, Pallas kernels for 11% -> 10%
where the time goes in v7:
time: 96.2 us; the launch traced here: 94.8 us
  blocking collectives  27.1 us (28%)
  starting transfers between devices  21.3 us (22%)
  waiting for transfers between devices  20.4 us (21%)
  Pallas kernels  20 us (21%)
  local copies, waits for them, and re-layouts  5.78 us (6%)
    all_to_all x1, blocking collectives, per_device(): lax.all_to_all(whole, 'chan', split_axis=0, concat_axis=0, tiled=True)  27.1 us
    pallas_call x2, Pallas kernels, spectra(): pl.pallas_call(functools.partial(spectra_kernel, rim), in_specs=[pl.Block...  12 us
    ppermute x1, waiting for transfers between devices, per_device(): lax.ppermute(turned, ('row', 'col'), [(4 * r + c, 4 * c + r) for r in rin...  8.25 us
    ppermute x1, waiting for transfers between devices, per_device(): far = lax.ppermute(turned, 'col', [(c, c ^ 2) for c in ring])  8.16 us
    pallas_call x2, Pallas kernels, correlate(): pl.pallas_call(functools.partial(correlate_kernel, late), in_specs=in_spe...  8.06 us
    ppermute x1, starting transfers between devices, per_device(): lax.ppermute(turned, ('row', 'col'), [(4 * r + c, 4 * c + r) for r in rin...  6.7 us
    ppermute x1, starting transfers between devices, per_device(): near = lax.ppermute(turned, 'col', [(c, c ^ 1) for c in ring])  4.74 us
    unnamed x6, local copies, waits for them, and re-layouts  4.25 us
  transfers between devices with their start and end apart: 9, of which 4 were waited for; matrix products, arithmetic and copies ran while one was open for 2% of the time, Pallas kernels for 10%

profile of v7, /device:TPU:1, one launch (start us, length us, event | category | flops | bytes accessed | tf_op | source)
XLA Modules:
  0.0 94.8 jit_solution(9452448924658459355)
XLA Ops:
  0.0 6.8 %shard_map.38 = bf16[2048,128]{1,0:T(8,128)(2,1)} custom-call(bf16[64,8,32,128]{3,2,1,0:T(8,128)(2,1)} %bitcast.13, f32[8,2048]{1,0:T(8,128)} %raw_ref.3, bf16[2,256,1024]{2,1,0:T(8,128)(2,1)} %constant.36.clone.table_any), custom_call_target="tpu_custom_call" | custom-call | flops 1073741824 | bytes 6291456 | tf_op jit(solution)/shard_map/pallas_call | solution.py:134
  6.8 1.3 %collective-permute-start = (bf16[16,128,128]{2,1,0:T(8,128)(2,1)}, bf16[16,128,128]{2,1,0:T(8,128)(2,1)S(1)}, u32[]{:S(2)}, u32[]{:S(2)}) collective-permute-start(bf16[16,128,128]{2,1,0:T(8,128)(2,1)} %bitcast.16), channel_id=1, source_target_pairs={{16,0},{32,16},{48,32},{64,48},{80,64},{96,80},{112,96},{128,112},... | collective-permute-start | bytes 1572872 | tf_op jit(solution)/shard_map/ppermute | solution.py:285
  8.1 0.0 copy-start
  8.1 2.2 %copy-done = bf16[64,8,2,2048]{3,2,1,0:T(2,128)(2,1)S(1)} copy-done((bf16[64,8,2,2048]{3,2,1,0:T(2,128)(2,1)S(1)}, bf16[64,8,2,2048]{3,2,1,0:T(2,128)(2,1)}, u32[]{:S(2)}) %copy-start) | copy-done | bytes 4194328
  10.3 0.0 copy-start.1
  10.3 1.2 %copy-done.1 = bf16[2,256,1024]{2,1,0:T(8,128)(2,1)S(1)} copy-done((bf16[2,256,1024]{2,1,0:T(8,128)(2,1)S(1)}, bf16[2,256,1024]{2,1,0:T(8,128)(2,1)}, u32[]{:S(2)}) %copy-start.1) | copy-done | bytes 1048600
  11.5 0.0 copy-start.2
  11.5 0.8 copy-done.2
  12.3 5.2 %shard_map.37 = f32[2048,128]{1,0:T(8,128)S(1)} custom-call(bf16[64,8,32,128]{3,2,1,0:T(8,128)(2,1)S(1)} %bitcast.14, f32[8,2048]{1,0:T(8,128)S(1)} %copy-done.2, bf16[2,256,1024]{2,1,0:T(8,128)(2,1)S(1)} %copy-done.1), custom_call_target="tpu_custom_call" | custom-call | flops 1073741824 | bytes 6291456 | tf_op jit(solution)/shard_map/pallas_call | solution.py:134
  17.5 2.7 %collective-permute-done = bf16[16,128,128]{2,1,0:T(8,128)(2,1)S(1)} collective-permute-done((bf16[16,128,128]{2,1,0:T(8,128)(2,1)}, bf16[16,128,128]{2,1,0:T(8,128)(2,1)S(1)}, u32[]{:S(2)}, u32[]{:S(2)}) %collective-permute-start) | collective-permute-done | bytes 524320 | tf_op jit(solution)/shard_map/ppermute | solution.py:285
  20.2 0.1 add_convert_fusion
  20.4 27.1 %all_to_all.5.refs_0_ = bf16[16,128,128]{2,1,0:T(8,128)(2,1)S(1)} all-to-all(bf16[16,128,128]{2,1,0:T(8,128)(2,1)S(1)} %add_convert_fusion), channel_id=1, replica_groups=mesh['chan'=16,'row'=4,'col'=4] {'chan'}, dimensions={0} | all-to-all | bytes 1048576 | tf_op jit(solution)/shard_map/all_to_all | solution.py:287
  47.5 6.7 %collective-permute-start.4 = (bf16[16,128,128]{2,1,0:T(8,128)(2,1)S(1)}, bf16[16,128,128]{2,1,0:T(8,128)(2,1)S(1)}, u32[]{:S(2)}, u32[]{:S(2)}) collective-permute-start(bf16[16,128,128]{2,1,0:T(8,128)(2,1)S(1)} %all_to_all.5.refs_0_), channel_id=1, source_target_pairs={{0,0},{1,4},{2,8},{3,12},{4,1},{5,5},{6,9},{7,13},{8,2},{9,6},{10,... | collective-permute-start | bytes 1572872 | tf_op jit(solution)/shard_map/ppermute | solution.py:288
  54.2 4.2 %collective-permute-start.2 = (bf16[16,128,128]{2,1,0:T(8,128)(2,1)S(1)}, bf16[16,128,128]{2,1,0:T(8,128)(2,1)S(1)}, u32[]{:S(2)}, u32[]{:S(2)}) collective-permute-start(bf16[16,128,128]{2,1,0:T(8,128)(2,1)S(1)} %all_to_all.5.refs_0_), channel_id=1, source_target_pairs={{0,2},{1,3},{2,0},{3,1},{4,6},{5,7},{6,4},{7,5},{8,10},{9,11},{10,... | collective-permute-start | bytes 1572872 | tf_op jit(solution)/shard_map/ppermute | solution.py:291
  58.4 8.3 %collective-permute-done.4.refs_4_ = bf16[16,128,128]{2,1,0:T(8,128)(2,1)S(1)} collective-permute-done((bf16[16,128,128]{2,1,0:T(8,128)(2,1)S(1)}, bf16[16,128,128]{2,1,0:T(8,128)(2,1)S(1)}, u32[]{:S(2)}, u32[]{:S(2)}) %collective-permute-start.4) | collective-permute-done | bytes 524320 | tf_op jit(solution)/shard_map/ppermute | solution.py:288
  66.7 1.7 %collective-permute-start.6 = (bf16[16,128,128]{2,1,0:T(8,128)(2,1)S(1)}, bf16[16,128,128]{2,1,0:T(8,128)(2,1)S(1)}, u32[]{:S(2)}, u32[]{:S(2)}) collective-permute-start(bf16[16,128,128]{2,1,0:T(8,128)(2,1)S(1)} %collective-permute-done.4.refs_4_), channel_id=1, source_target_pairs={{0,12},{4,0},{8,4},{12,8},{1,13},{5,1},{9,5},{13,9},{2,14},{6,2},{... | collective-permute-start | bytes 1572872 | tf_op jit(solution)/shard_map/ppermute | solution.py:295
  68.4 0.0 collective-permute-start.5
  68.4 4.7 %collective-permute-start.1 = (bf16[16,128,128]{2,1,0:T(8,128)(2,1)S(1)}, bf16[16,128,128]{2,1,0:T(8,128)(2,1)S(1)}, u32[]{:S(2)}, u32[]{:S(2)}) collective-permute-start(bf16[16,128,128]{2,1,0:T(8,128)(2,1)S(1)} %all_to_all.5.refs_0_), channel_id=1, source_target_pairs={{0,1},{1,0},{2,3},{3,2},{4,5},{5,4},{6,7},{7,6},{8,9},{9,8},{10,11... | collective-permute-start | bytes 1572872 | tf_op jit(solution)/shard_map/ppermute | solution.py:292
  73.2 8.2 %collective-permute-done.2.refs_2_ = bf16[16,128,128]{2,1,0:T(8,128)(2,1)S(1)} collective-permute-done((bf16[16,128,128]{2,1,0:T(8,128)(2,1)S(1)}, bf16[16,128,128]{2,1,0:T(8,128)(2,1)S(1)}, u32[]{:S(2)}, u32[]{:S(2)}) %collective-permute-start.2) | collective-permute-done | bytes 524320 | tf_op jit(solution)/shard_map/ppermute | solution.py:291
  81.3 1.1 %collective-permute-start.3 = (bf16[16,128,128]{2,1,0:T(8,128)(2,1)S(1)}, bf16[16,128,128]{2,1,0:T(8,128)(2,1)}, u32[]{:S(2)}, u32[]{:S(2)}) collective-permute-start(bf16[16,128,128]{2,1,0:T(8,128)(2,1)S(1)} %collective-permute-done.2.refs_2_), channel_id=1, source_target_pairs={{0,1},{1,0},{2,3},{3,2},{4,5},{5,4},{6,7},{7,6},{8,9},{9,8},{10,11... | collective-permute-start | bytes 1572872 | tf_op jit(solution)/shard_map/ppermute | solution.py:293
  82.4 0.0 collective-permute-done.6.refs_6_.refs_2_
  82.4 0.7 slice.9
  83.2 0.0 collective-permute-start.8
  83.2 0.0 collective-permute-done.5.refs_5_.refs_1_
  83.2 0.7 slice.8
  83.9 1.5 %collective-permute-start.7 = (bf16[16,64,128]{2,1,0:T(8,128)(2,1)}, bf16[16,64,128]{2,1,0:T(8,128)(2,1)}, u32[]{:S(2)}, u32[]{:S(2)}) collective-permute-start(bf16[16,64,128]{2,1,0:T(8,128)(2,1)} %slice.8), channel_id=1, source_target_pairs={{0,4},{4,8},{8,12},{12,0},{1,5},{5,9},{9,13},{13,1},{2,6},{6,10},{... | collective-permute-start | bytes 786440 | tf_op jit(solution)/shard_map/ppermute | solution.py:296
  85.4 0.1 stack.27.place_ref
  85.5 0.0 collective-permute-done.1.refs_1_
  85.5 0.0 collective-permute-done.3.refs_3_
  85.5 4.7 %shard_map.39 = (f32[16,2,256,256]{3,2,1,0:T(8,128)}, bf16[16,256,256]{2,1,0:T(8,128)(2,1)S(1)}) custom-call(s32[6]{0:T(128)S(1)} %stack.27.place_ref, bf16[16,128,128]{2,1,0:T(8,128)(2,1)S(1)} %all_to_all.5.refs_0_, bf16[16,128,128]{2,1,0:T(8,128)(2,1)S(1)} %collective-permute-done.1.refs_1_, bf16[16,128,128]{2,1,0:T(8,128)(2,1)S(1)} %collective-permute-done.2.refs_2_, ...), custom_call_target="tpu_custom_call" | custom-call | flops 536870912 | bytes 8388608 | tf_op jit(solution)/shard_map/pallas_call | solution.py:260
  90.1 1.3 %collective-permute-done.8.refs_4_ = bf16[16,64,128]{2,1,0:T(8,128)(2,1)S(1)} collective-permute-done((bf16[16,64,128]{2,1,0:T(8,128)(2,1)}, bf16[16,64,128]{2,1,0:T(8,128)(2,1)S(1)}, u32[]{:S(2)}, u32[]{:S(2)}) %collective-permute-start.8) | collective-permute-done | bytes 262176 | tf_op jit(solution)/shard_map/ppermute | solution.py:296
  91.4 0.0 collective-permute-done.7.refs_3_
  91.4 3.4 %shard_map.40 = f32[16,2,256,256]{3,2,1,0:T(8,128)} custom-call(s32[6]{0:T(128)S(1)} %stack.27.place_ref, bf16[16,256,256]{2,1,0:T(8,128)(2,1)S(1)} %get-tuple-element.7.refs_0_, bf16[16,128,128]{2,1,0:T(8,128)(2,1)S(1)} %collective-permute-done.5.refs_5_.refs_1_, ...), custom_call_target="tpu_custom_call", output_to_operand_aliasing={{}: (6, {})} | custom-call | flops 536870912 | bytes 8388608 | tf_op jit(solution)/shard_map/pallas_call | solution.py:260
Async XLA Ops:
  6.8 13.5 %collective-permute-start = (bf16[16,128,128]{2,1,0:T(8,128)(2,1)}, bf16[16,128,128]{2,1,0:T(8,128)(2,1)S(1)}, u32[]{:S(2)}, u32[]{:S(2)}) collective-permute-start(bf16[16,128,128]{2,1,0:T(8,128)(2,1)} %bitcast.16), channel_id=1, source_target_pairs={{16,0},{32,16},{48,32},{64,48},{80,64},{96,80},{112,96},{128,112},... | collective-permute-start | bytes 1572872 | tf_op jit(solution)/shard_map/ppermute | solution.py:285
  8.1 2.2 %copy-start = (bf16[64,8,2,2048]{3,2,1,0:T(2,128)(2,1)S(1)}, bf16[64,8,2,2048]{3,2,1,0:T(2,128)(2,1)}, u32[]{:S(2)}) copy-start(bf16[64,8,2,2048]{3,2,1,0:T(2,128)(2,1)} %param.3) | copy-start | bytes 12582916
  10.3 1.2 %copy-start.1 = (bf16[2,256,1024]{2,1,0:T(8,128)(2,1)S(1)}, bf16[2,256,1024]{2,1,0:T(8,128)(2,1)}, u32[]{:S(2)}) copy-start(bf16[2,256,1024]{2,1,0:T(8,128)(2,1)} %constant.36.clone.table_any) | copy-start | bytes 3145732
  11.5 0.8 copy-start.2
  47.5 19.2 %collective-permute-start.4 = (bf16[16,128,128]{2,1,0:T(8,128)(2,1)S(1)}, bf16[16,128,128]{2,1,0:T(8,128)(2,1)S(1)}, u32[]{:S(2)}, u32[]{:S(2)}) collective-permute-start(bf16[16,128,128]{2,1,0:T(8,128)(2,1)S(1)} %all_to_all.5.refs_0_), channel_id=1, source_target_pairs={{0,0},{1,4},{2,8},{3,12},{4,1},{5,5},{6,9},{7,13},{8,2},{9,6},{10,... | collective-permute-start | bytes 1572872 | tf_op jit(solution)/shard_map/ppermute | solution.py:288
  54.2 27.1 %collective-permute-start.2 = (bf16[16,128,128]{2,1,0:T(8,128)(2,1)S(1)}, bf16[16,128,128]{2,1,0:T(8,128)(2,1)S(1)}, u32[]{:S(2)}, u32[]{:S(2)}) collective-permute-start(bf16[16,128,128]{2,1,0:T(8,128)(2,1)S(1)} %all_to_all.5.refs_0_), channel_id=1, source_target_pairs={{0,2},{1,3},{2,0},{3,1},{4,6},{5,7},{6,4},{7,5},{8,10},{9,11},{10,... | collective-permute-start | bytes 1572872 | tf_op jit(solution)/shard_map/ppermute | solution.py:291
  66.7 15.7 %collective-permute-start.6 = (bf16[16,128,128]{2,1,0:T(8,128)(2,1)S(1)}, bf16[16,128,128]{2,1,0:T(8,128)(2,1)S(1)}, u32[]{:S(2)}, u32[]{:S(2)}) collective-permute-start(bf16[16,128,128]{2,1,0:T(8,128)(2,1)S(1)} %collective-permute-done.4.refs_4_), channel_id=1, source_target_pairs={{0,12},{4,0},{8,4},{12,8},{1,13},{5,1},{9,5},{13,9},{2,14},{6,2},{... | collective-permute-start | bytes 1572872 | tf_op jit(solution)/shard_map/ppermute | solution.py:295
  68.4 14.8 %collective-permute-start.5 = (bf16[16,128,128]{2,1,0:T(8,128)(2,1)S(1)}, bf16[16,128,128]{2,1,0:T(8,128)(2,1)S(1)}, u32[]{:S(2)}, u32[]{:S(2)}) collective-permute-start(bf16[16,128,128]{2,1,0:T(8,128)(2,1)S(1)} %collective-permute-done.4.refs_4_), channel_id=1, source_target_pairs={{0,4},{4,8},{8,12},{12,0},{1,5},{5,9},{9,13},{13,1},{2,6},{6,10},{... | collective-permute-start | bytes 1572872 | tf_op jit(solution)/shard_map/ppermute | solution.py:294
  68.4 17.0 %collective-permute-start.1 = (bf16[16,128,128]{2,1,0:T(8,128)(2,1)S(1)}, bf16[16,128,128]{2,1,0:T(8,128)(2,1)S(1)}, u32[]{:S(2)}, u32[]{:S(2)}) collective-permute-start(bf16[16,128,128]{2,1,0:T(8,128)(2,1)S(1)} %all_to_all.5.refs_0_), channel_id=1, source_target_pairs={{0,1},{1,0},{2,3},{3,2},{4,5},{5,4},{6,7},{7,6},{8,9},{9,8},{10,11... | collective-permute-start | bytes 1572872 | tf_op jit(solution)/shard_map/ppermute | solution.py:292
  81.3 4.1 %collective-permute-start.3 = (bf16[16,128,128]{2,1,0:T(8,128)(2,1)S(1)}, bf16[16,128,128]{2,1,0:T(8,128)(2,1)}, u32[]{:S(2)}, u32[]{:S(2)}) collective-permute-start(bf16[16,128,128]{2,1,0:T(8,128)(2,1)S(1)} %collective-permute-done.2.refs_2_), channel_id=1, source_target_pairs={{0,1},{1,0},{2,3},{3,2},{4,5},{5,4},{6,7},{7,6},{8,9},{9,8},{10,11... | collective-permute-start | bytes 1572872 | tf_op jit(solution)/shard_map/ppermute | solution.py:293
  83.2 8.3 %collective-permute-start.8 = (bf16[16,64,128]{2,1,0:T(8,128)(2,1)}, bf16[16,64,128]{2,1,0:T(8,128)(2,1)S(1)}, u32[]{:S(2)}, u32[]{:S(2)}) collective-permute-start(bf16[16,64,128]{2,1,0:T(8,128)(2,1)} %slice.9), channel_id=1, source_target_pairs={{0,12},{4,0},{8,4},{12,8},{1,13},{5,1},{9,5},{13,9},{2,14},{6,2},{... | collective-permute-start | bytes 786440 | tf_op jit(solution)/shard_map/ppermute | solution.py:296
  83.9 7.5 %collective-permute-start.7 = (bf16[16,64,128]{2,1,0:T(8,128)(2,1)}, bf16[16,64,128]{2,1,0:T(8,128)(2,1)}, u32[]{:S(2)}, u32[]{:S(2)}) collective-permute-start(bf16[16,64,128]{2,1,0:T(8,128)(2,1)} %slice.8), channel_id=1, source_target_pairs={{0,4},{4,8},{8,12},{12,0},{1,5},{5,9},{9,13},{13,1},{2,6},{6,10},{... | collective-permute-start | bytes 786440 | tf_op jit(solution)/shard_map/ppermute | solution.py:296

commit v8 on v7

--- a/solution.py
+++ b/solution.py
@@ -90,7 +90,7 @@
 
     for b, load in enumerate(loads):
         load.wait()
-        lax.fori_loop(b * INPUTS, (b + 1) * INPUTS, filter_input, 0, unroll=4)
+        lax.fori_loop(b * INPUTS, (b + 1) * INPUTS, filter_input, 0, unroll=8)
 
     table_load.wait()
     def transform(low_bit, carry):

time: 96.2 us -> 96.2 us (level)
  no operation moved by 1% of the time
where the time goes in v8:
time: 96.2 us; the launch traced here: 94.9 us
  blocking collectives  27.1 us (28%)
  starting transfers between devices  21.3 us (22%)
  waiting for transfers between devices  20.6 us (21%)
  Pallas kernels  19.7 us (20%)
  local copies, waits for them, and re-layouts  5.78 us (6%)
    all_to_all x1, blocking collectives, per_device(): lax.all_to_all(whole, 'chan', split_axis=0, concat_axis=0, tiled=True)  27.1 us
    pallas_call x2, Pallas kernels, spectra(): pl.pallas_call(functools.partial(spectra_kernel, rim), in_specs=[pl.Block...  11.6 us
    ppermute x1, waiting for transfers between devices, per_device(): lax.ppermute(turned, ('row', 'col'), [(4 * r + c, 4 * c + r) for r in rin...  8.26 us
    ppermute x1, waiting for transfers between devices, per_device(): far = lax.ppermute(turned, 'col', [(c, c ^ 2) for c in ring])  8.16 us
    pallas_call x2, Pallas kernels, correlate(): pl.pallas_call(functools.partial(correlate_kernel, late), in_specs=in_spe...  8.06 us
    ppermute x1, starting transfers between devices, per_device(): lax.ppermute(turned, ('row', 'col'), [(4 * r + c, 4 * c + r) for r in rin...  6.71 us
    ppermute x1, starting transfers between devices, per_device(): near = lax.ppermute(turned, 'col', [(c, c ^ 1) for c in ring])  4.74 us
    unnamed x6, local copies, waits for them, and re-layouts  4.25 us
  transfers between devices with their start and end apart: 9, of which 4 were waited for; matrix products, arithmetic and copies ran while one was open for 2% of the time, Pallas kernels for 10%

profile of v8, /device:TPU:1, one launch (start us, length us, event | category | flops | bytes accessed | tf_op | source)
XLA Modules:
  0.0 94.9 jit_solution(479317161253139779)
XLA Ops:
  0.0 6.7 %shard_map.38 = bf16[2048,128]{1,0:T(8,128)(2,1)} custom-call(bf16[64,8,32,128]{3,2,1,0:T(8,128)(2,1)} %bitcast.13, f32[8,2048]{1,0:T(8,128)} %raw_ref.3, bf16[2,256,1024]{2,1,0:T(8,128)(2,1)} %constant.36.clone.table_any), custom_call_target="tpu_custom_call" | custom-call | flops 1073741824 | bytes 6291456 | tf_op jit(solution)/shard_map/pallas_call | solution.py:134
  6.7 1.3 %collective-permute-start = (bf16[16,128,128]{2,1,0:T(8,128)(2,1)}, bf16[16,128,128]{2,1,0:T(8,128)(2,1)S(1)}, u32[]{:S(2)}, u32[]{:S(2)}) collective-permute-start(bf16[16,128,128]{2,1,0:T(8,128)(2,1)} %bitcast.16), channel_id=1, source_target_pairs={{16,0},{32,16},{48,32},{64,48},{80,64},{96,80},{112,96},{128,112},... | collective-permute-start | bytes 1572872 | tf_op jit(solution)/shard_map/ppermute | solution.py:285
  8.0 0.0 copy-start
  8.0 2.2 %copy-done = bf16[64,8,2,2048]{3,2,1,0:T(2,128)(2,1)S(1)} copy-done((bf16[64,8,2,2048]{3,2,1,0:T(2,128)(2,1)S(1)}, bf16[64,8,2,2048]{3,2,1,0:T(2,128)(2,1)}, u32[]{:S(2)}) %copy-start) | copy-done | bytes 4194328
  10.2 0.0 copy-start.1
  10.2 1.2 %copy-done.1 = bf16[2,256,1024]{2,1,0:T(8,128)(2,1)S(1)} copy-done((bf16[2,256,1024]{2,1,0:T(8,128)(2,1)S(1)}, bf16[2,256,1024]{2,1,0:T(8,128)(2,1)}, u32[]{:S(2)}) %copy-start.1) | copy-done | bytes 1048600
  11.4 0.0 copy-start.2
  11.4 0.8 copy-done.2
  12.2 5.0 %shard_map.37 = f32[2048,128]{1,0:T(8,128)S(1)} custom-call(bf16[64,8,32,128]{3,2,1,0:T(8,128)(2,1)S(1)} %bitcast.14, f32[8,2048]{1,0:T(8,128)S(1)} %copy-done.2, bf16[2,256,1024]{2,1,0:T(8,128)(2,1)S(1)} %copy-done.1), custom_call_target="tpu_custom_call" | custom-call | flops 1073741824 | bytes 6291456 | tf_op jit(solution)/shard_map/pallas_call | solution.py:134
  17.2 2.9 %collective-permute-done = bf16[16,128,128]{2,1,0:T(8,128)(2,1)S(1)} collective-permute-done((bf16[16,128,128]{2,1,0:T(8,128)(2,1)}, bf16[16,128,128]{2,1,0:T(8,128)(2,1)S(1)}, u32[]{:S(2)}, u32[]{:S(2)}) %collective-permute-start) | collective-permute-done | bytes 524320 | tf_op jit(solution)/shard_map/ppermute | solution.py:285
  20.1 0.1 add_convert_fusion
  20.2 27.1 %all_to_all.5.refs_0_ = bf16[16,128,128]{2,1,0:T(8,128)(2,1)S(1)} all-to-all(bf16[16,128,128]{2,1,0:T(8,128)(2,1)S(1)} %add_convert_fusion), channel_id=1, replica_groups=mesh['chan'=16,'row'=4,'col'=4] {'chan'}, dimensions={0} | all-to-all | bytes 1048576 | tf_op jit(solution)/shard_map/all_to_all | solution.py:287
  47.4 6.7 %collective-permute-start.4 = (bf16[16,128,128]{2,1,0:T(8,128)(2,1)S(1)}, bf16[16,128,128]{2,1,0:T(8,128)(2,1)S(1)}, u32[]{:S(2)}, u32[]{:S(2)}) collective-permute-start(bf16[16,128,128]{2,1,0:T(8,128)(2,1)S(1)} %all_to_all.5.refs_0_), channel_id=1, source_target_pairs={{0,0},{1,4},{2,8},{3,12},{4,1},{5,5},{6,9},{7,13},{8,2},{9,6},{10,... | collective-permute-start | bytes 1572872 | tf_op jit(solution)/shard_map/ppermute | solution.py:288
  54.1 4.2 %collective-permute-start.2 = (bf16[16,128,128]{2,1,0:T(8,128)(2,1)S(1)}, bf16[16,128,128]{2,1,0:T(8,128)(2,1)S(1)}, u32[]{:S(2)}, u32[]{:S(2)}) collective-permute-start(bf16[16,128,128]{2,1,0:T(8,128)(2,1)S(1)} %all_to_all.5.refs_0_), channel_id=1, source_target_pairs={{0,2},{1,3},{2,0},{3,1},{4,6},{5,7},{6,4},{7,5},{8,10},{9,11},{10,... | collective-permute-start | bytes 1572872 | tf_op jit(solution)/shard_map/ppermute | solution.py:291
  58.3 8.3 %collective-permute-done.4.refs_4_ = bf16[16,128,128]{2,1,0:T(8,128)(2,1)S(1)} collective-permute-done((bf16[16,128,128]{2,1,0:T(8,128)(2,1)S(1)}, bf16[16,128,128]{2,1,0:T(8,128)(2,1)S(1)}, u32[]{:S(2)}, u32[]{:S(2)}) %collective-permute-start.4) | collective-permute-done | bytes 524320 | tf_op jit(solution)/shard_map/ppermute | solution.py:288
  66.6 1.7 %collective-permute-start.6 = (bf16[16,128,128]{2,1,0:T(8,128)(2,1)S(1)}, bf16[16,128,128]{2,1,0:T(8,128)(2,1)S(1)}, u32[]{:S(2)}, u32[]{:S(2)}) collective-permute-start(bf16[16,128,128]{2,1,0:T(8,128)(2,1)S(1)} %collective-permute-done.4.refs_4_), channel_id=1, source_target_pairs={{0,12},{4,0},{8,4},{12,8},{1,13},{5,1},{9,5},{13,9},{2,14},{6,2},{... | collective-permute-start | bytes 1572872 | tf_op jit(solution)/shard_map/ppermute | solution.py:295
  68.3 0.0 collective-permute-start.5
  68.3 4.7 %collective-permute-start.1 = (bf16[16,128,128]{2,1,0:T(8,128)(2,1)S(1)}, bf16[16,128,128]{2,1,0:T(8,128)(2,1)S(1)}, u32[]{:S(2)}, u32[]{:S(2)}) collective-permute-start(bf16[16,128,128]{2,1,0:T(8,128)(2,1)S(1)} %all_to_all.5.refs_0_), channel_id=1, source_target_pairs={{0,1},{1,0},{2,3},{3,2},{4,5},{5,4},{6,7},{7,6},{8,9},{9,8},{10,11... | collective-permute-start | bytes 1572872 | tf_op jit(solution)/shard_map/ppermute | solution.py:292
  73.0 8.2 %collective-permute-done.2.refs_2_ = bf16[16,128,128]{2,1,0:T(8,128)(2,1)S(1)} collective-permute-done((bf16[16,128,128]{2,1,0:T(8,128)(2,1)S(1)}, bf16[16,128,128]{2,1,0:T(8,128)(2,1)S(1)}, u32[]{:S(2)}, u32[]{:S(2)}) %collective-permute-start.2) | collective-permute-done | bytes 524320 | tf_op jit(solution)/shard_map/ppermute | solution.py:291
  81.2 1.1 %collective-permute-start.3 = (bf16[16,128,128]{2,1,0:T(8,128)(2,1)S(1)}, bf16[16,128,128]{2,1,0:T(8,128)(2,1)}, u32[]{:S(2)}, u32[]{:S(2)}) collective-permute-start(bf16[16,128,128]{2,1,0:T(8,128)(2,1)S(1)} %collective-permute-done.2.refs_2_), channel_id=1, source_target_pairs={{0,1},{1,0},{2,3},{3,2},{4,5},{5,4},{6,7},{7,6},{8,9},{9,8},{10,11... | collective-permute-start | bytes 1572872 | tf_op jit(solution)/shard_map/ppermute | solution.py:293
  82.3 0.0 collective-permute-done.6.refs_6_.refs_2_
  82.3 0.7 slice.9
  83.1 0.0 collective-permute-start.8
  83.1 0.0 collective-permute-done.5.refs_5_.refs_1_
  83.1 0.7 slice.8
  83.8 1.5 %collective-permute-start.7 = (bf16[16,64,128]{2,1,0:T(8,128)(2,1)}, bf16[16,64,128]{2,1,0:T(8,128)(2,1)}, u32[]{:S(2)}, u32[]{:S(2)}) collective-permute-start(bf16[16,64,128]{2,1,0:T(8,128)(2,1)} %slice.8), channel_id=1, source_target_pairs={{0,4},{4,8},{8,12},{12,0},{1,5},{5,9},{9,13},{13,1},{2,6},{6,10},{... | collective-permute-start | bytes 786440 | tf_op jit(solution)/shard_map/ppermute | solution.py:296
  85.2 0.1 stack.27.place_ref
  85.3 0.0 collective-permute-done.1.refs_1_
  85.3 0.0 collective-permute-done.3.refs_3_
  85.3 4.7 %shard_map.39 = (f32[16,2,256,256]{3,2,1,0:T(8,128)}, bf16[16,256,256]{2,1,0:T(8,128)(2,1)S(1)}) custom-call(s32[6]{0:T(128)S(1)} %stack.27.place_ref, bf16[16,128,128]{2,1,0:T(8,128)(2,1)S(1)} %all_to_all.5.refs_0_, bf16[16,128,128]{2,1,0:T(8,128)(2,1)S(1)} %collective-permute-done.1.refs_1_, bf16[16,128,128]{2,1,0:T(8,128)(2,1)S(1)} %collective-permute-done.2.refs_2_, ...), custom_call_target="tpu_custom_call" | custom-call | flops 536870912 | bytes 8388608 | tf_op jit(solution)/shard_map/pallas_call | solution.py:260
  90.0 1.3 %collective-permute-done.8.refs_4_ = bf16[16,64,128]{2,1,0:T(8,128)(2,1)S(1)} collective-permute-done((bf16[16,64,128]{2,1,0:T(8,128)(2,1)}, bf16[16,64,128]{2,1,0:T(8,128)(2,1)S(1)}, u32[]{:S(2)}, u32[]{:S(2)}) %collective-permute-start.8) | collective-permute-done | bytes 262176 | tf_op jit(solution)/shard_map/ppermute | solution.py:296
  91.3 0.0 collective-permute-done.7.refs_3_
  91.3 3.4 %shard_map.40 = f32[16,2,256,256]{3,2,1,0:T(8,128)} custom-call(s32[6]{0:T(128)S(1)} %stack.27.place_ref, bf16[16,256,256]{2,1,0:T(8,128)(2,1)S(1)} %get-tuple-element.7.refs_0_, bf16[16,128,128]{2,1,0:T(8,128)(2,1)S(1)} %collective-permute-done.5.refs_5_.refs_1_, ...), custom_call_target="tpu_custom_call", output_to_operand_aliasing={{}: (6, {})} | custom-call | flops 536870912 | bytes 8388608 | tf_op jit(solution)/shard_map/pallas_call | solution.py:260
Async XLA Ops:
  6.7 13.4 %collective-permute-start = (bf16[16,128,128]{2,1,0:T(8,128)(2,1)}, bf16[16,128,128]{2,1,0:T(8,128)(2,1)S(1)}, u32[]{:S(2)}, u32[]{:S(2)}) collective-permute-start(bf16[16,128,128]{2,1,0:T(8,128)(2,1)} %bitcast.16), channel_id=1, source_target_pairs={{16,0},{32,16},{48,32},{64,48},{80,64},{96,80},{112,96},{128,112},... | collective-permute-start | bytes 1572872 | tf_op jit(solution)/shard_map/ppermute | solution.py:285
  8.0 2.2 %copy-start = (bf16[64,8,2,2048]{3,2,1,0:T(2,128)(2,1)S(1)}, bf16[64,8,2,2048]{3,2,1,0:T(2,128)(2,1)}, u32[]{:S(2)}) copy-start(bf16[64,8,2,2048]{3,2,1,0:T(2,128)(2,1)} %param.3) | copy-start | bytes 12582916
  10.2 1.2 %copy-start.1 = (bf16[2,256,1024]{2,1,0:T(8,128)(2,1)S(1)}, bf16[2,256,1024]{2,1,0:T(8,128)(2,1)}, u32[]{:S(2)}) copy-start(bf16[2,256,1024]{2,1,0:T(8,128)(2,1)} %constant.36.clone.table_any) | copy-start | bytes 3145732
  11.4 0.8 copy-start.2
  47.4 19.2 %collective-permute-start.4 = (bf16[16,128,128]{2,1,0:T(8,128)(2,1)S(1)}, bf16[16,128,128]{2,1,0:T(8,128)(2,1)S(1)}, u32[]{:S(2)}, u32[]{:S(2)}) collective-permute-start(bf16[16,128,128]{2,1,0:T(8,128)(2,1)S(1)} %all_to_all.5.refs_0_), channel_id=1, source_target_pairs={{0,0},{1,4},{2,8},{3,12},{4,1},{5,5},{6,9},{7,13},{8,2},{9,6},{10,... | collective-permute-start | bytes 1572872 | tf_op jit(solution)/shard_map/ppermute | solution.py:288
  54.1 27.1 %collective-permute-start.2 = (bf16[16,128,128]{2,1,0:T(8,128)(2,1)S(1)}, bf16[16,128,128]{2,1,0:T(8,128)(2,1)S(1)}, u32[]{:S(2)}, u32[]{:S(2)}) collective-permute-start(bf16[16,128,128]{2,1,0:T(8,128)(2,1)S(1)} %all_to_all.5.refs_0_), channel_id=1, source_target_pairs={{0,2},{1,3},{2,0},{3,1},{4,6},{5,7},{6,4},{7,5},{8,10},{9,11},{10,... | collective-permute-start | bytes 1572872 | tf_op jit(solution)/shard_map/ppermute | solution.py:291
  66.6 15.7 %collective-permute-start.6 = (bf16[16,128,128]{2,1,0:T(8,128)(2,1)S(1)}, bf16[16,128,128]{2,1,0:T(8,128)(2,1)S(1)}, u32[]{:S(2)}, u32[]{:S(2)}) collective-permute-start(bf16[16,128,128]{2,1,0:T(8,128)(2,1)S(1)} %collective-permute-done.4.refs_4_), channel_id=1, source_target_pairs={{0,12},{4,0},{8,4},{12,8},{1,13},{5,1},{9,5},{13,9},{2,14},{6,2},{... | collective-permute-start | bytes 1572872 | tf_op jit(solution)/shard_map/ppermute | solution.py:295
  68.3 14.8 %collective-permute-start.5 = (bf16[16,128,128]{2,1,0:T(8,128)(2,1)S(1)}, bf16[16,128,128]{2,1,0:T(8,128)(2,1)S(1)}, u32[]{:S(2)}, u32[]{:S(2)}) collective-permute-start(bf16[16,128,128]{2,1,0:T(8,128)(2,1)S(1)} %collective-permute-done.4.refs_4_), channel_id=1, source_target_pairs={{0,4},{4,8},{8,12},{12,0},{1,5},{5,9},{9,13},{13,1},{2,6},{6,10},{... | collective-permute-start | bytes 1572872 | tf_op jit(solution)/shard_map/ppermute | solution.py:294
  68.3 17.0 %collective-permute-start.1 = (bf16[16,128,128]{2,1,0:T(8,128)(2,1)S(1)}, bf16[16,128,128]{2,1,0:T(8,128)(2,1)S(1)}, u32[]{:S(2)}, u32[]{:S(2)}) collective-permute-start(bf16[16,128,128]{2,1,0:T(8,128)(2,1)S(1)} %all_to_all.5.refs_0_), channel_id=1, source_target_pairs={{0,1},{1,0},{2,3},{3,2},{4,5},{5,4},{6,7},{7,6},{8,9},{9,8},{10,11... | collective-permute-start | bytes 1572872 | tf_op jit(solution)/shard_map/ppermute | solution.py:292
  81.2 4.1 %collective-permute-start.3 = (bf16[16,128,128]{2,1,0:T(8,128)(2,1)S(1)}, bf16[16,128,128]{2,1,0:T(8,128)(2,1)}, u32[]{:S(2)}, u32[]{:S(2)}) collective-permute-start(bf16[16,128,128]{2,1,0:T(8,128)(2,1)S(1)} %collective-permute-done.2.refs_2_), channel_id=1, source_target_pairs={{0,1},{1,0},{2,3},{3,2},{4,5},{5,4},{6,7},{7,6},{8,9},{9,8},{10,11... | collective-permute-start | bytes 1572872 | tf_op jit(solution)/shard_map/ppermute | solution.py:293
  83.1 8.3 %collective-permute-start.8 = (bf16[16,64,128]{2,1,0:T(8,128)(2,1)}, bf16[16,64,128]{2,1,0:T(8,128)(2,1)S(1)}, u32[]{:S(2)}, u32[]{:S(2)}) collective-permute-start(bf16[16,64,128]{2,1,0:T(8,128)(2,1)} %slice.9), channel_id=1, source_target_pairs={{0,12},{4,0},{8,4},{12,8},{1,13},{5,1},{9,5},{13,9},{2,14},{6,2},{... | collective-permute-start | bytes 786440 | tf_op jit(solution)/shard_map/ppermute | solution.py:296
  83.8 7.5 %collective-permute-start.7 = (bf16[16,64,128]{2,1,0:T(8,128)(2,1)}, bf16[16,64,128]{2,1,0:T(8,128)(2,1)}, u32[]{:S(2)}, u32[]{:S(2)}) collective-permute-start(bf16[16,64,128]{2,1,0:T(8,128)(2,1)} %slice.8), channel_id=1, source_target_pairs={{0,4},{4,8},{8,12},{12,0},{1,5},{5,9},{9,13},{13,1},{2,6},{6,10},{... | collective-permute-start | bytes 786440 | tf_op jit(solution)/shard_map/ppermute | solution.py:296
